TPU v7x, 256 devices: a whole 4x4x8 slice. The times are simulated.
256 devices in a mesh: gs: 64 (over y, z, core), view: 4 (over x).
Axes of the slice: x: 4, y: 4, z: 8, core: 2. Of those that a mesh axis runs over, the one named last changes fastest.
Arguments:
- gauss_params: float32 [59, 524288], P(None, 'gs'), may hold values from -104 to 104
- first_moment: float32 [59, 524288], P(None, 'gs'), may hold values from -4 to 4
- second_moment: float32 [59, 524288], P(None, 'gs'), may hold values from 0.001 to 1
- view_pose: float32 [4, 4], P('view'), may hold values from -259 to 3
- tile_blocks: int32 [4, 512, 16], P('view', 'gs'), may hold values from -1 to 4095, as said below
- tile_order: int32 [4, 512, 16], P('view', 'gs'), may hold values from 0 to 15, as said below
- target_image: float32 [4, 512, 3, 256], P('view', 'gs'), may hold values from 0 to 1
Outputs:
- new_params: float32 [59, 524288], P(None, 'gs')
- new_first: float32 [59, 524288], P(None, 'gs')
- new_second: float32 [59, 524288], P(None, 'gs')
- rendered: float32 [4, 512, 3, 256], P('view', 'gs')
Inputs may be any that keep to these rules, and one draw needn't show every extreme that they name: `tile_blocks`: block b is held by index b // 64 of gs. In each view, the lists of the 8 tiles of one index of gs name at most 2 blocks held by one index of gs, and some reach 2; no block is named twice in them. tile_order[v, t] is a permutation of the 16 slots.
All inputs are finite; a program needn't handle non-finite values.
Results may differ from a plain program's by a relative error of at most 0.0003.
Values sent between devices are 32-bit elements; how exact they have to be, the bound alone decides.
No kernel may reach another device: no remote copies, remote signals or barrier semaphores. Data moves between devices by JAX's collectives and lax.ppermute only.
A program may use at most 128 MiB of HBM per device.

v0:
```python
import jax
import jax.numpy as jnp
from jax import lax
from jax.sharding import PartitionSpec as P

PARAMS = 59
BLK = 128
TILE_PIX = 256
ADAM_STEP = 20


beta_one = 0.9
beta_two = 0.999
learn_rate = 0.01
adam_eps = 1e-08
dilation = 0.3


def harmonics(look_axis):
    x, y, z = (look_axis[0], look_axis[1], look_axis[2])
    square_x, square_y, square_z = (x * x, y * y, z * z)
    return jnp.stack(
        [
            0.28209479177387814 + 0.0 * x,
            -0.4886025119029199 * y,
            0.4886025119029199 * z,
            -0.4886025119029199 * x,
            1.0925484305920792 * x * y,
            -1.0925484305920792 * y * z,
            0.31539156525252005 * (2.0 * square_z - square_x - square_y),
            -1.0925484305920792 * x * z,
            0.5462742152960396 * (square_x - square_y),
            -0.5900435899266435 * y * (3.0 * square_x - square_y),
            2.890611442640554 * x * y * z,
            -0.4570457994644658 * y * (4.0 * square_z - square_x - square_y),
            0.3731763325901154 * z * (2.0 * square_z - 3.0 * square_x - 3.0 * square_y),
            -0.4570457994644658 * x * (4.0 * square_z - square_x - square_y),
            1.445305721320277 * z * (square_x - square_y),
            -0.5900435899266435 * x * (square_x - 3.0 * square_y),
        ]
    )


def project(params, camera):
    sin_yaw, cos_yaw = (jnp.sin(camera[0]), jnp.cos(camera[0]))
    sin_tilt, cos_tilt = (jnp.sin(camera[1]), jnp.cos(camera[1]))
    right_axis = (cos_yaw, 0.0 * cos_yaw, -sin_yaw)
    upward = (sin_yaw * sin_tilt, cos_tilt, cos_yaw * sin_tilt)
    look_axis = jnp.stack([sin_yaw * cos_tilt, -sin_tilt, cos_yaw * cos_tilt])
    centre = params[0:3]
    across = (
        16.0 * (right_axis[0] * centre[0] + right_axis[1] * centre[1] + right_axis[2] * centre[2])
        + camera[2]
    )
    downward = (
        16.0 * (upward[0] * centre[0] + upward[1] * centre[1] + upward[2] * centre[2]) + camera[3]
    )
    scales = jnp.exp(params[3:6])
    quaternion = params[6:10]
    length = jnp.sum(quaternion * quaternion, axis=0)
    quaternion = quaternion * lax.rsqrt(jnp.maximum(length, 1.0))
    w, x, y, z = (quaternion[0], quaternion[1], quaternion[2], quaternion[3])
    rotation = (
        (1.0 - 2.0 * (y * y + z * z), 2.0 * (x * y - w * z), 2.0 * (x * z + w * y)),
        (2.0 * (x * y + w * z), 1.0 - 2.0 * (x * x + z * z), 2.0 * (y * z - w * x)),
        (2.0 * (x * z - w * y), 2.0 * (y * z + w * x), 1.0 - 2.0 * (x * x + y * y)),
    )
    mapped = []
    for direction in (right_axis, upward):
        mapped.append(
            [
                16.0
                * scales[k]
                * (
                    direction[0] * rotation[0][k]
                    + direction[1] * rotation[1][k]
                    + direction[2] * rotation[2][k]
                )
                for k in range(3)
            ]
        )
    first_row, second_row = mapped
    spread_first = (
        first_row[0] * first_row[0]
        + first_row[1] * first_row[1]
        + first_row[2] * first_row[2]
        + dilation
    )
    spread_mixed = (
        first_row[0] * second_row[0] + first_row[1] * second_row[1] + first_row[2] * second_row[2]
    )
    spread_second = (
        second_row[0] * second_row[0]
        + second_row[1] * second_row[1]
        + second_row[2] * second_row[2]
        + dilation
    )
    determinant = spread_first * spread_second - spread_mixed * spread_mixed
    opacity = jax.nn.sigmoid(params[10])
    harmonic = harmonics(look_axis).reshape((1, 16) + (1,) * (params.ndim - 1))
    coeffs = params[11:59].reshape((3, 16) + params.shape[1:])
    colour = jnp.maximum(0.5 + jnp.sum(harmonic * coeffs, axis=1), 0.0)
    return jnp.concatenate(
        [
            jnp.stack(
                [
                    across,
                    downward,
                    spread_second / determinant,
                    -spread_mixed / determinant,
                    spread_first / determinant,
                    opacity,
                ]
            ),
            colour,
        ],
        axis=0,
    )


def composite(ordered, active, across, downward):

    def advance(carry, inputs):
        transmit, colour = carry
        feature, weight_on = inputs
        offset_x = across[None, :] - feature[0][:, None]
        offset_y = downward[None, :] - feature[1][:, None]
        exponent = 0.5 * (
            feature[2][:, None] * offset_x * offset_x
            + 2.0 * feature[3][:, None] * offset_x * offset_y
            + feature[4][:, None] * offset_y * offset_y
        )
        alphas = weight_on * feature[5][:, None] * jnp.exp(-exponent)
        losses = jnp.log1p(-alphas)
        running = jnp.cumsum(losses, axis=0)
        weights = alphas * transmit[None, :] * jnp.exp(running - losses)
        colour = colour + jnp.dot(
            feature[6:9],
            weights,
            precision=lax.Precision.HIGHEST,
            preferred_element_type=jnp.float32,
        )
        return ((transmit * jnp.exp(running[-1]), colour), None)

    initial = (jnp.ones(across.shape, jnp.float32), jnp.zeros((3,) + across.shape, jnp.float32))
    (transmit, colour), _ = lax.scan(jax.checkpoint(advance), initial, (ordered, active))
    return colour


def render_row(gathered, in_use, depth_order, row_index, goal_image):
    ordered = jnp.take_along_axis(gathered, depth_order[:, :, None, None], axis=1)
    active = jnp.take_along_axis(in_use, depth_order, axis=1)
    pixels = jnp.arange(TILE_PIX, dtype=jnp.int32)
    tile_col = jnp.arange(gathered.shape[0], dtype=jnp.int32)
    across = (16 * tile_col[:, None] + pixels[None, :] % 16).astype(jnp.float32) + 0.5
    downward = (16 * row_index + pixels // 16).astype(jnp.float32) + 0.5
    downward = jnp.broadcast_to(downward[None, :], across.shape)
    rendered = jax.vmap(composite)(ordered, active, across, downward)
    total_loss = 0.5 * jnp.sum((rendered - goal_image) ** 2)
    return (total_loss, rendered)


def apply_adam(weights_in, moment_one, moment_two, gradient):
    new_first = beta_one * moment_one + (1.0 - beta_one) * gradient
    new_second = beta_two * moment_two + (1.0 - beta_two) * gradient * gradient
    step_size = learn_rate / (1.0 - beta_one**ADAM_STEP)
    new_params = weights_in - step_size * new_first / (
        jnp.sqrt(new_second / (1.0 - beta_two**ADAM_STEP)) + adam_eps
    )
    return (new_params, new_first, new_second)


def view_total(gradient):
    return lax.psum(gradient, "view")


def shards(
    gauss_params, first_moment, second_moment, view_pose, tile_blocks, tile_order, target_image
):
    groups = lax.axis_size("gs")
    my_row = lax.axis_index("gs")
    columns = gauss_params.shape[1]
    block_count = columns // BLK
    tile_count = tile_blocks.shape[1]
    slot_count = tile_blocks.shape[2]
    requests = tile_count * slot_count
    capacity = max(2, requests // groups)
    camera = view_pose[0]
    depth_order = tile_order[0]
    goal_image = target_image[0]
    block_ids = tile_blocks[0].reshape(requests)
    in_use = block_ids >= 0
    holder = jnp.where(in_use, block_ids // block_count, -1)
    within = jnp.where(in_use, block_ids % block_count, 0)
    member = (holder[:, None] == jnp.arange(groups, dtype=jnp.int32)[None, :]).astype(jnp.int32)
    earlier = jnp.cumsum(member, axis=0) - member
    position = jnp.sum(earlier * member, axis=1)
    slot_at = jnp.where(in_use, holder * capacity + position, -1)
    matches = slot_at[None, :] == jnp.arange(groups * capacity, dtype=jnp.int32)[:, None]
    filled = jnp.any(matches, axis=1)
    request_of = jnp.sum(
        jnp.where(matches, jnp.arange(requests, dtype=jnp.int32)[None, :], 0), axis=1
    )
    wanted = jnp.where(filled, jnp.take(within, request_of), -1)
    asked_ids = lax.all_to_all(
        wanted.reshape(groups, capacity), "gs", split_axis=0, concat_axis=0, tiled=True
    ).reshape(groups * capacity)
    served = asked_ids >= 0
    fetch_ids = jnp.maximum(asked_ids, 0)
    pick_back = jnp.maximum(slot_at, 0)
    use_mask = in_use.astype(jnp.float32).reshape(tile_count, slot_count)
    spread = jnp.where(
        served[:, None],
        (fetch_ids[:, None] == jnp.arange(block_count, dtype=jnp.int32)[None, :]).astype(
            jnp.float32
        ),
        0.0,
    )
    already_summed = False
    lookup = gauss_params.reshape(PARAMS, block_count, BLK)
    outgoing = jnp.where(served[None, :, None], jnp.take(lookup, fetch_ids, axis=1), 0.0)
    arrived = lax.all_to_all(
        outgoing.reshape(PARAMS, groups, capacity, BLK),
        "gs",
        split_axis=1,
        concat_axis=1,
        tiled=True,
    )
    my_blocks = jnp.take(
        arrived.reshape(PARAMS, groups * capacity, BLK), pick_back, axis=1
    ).reshape(PARAMS, tile_count, slot_count, BLK)

    def shade_raw(raw_rows):
        projected = project(raw_rows, camera)
        return render_row(
            jnp.transpose(projected, (1, 2, 0, 3)), use_mask, depth_order, my_row, goal_image
        )

    total_loss, pull_row, rendered = jax.vjp(shade_raw, my_blocks, has_aux=True)
    (back_rows,) = pull_row(jnp.ones((), jnp.float32))
    returned = jnp.where(
        filled[None, :, None],
        jnp.take(back_rows.reshape(PARAMS, requests, BLK), request_of, axis=1),
        0.0,
    )
    landed = lax.all_to_all(
        returned.reshape(PARAMS, groups, capacity, BLK),
        "gs",
        split_axis=1,
        concat_axis=1,
        tiled=True,
    )
    summed = jnp.einsum(
        "shn,ho->son",
        landed.reshape(PARAMS, groups * capacity, BLK),
        spread,
        precision=lax.Precision.HIGHEST,
    )
    gradient = summed.reshape(PARAMS, columns)
    summed_grad = view_total(gradient)
    new_params, new_first, new_second = apply_adam(
        gauss_params, first_moment, second_moment, summed_grad
    )
    return (new_params, new_first, new_second, rendered[None])


def solution(mesh):
    placed = (
        P(None, "gs"),
        P(None, "gs"),
        P(None, "gs"),
        P("view", None),
        P("view", "gs", None),
        P("view", "gs", None),
        P("view", "gs", None, None),
    )
    return jax.shard_map(
        shards,
        mesh=mesh,
        in_specs=placed,
        out_specs=(P(None, "gs"), P(None, "gs"), P(None, "gs"), P("view", "gs", None, None)),
        check_vma=False,
    )
```

profile of v0, /device:TPU:1, one launch (start us, length us, event | category | flops | bytes accessed | tf_op | source)
XLA Modules:
  0.0 732.1 jit_solution(16836305710933082786)
XLA Ops:
  11.0 13.2 %all-to-all-start = ((s32[64,1,2]{2,1,0:T(1,128)}), s32[64,1,2]{2,1,0:T(1,128)S(1)}, u32[]{:S(2)}, u32[]{:S(2)}) async-start(s32[64,1,2]{2,1,0:T(1,128)} %bitcast.2), calls=%async_computation | async-start | bytes 65536 | tf_op jit(solution)/shard_map/all_to_all | solution.py:205
  27.5 5.9 all-to-all-done
  33.5 2.8 gather_fusion.1
  36.3 10.6 %fusion.64 = f32[59,64,2,128]{3,2,0,1:T(2,128)} fusion(f32[59,64,2,128]{3,0,2,1:T(8,128)} %bitcast.223, pred[64,2]{1,0:T(8,128)(4,1)S(1)} %get-tuple-element.579, pred[64,2]{1,0:T(8,128)(4,1)S(1)} %bitcast.295), kind=kLoop, calls=%fused_computation.120 | loop fusion | flops 1933312 | bytes 7733504 | tf_op jit(solution)/shard_map/jit(_where)/select_n | solution.py:221
  46.9 6.0 all-to-all-start.1
  59.2 82.7 %all-to-all-done.1 = f32[59,64,2,128]{3,2,0,1:T(2,128)} async-done(((f32[59,64,2,128]{3,2,0,1:T(2,128)}), f32[59,64,2,128]{3,2,0,1:T(2,128)}, u32[]{:S(2)}, u32[]{:S(2)}) %all-to-all-start.1) | async-done | bytes 3866656 | tf_op jit(solution)/shard_map/all_to_all | solution.py:222
  141.9 4.7 copy.234
  146.6 5.0 gather_fusion.4
  151.6 4.7 fusion.63
  163.6 72.4 %while.34 = (s32[]{:T(128)}, f32[8,256]{1,0:T(8,128)S(1)}, f32[8,3,256]{2,1,0:T(4,128)S(1)}, f32[16,8,256]{2,1,0:T(8,128)}, f32[16,8]{1,0:T(8,128)S(1)}, /*index...) while((s32[]{:T(128)}, f32[8,256]{1,0:T(8,128)S(1)}, ...), condition=%wide.region_8.10_spmd.clone, body=%wide.region_6.9_spmd.clone.sunk | while | flops 50883328 | bytes 3501828 | solution.py:146
  236.1 288.9 %while.35 = (s32[]{:T(128)}, f32[8,256]{1,0:T(8,128)S(1)}, f32[8,3,256]{2,1,0:T(4,128)S(1)}, f32[16,8,9,128]{3,0,1,2:T(8,128)S(1)}, f32[16,8,256]{2,1,0:T(8,128)...) while((s32[]{:T(128)}, f32[8,256]{1,0:T(8,128)S(1)}, ...), condition=%wide.region_19.21_spmd.clone, body=%wide.region_9.20_spmd.clone.sunk | while | flops 116985856 | bytes 19749188 | solution.py:146
  239.0 2.7 pad_add_fusion.5
  241.8 2.5 fusion.155
  246.8 3.1 fusion.156
  257.1 2.7 pad_add_fusion.5
  259.8 2.5 fusion.155
  264.8 3.1 fusion.156
  275.1 2.7 pad_add_fusion.5
  277.8 2.5 fusion.155
  282.8 3.1 fusion.156
  293.1 2.7 pad_add_fusion.5
  295.9 2.5 fusion.155
  300.9 3.1 fusion.156
  311.2 2.7 pad_add_fusion.5
  313.9 2.5 fusion.155
  318.9 3.1 fusion.156
  329.2 2.7 pad_add_fusion.5
  331.9 2.5 fusion.155
  336.9 3.1 fusion.156
  347.2 2.7 pad_add_fusion.5
  350.0 2.5 fusion.155
  355.0 3.1 fusion.156
  365.3 2.7 pad_add_fusion.5
  368.0 2.5 fusion.155
  373.0 3.1 fusion.156
  383.3 2.7 pad_add_fusion.5
  386.0 2.5 fusion.155
  391.0 3.1 fusion.156
  401.3 2.7 pad_add_fusion.5
  404.1 2.5 fusion.155
  409.1 3.1 fusion.156
  419.4 2.7 pad_add_fusion.5
  427.1 3.1 fusion.156
  437.4 2.7 pad_add_fusion.5
  445.1 3.1 fusion.156
  455.4 2.7 pad_add_fusion.5
  463.2 3.1 fusion.156
  473.5 2.7 pad_add_fusion.5
  481.2 3.1 fusion.156
  491.5 2.7 pad_add_fusion.5
  494.2 2.5 fusion.155
  499.2 3.1 fusion.156
  509.5 2.7 pad_add_fusion.5
  517.3 3.1 fusion.156
  525.6 6.9 scatter_fusion
  536.8 4.3 copy.246
  541.1 4.9 gather_fusion.5
  546.0 2.8 bitcast_select_fusion
  548.8 5.3 copy.247
  554.2 5.9 all-to-all-start.2
  560.5 88.5 %all-to-all-done.2 = f32[59,64,2,128]{3,2,0,1:T(2,128)} async-done(((f32[59,64,2,128]{3,2,0,1:T(2,128)}), f32[59,64,2,128]{3,2,0,1:T(2,128)}, u32[]{:S(2)}, u32[]{:S(2)}) %all-to-all-start.2) | async-done | bytes 3866656 | tf_op jit(solution)/shard_map/all_to_all | solution.py:246
  649.0 4.3 copy.248
  658.9 59.8 %all-reduce.31.cloned.1.call-done = f32[59,8192]{1,0:T(8,128)} async-done(((f32[59,8192]{1,0:T(8,128)}), f32[59,8192]{1,0:T(8,128)}) %all-reduce.31.cloned.1.call-update) | async-done | bytes 1933328 | tf_op jit(solution)/shard_map/psum | solution.py:174
  718.7 6.4 divide_subtract_fusion
  (776 shorter events, 264.5 us)
Async XLA Ops:
  8.8 17.3 %copy-start.39 = (pred[128]{0:T(512)(128)(4,1)}, pred[128]{0:T(512)(128)(4,1)S(1)}, u32[]{:S(2)}) copy-start(pred[128]{0:T(512)(128)(4,1)S(1)} %fusion.83) | copy-start | bytes 388
  11.0 22.4 %all-to-all-start = ((s32[64,1,2]{2,1,0:T(1,128)}), s32[64,1,2]{2,1,0:T(1,128)S(1)}, u32[]{:S(2)}, u32[]{:S(2)}) async-start(s32[64,1,2]{2,1,0:T(1,128)} %bitcast.2), calls=%async_computation | async-start | bytes 65536 | tf_op jit(solution)/shard_map/all_to_all | solution.py:205
  46.9 6.0 copy-start.38
  46.9 9.7 %copy-start.36 = (s32[1,8,16]{2,1,0:T(8,128)S(1)}, s32[1,8,16]{2,1,0:T(8,128)}, u32[]{:S(2)}) copy-start(s32[1,8,16]{2,1,0:T(8,128)} %param.18) | copy-start | bytes 1540
  46.9 9.8 %copy-start.37 = (s32[1,8,16]{2,1,0:T(8,128)S(1)}, s32[1,8,16]{2,1,0:T(8,128)}, u32[]{:S(2)}) copy-start(s32[1,8,16]{2,1,0:T(8,128)} %param.17) | copy-start | bytes 1540
  46.9 95.0 %all-to-all-start.1 = ((f32[59,64,2,128]{3,2,0,1:T(2,128)}), f32[59,64,2,128]{3,2,0,1:T(2,128)}, u32[]{:S(2)}, u32[]{:S(2)}) async-start(f32[59,64,2,128]{3,2,0,1:T(2,128)} %fusion.64), calls=%async_computation.1 | async-start | bytes 7733248 | tf_op jit(solution)/shard_map/all_to_all | solution.py:222
  156.3 2.1 copy-start
  157.1 2.7 copy-start.4
  158.3 2.0 copy-start.20
  158.3 1.9 copy-start.11
  159.8 2.1 copy-start.14
  159.8 1.6 copy-start.16
  159.8 1.6 copy-start.18
  159.8 1.6 copy-start.19
  160.2 2.9 copy-start.2
  161.3 2.3 copy-start.6
  161.3 2.3 copy-start.8
  163.6 72.4 %copy-start.35 = (f32[1,8,3,256]{3,1,2,0:T(8,128)S(1)}, f32[1,8,3,256]{3,1,2,0:T(8,128)}, u32[]{:S(2)}) copy-start(f32[1,8,3,256]{3,1,2,0:T(8,128)} %param.19) | copy-start | bytes 73732
  525.0 7.7 %copy-start.3 = (f32[3,8,16,128]{3,2,1,0:T(8,128)S(1)}, f32[3,8,16,128]{3,2,1,0:T(8,128)}, u32[]{:S(2)}) copy-start(f32[3,8,16,128]{3,2,1,0:T(8,128)} %copy-done.2) | copy-start | bytes 589828
  525.1 7.7 %copy-start.7 = (f32[1,8,16,128]{3,2,1,0:T(8,128)S(1)}, f32[1,8,16,128]{3,2,1,0:T(8,128)}, u32[]{:S(2)}) copy-start(f32[1,8,16,128]{3,2,1,0:T(8,128)} %copy-done.6) | copy-start | bytes 196612
  525.1 7.7 %copy-start.9 = (f32[1,8,16,128]{3,2,1,0:T(8,128)S(1)}, f32[1,8,16,128]{3,2,1,0:T(8,128)}, u32[]{:S(2)}) copy-start(f32[1,8,16,128]{3,2,1,0:T(8,128)} %copy-done.8) | copy-start | bytes 196612
  525.1 7.7 %copy-start.13 = (f32[1,8,16,128]{3,2,1,0:T(8,128)S(1)}, f32[1,8,16,128]{3,2,1,0:T(8,128)}, u32[]{:S(2)}) copy-start(f32[1,8,16,128]{3,2,1,0:T(8,128)} %get-tuple-element.512) | copy-start | bytes 196612
  525.1 7.7 %copy-start.15 = (f32[1,128,128]{2,1,0:T(8,128)S(1)}, f32[1,128,128]{2,1,0:T(8,128)}, u32[]{:S(2)}) copy-start(f32[1,128,128]{2,1,0:T(8,128)} %copy-done.14) | copy-start | bytes 196612
  525.5 7.4 %copy-start.17 = (f32[1,128,128]{2,1,0:T(8,128)S(1)}, f32[1,128,128]{2,1,0:T(8,128)}, u32[]{:S(2)}) copy-start(f32[1,128,128]{2,1,0:T(8,128)} %copy-done.16) | copy-start | bytes 196612
  532.5 2.2 copy-start.10
  532.5 2.2 copy-start.21
  532.5 2.2 copy-start.28
  532.5 2.2 copy-start.12
  532.7 3.1 copy-start.41
  534.2 1.9 copy-start.22
  534.2 1.9 copy-start.23
  534.2 1.9 copy-start.24
  534.3 1.9 copy-start.25
  534.3 1.9 copy-start.26
  534.3 1.9 copy-start.27
  534.3 1.9 copy-start.29
  534.3 1.9 copy-start.30
  534.3 1.9 copy-start.31
  534.3 1.9 copy-start.32
  534.3 1.9 copy-start.33
  534.3 1.9 copy-start.34
  534.5 1.8 copy-start.5
  541.1 4.9 copy-start.40
  541.1 5.0 copy-start.42
  554.2 94.8 %all-to-all-start.2 = ((f32[59,64,2,128]{3,2,0,1:T(2,128)}), f32[59,64,2,128]{3,2,0,1:T(2,128)}, u32[]{:S(2)}, u32[]{:S(2)}) async-start(f32[59,64,2,128]{3,2,0,1:T(2,128)} %copy.247), calls=%async_computation.2 | async-start | bytes 7733248 | tf_op jit(solution)/shard_map/all_to_all | solution.py:246
  560.1 158.6 %all-reduce.31.cloned.1.call-start = ((), (), s32[]{:S(2)}) async-start(), calls=%async_computation.3 | async-start | bytes 4194304 | tf_op jit(solution)/shard_map/psum | solution.py:174
  655.7 62.9 %copy-start.1 = (f32[59,8192]{1,0:T(8,128)S(1)}, f32[59,8192]{1,0:T(8,128)}, u32[]{:S(2)}) copy-start(f32[59,8192]{1,0:T(8,128)} %param.13) | copy-start | bytes 5799940
Sparse Core Ops, SparseCore 0:
  658.4 60.2 all-reduce.30
where the time goes:
time: 742 us; the launch traced here: 732 us
  other arithmetic  249 us (34%)
  waiting for transfers between devices  237 us (32%)
  local copies, waits for them, and re-layouts  102 us (14%)
  matrix products  97.4 us (13%)
  starting transfers between devices  25.3 us (3%)
  between operations  18.4 us (2%)
    dot_general x48, matrix products, advance(): jnp.dot(feature[6:9], weights, precision=lax.Precision.HIGHEST, preferred...  95.3 us
    all_to_all x1, waiting for transfers between devices, shards(): lax.all_to_all(returned.reshape(PARAMS, groups, capacity, BLK), 'gs', spl...  88.5 us
    another operation x48, other arithmetic, advance(): running = jnp.cumsum(losses, axis=0)  85.8 us
    all_to_all x1, waiting for transfers between devices, shards(): lax.all_to_all(outgoing.reshape(PARAMS, groups, capacity, BLK), 'gs', spl...  82.7 us
    psum x1, waiting for transfers between devices, view_total(): return lax.psum(gradient, 'view')  59.8 us
    reduce_sum x16, other arithmetic, advance(): offset_y = downward[None, :] - feature[1][:, None]  49.8 us
    mul x16, other arithmetic, advance(): 0.5 * (feature[2][:, None] * offset_x * offset_x + 2.0 * feature[3][:, No...  39.1 us
    dynamic_update_slice x32, local copies, waits for them, and re-layouts, composite(): lax.scan(jax.checkpoint(advance), initial, (ordered, active))  33.7 us
  transfers between devices with their start and end apart: 4, of which 4 were waited for; matrix products, arithmetic and copies ran while one was open for 1% of the time, Pallas kernels for 0%

commit v1 on v0

v1 whole, which is shorter than its diff:
```python
import functools
import math

import jax
import jax.numpy as jnp
from jax import lax
from jax.experimental import pallas as pl
from jax.experimental.pallas import tpu as pltpu
from jax.sharding import PartitionSpec as P

PARAMS = 59
BLK = 128
PIX = 256
FEATS = 9
CAP = 2
ADAM_STEP = 20

beta_one = 0.9
beta_two = 0.999
learn_rate = 0.01
adam_eps = 1e-08
dilation = 0.3
LOG2E = 1.4426950408889634
TINY = 1.1754944e-38
BELOW_ONE = 0.99999994

VMEM = pl.BlockSpec(memory_space=pltpu.VMEM)
SMEM = pl.BlockSpec(memory_space=pltpu.SMEM)


def params_of(megabytes):
    return pltpu.CompilerParams(vmem_limit_bytes=megabytes << 20)


def harmonics(x, y, z):
    square_x, square_y, square_z = (x * x, y * y, z * z)
    return [
        0.28209479177387814 + 0.0 * x,
        -0.4886025119029199 * y,
        0.4886025119029199 * z,
        -0.4886025119029199 * x,
        1.0925484305920792 * x * y,
        -1.0925484305920792 * y * z,
        0.31539156525252005 * (2.0 * square_z - square_x - square_y),
        -1.0925484305920792 * x * z,
        0.5462742152960396 * (square_x - square_y),
        -0.5900435899266435 * y * (3.0 * square_x - square_y),
        2.890611442640554 * x * y * z,
        -0.4570457994644658 * y * (4.0 * square_z - square_x - square_y),
        0.3731763325901154 * z * (2.0 * square_z - 3.0 * square_x - 3.0 * square_y),
        -0.4570457994644658 * x * (4.0 * square_z - square_x - square_y),
        1.445305721320277 * z * (square_x - square_y),
        -0.5900435899266435 * x * (square_x - 3.0 * square_y),
    ]


def geometry(rows, camera):
    sin_yaw, cos_yaw, sin_tilt, cos_tilt, shift_x, shift_y = camera
    right_axis = (cos_yaw, 0.0 * cos_yaw, -sin_yaw)
    upward = (sin_yaw * sin_tilt, cos_tilt, cos_yaw * sin_tilt)
    across = (
        16.0 * (right_axis[0] * rows[0] + right_axis[1] * rows[1] + right_axis[2] * rows[2])
        + shift_x
    )
    downward = 16.0 * (upward[0] * rows[0] + upward[1] * rows[1] + upward[2] * rows[2]) + shift_y
    scales = [jnp.exp(rows[3]), jnp.exp(rows[4]), jnp.exp(rows[5])]
    w, x, y, z = rows[6:10]
    inverse = lax.rsqrt(jnp.maximum(w * w + x * x + y * y + z * z, 1.0))
    w, x, y, z = (w * inverse, x * inverse, y * inverse, z * inverse)
    rotation = (
        (1.0 - 2.0 * (y * y + z * z), 2.0 * (x * y - w * z), 2.0 * (x * z + w * y)),
        (2.0 * (x * y + w * z), 1.0 - 2.0 * (x * x + z * z), 2.0 * (y * z - w * x)),
        (2.0 * (x * z - w * y), 2.0 * (y * z + w * x), 1.0 - 2.0 * (x * x + y * y)),
    )
    first, second = [
        [
            16.0
            * scales[k]
            * (
                direction[0] * rotation[0][k]
                + direction[1] * rotation[1][k]
                + direction[2] * rotation[2][k]
            )
            for k in range(3)
        ]
        for direction in (right_axis, upward)
    ]
    spread_first = first[0] * first[0] + first[1] * first[1] + first[2] * first[2] + dilation
    spread_mixed = first[0] * second[0] + first[1] * second[1] + first[2] * second[2]
    spread_second = second[0] * second[0] + second[1] * second[1] + second[2] * second[2] + dilation
    determinant = spread_first * spread_second - spread_mixed * spread_mixed
    return [
        across,
        downward,
        spread_second / determinant,
        -spread_mixed / determinant,
        spread_first / determinant,
    ]


def split(value, parts):
    out = []
    for _ in range(parts - 1):
        high = value.astype(jnp.bfloat16).astype(jnp.float32)
        out.append(high)
        value = value - high
    out.append(value)
    return out


def request_kernel(blocks_ref, order_ref, wanted_ref, table_ref, count_ref, held_ref):
    holders = wanted_ref.shape[0]
    tiles, slots = blocks_ref.shape
    per_holder = 64

    def clear(h, _):
        wanted_ref[h, 0, 0] = -1
        wanted_ref[h, 0, 1] = -1
        held_ref[h] = 0
        return 0

    lax.fori_loop(0, holders, clear, 0)

    def tile(t, _):
        def slot(i, used):
            block = blocks_ref[t, order_ref[t, i]]
            holder = lax.max(block, 0) // per_holder
            position = held_ref[holder]

            @pl.when(block >= 0)
            def _():
                held_ref[holder] = position + 1
                wanted_ref[holder, 0, position] = block - holder * per_holder
                table_ref[t, used] = holder * CAP + position

            return used + (block >= 0).astype(jnp.int32)

        count_ref[t] = lax.fori_loop(0, slots, slot, jnp.int32(0))
        return 0

    lax.fori_loop(0, tiles, tile, 0)


def project_kernel(camera_ref, params_ref, feats_ref, turned):
    blocks = feats_ref.shape[0]
    sin_yaw, cos_yaw, sin_tilt, cos_tilt = [camera_ref[k] for k in range(4)]
    camera = [camera_ref[k] for k in range(6)]
    terms = harmonics(sin_yaw * cos_tilt, -sin_tilt, cos_yaw * cos_tilt)
    row = lax.broadcasted_iota(jnp.int32, (8, PARAMS), 0)
    column = lax.broadcasted_iota(jnp.int32, (8, PARAMS), 1)
    which = column - 11 - 16 * row
    weight = jnp.zeros((8, PARAMS), jnp.float32)
    for j in range(16):
        weight = jnp.where((which == j) & (row < 3), terms[j], weight)
    for j in range(blocks):
        turned[j] = params_ref[0:16, j * BLK : (j + 1) * BLK]
    chunk = 8 * BLK
    for g in range(blocks // 8):
        shade = 0.5 + jnp.dot(
            weight,
            params_ref[:, g * chunk : (g + 1) * chunk],
            precision=lax.Precision.HIGHEST,
            preferred_element_type=jnp.float32,
        )
        mask = jnp.where(shade > 0.0, 1.0, jnp.where(shade == 0.0, 0.5, 0.0))
        shade = jnp.maximum(shade, 0.0)
        for j in range(8):
            feats_ref[8 * g + j, 6:9, :] = shade[0:3, j * BLK : (j + 1) * BLK]
            feats_ref[8 * g + j, 9:12, :] = mask[0:3, j * BLK : (j + 1) * BLK]
        rows = [turned[8 * g : 8 * g + 8, r, :] for r in range(11)]
        shaped = geometry(rows, camera)
        opacity = 1.0 / (1.0 + jnp.exp(-rows[10]))
        for r, value in enumerate(shaped + [opacity]):
            feats_ref[8 * g : 8 * g + 8, r, :] = value


def pick_kernel(asked_ref, feats_ref, out_ref):
    def one(h, _):
        for c in range(CAP):
            block = lax.max(asked_ref[h, 0, c], 0)
            out_ref[h, :, c, :] = feats_ref[block][0:FEATS]
        return 0

    lax.fori_loop(0, out_ref.shape[0], one, 0)


def bands(lower):
    row = lax.broadcasted_iota(jnp.int32, (BLK, 2 * BLK), 0)
    column = lax.broadcasted_iota(jnp.int32, (BLK, 2 * BLK), 1) % BLK
    inside = column < row if lower else column > row
    return inside.astype(jnp.float32).astype(jnp.bfloat16)


def nt(a, b):
    return lax.dot_general(a, b, (((1,), (1,)), ((), ())), preferred_element_type=jnp.float32)


def render_kernel(
    table_ref,
    count_ref,
    arrived_ref,
    goal_ref,
    image_ref,
    back_ref,
    before,
    after,
    basis,
    alphas,
    weights,
    halves,
    coefs,
):
    my_row = lax.axis_index("gs")
    before[...] = bands(True)
    after[...] = bands(False)
    pixel = lax.broadcasted_iota(jnp.int32, (8, PIX), 1)
    place = lax.broadcasted_iota(jnp.int32, (8, PIX), 0)
    x = (pixel % 16).astype(jnp.float32) - 7.5
    y = (pixel // 16).astype(jnp.float32) - 7.5
    terms = jnp.where(place == 0, 1.0, 0.0)
    for k, value in enumerate((x, y, x * x, x * y, y * y)):
        terms = jnp.where(place == k + 1, value, terms)
    basis[0:8] = terms
    basis[8:16] = terms
    basis[16:24] = terms
    basis[24:48] = jnp.zeros((24, PIX), jnp.float32)
    back_ref[...] = jnp.zeros_like(back_ref)
    zero = jnp.zeros((1, BLK), jnp.float32)

    def fetch(t, i):
        slot = table_ref[t, i]
        holder, place = slot // CAP, slot % CAP
        rows = [arrived_ref[holder, f, pl.ds(place, 1), :] for f in range(FEATS)]
        rows[0] = rows[0] - (16 * t + 8).astype(jnp.float32)
        rows[1] = rows[1] - (16 * my_row + 8).astype(jnp.float32)
        return holder, place, rows

    def tile(t, _):
        used = count_ref[t]

        def forward(i, carry):
            logs, image = carry
            _, _, (u, v, a, b, c, opacity, red, green, blue) = fetch(t, i)
            au, bv = (a * u + b * v, b * u + c * v)
            ks = [
                jnp.log2(jnp.maximum(opacity, TINY)) - (0.5 * LOG2E) * (au * u + bv * v),
                LOG2E * au,
                LOG2E * bv,
                (-0.5 * LOG2E) * a,
                -LOG2E * b,
                (-0.5 * LOG2E) * c,
                zero,
                zero,
            ]
            geo = split(jnp.concatenate(ks, axis=0), 3)
            high, mid, low = split(jnp.concatenate([red, green, blue] + [zero] * 5, axis=0), 3)
            stack = jnp.concatenate(
                geo + [
                    high[0:3], high[0:3], mid[0:3], high[0:3], low[0:3], mid[0:3],
                    jnp.zeros((6, BLK), jnp.float32),
                ],
                axis=0,
            )
            turned = stack.T.astype(jnp.bfloat16)
            coefs[i] = turned
            alpha = jnp.exp2(
                jnp.dot(turned, basis[...].astype(jnp.bfloat16), preferred_element_type=jnp.float32)
            )
            alpha = jnp.minimum(alpha, BELOW_ONE)
            alphas[i] = alpha
            loss = jnp.log2(1.0 - alpha)
            pair = jnp.concatenate([q.astype(jnp.bfloat16) for q in split(loss, 2)], axis=0)
            run = jnp.dot(before[...], pair, preferred_element_type=jnp.float32)
            weight = alpha * jnp.exp2(run + logs)
            weights[i] = weight
            pair = jnp.concatenate([q.astype(jnp.bfloat16) for q in split(weight, 2)], axis=0)
            halves[i] = pair
            colours = stack[24:48].astype(jnp.bfloat16)
            shade = jnp.dot(
                jnp.concatenate([colours, colours], axis=1), pair, preferred_element_type=jnp.float32
            )
            image = image + (shade[0:3] + (shade[6:9] + shade[12:15]))
            logs = logs + (run[BLK - 1 : BLK] + loss[BLK - 1 : BLK])
            return logs, image

        _, image = lax.fori_loop(
            0, used, forward,
            (jnp.zeros((1, PIX), jnp.float32), jnp.zeros((3, PIX), jnp.float32)),
        )
        image_ref[t] = image
        pull = image - goal_ref[t]
        high, mid, low = split(pull, 3)
        pulls = jnp.concatenate(
            [high, mid, high, low, high, mid, jnp.zeros((6, PIX), jnp.float32)], axis=0
        )
        basis[24:48] = pulls
        pulled = jnp.concatenate([jnp.zeros((24, PIX), jnp.float32), pulls], axis=0).astype(
            jnp.bfloat16
        )
        colour_pulls = jnp.concatenate(
            [high, mid, low, jnp.zeros((7, PIX), jnp.float32)], axis=0
        ).astype(jnp.bfloat16)
        moments_of = basis[0:16].astype(jnp.bfloat16)

        def backward(step, later):
            i = used - 1 - step
            holder, place, (u, v, a, b, c, _, _, _, _) = fetch(t, i)
            reach = jnp.dot(coefs[i], pulled, preferred_element_type=jnp.float32) * weights[i]
            pair = jnp.concatenate([q.astype(jnp.bfloat16) for q in split(reach, 2)], axis=0)
            behind = jnp.dot(after[...], pair, preferred_element_type=jnp.float32)
            alpha = alphas[i]
            push = reach - (behind + later) * (alpha / (1.0 - alpha))
            trio = jnp.concatenate([q.astype(jnp.bfloat16) for q in split(push, 3)], axis=0)
            moments = nt(moments_of, trio)
            moments = moments[:, 0:BLK] + (moments[:, BLK : 2 * BLK] + moments[:, 2 * BLK :])
            tints = nt(colour_pulls, halves[i])
            tints = tints[:, 0:BLK] + tints[:, BLK:]
            tints = tints[0:3] + (tints[3:6] + tints[6:9])
            m0, mx, my, mxx, mxy, myy = [moments[k : k + 1] for k in range(6)]
            cx, cy = (mx - u * m0, my - v * m0)
            grads = [
                a * cx + b * cy,
                b * cx + c * cy,
                -0.5 * (mxx - u * (mx + cx)),
                -(mxy - u * my - v * cx),
                -0.5 * (myy - v * (my + cy)),
                m0,
                tints[0:1],
                tints[1:2],
                tints[2:3],
            ]
            for f, value in enumerate(grads):
                back_ref[holder, f, pl.ds(place, 1), :] = value
            return later + (behind[0:1] + reach[0:1])

        lax.fori_loop(0, used, backward, jnp.zeros((1, PIX), jnp.float32))
        basis[24:48] = jnp.zeros((24, PIX), jnp.float32)
        return 0

    lax.fori_loop(0, image_ref.shape[0], tile, 0)


def land_kernel(asked_ref, camera_ref, landed_ref, feats_ref, out_ref, total):
    total[...] = jnp.zeros_like(total)

    def one(h, _):
        for c in range(CAP):
            block = asked_ref[h, 0, c]

            @pl.when(block >= 0)
            def _():
                total[block, 0:FEATS, :] = total[block, 0:FEATS, :] + landed_ref[h, :, c, :]

        return 0

    lax.fori_loop(0, landed_ref.shape[0], one, 0)
    groups = total.shape[0] // 8
    for g in range(groups):
        for f in range(FEATS):
            value = total[8 * g : 8 * g + 8, f, :]
            if f >= 6:
                value = value * feats_ref[8 * g : 8 * g + 8, f + 3, :]
            out_ref[g, f] = value
    place = lax.broadcasted_iota(jnp.int32, (8, BLK), 0)
    shown = jnp.zeros((8, BLK), jnp.float32)
    for k in range(6):
        shown = jnp.where(place == k, camera_ref[k], shown)
    for g in range(groups):
        out_ref[g, FEATS] = shown


def adam(weights_in, moment_one, moment_two, gradient):
    new_first = beta_one * moment_one + (1.0 - beta_one) * gradient
    new_second = beta_two * moment_two + (1.0 - beta_two) * gradient * gradient
    step_size = learn_rate / (1.0 - beta_one**ADAM_STEP)
    new_params = weights_in - step_size * new_first / (
        jnp.sqrt(new_second / (1.0 - beta_two**ADAM_STEP)) + adam_eps
    )
    return (new_params, new_first, new_second)


def update_kernel(
    params_ref, first_ref, second_ref, own_ref, next_ref, across_ref, last_ref,
    new_params_ref, new_first_ref, new_second_ref, pulls, turned, shades, waves,
):
    me = lax.axis_index("view")
    views = 4
    for k, ref in enumerate((own_ref, next_ref, across_ref, last_ref)):
        pulls[(me + k) % views] = ref[0]
    for j in range(8):
        turned[j] = params_ref[0:16, j * BLK : (j + 1) * BLK]
    rows = [turned[:, r, :] for r in range(11)]
    opacity = 1.0 / (1.0 + jnp.exp(-rows[10]))
    total = [None] * 11
    for v in range(views):
        camera = [pulls[v, FEATS, k : k + 1, :] for k in range(6)]
        _, pull_back = jax.vjp(lambda *r: geometry(r, camera), *rows[0:10])
        grads = list(pull_back([pulls[v, f] for f in range(5)]))
        grads.append(pulls[v, 5] * (1.0 - opacity))
        total = grads if v == 0 else [p + q for p, q in zip(total, grads)]
        for c in range(3):
            shades[:, 3 * v + c, :] = pulls[v, 6 + c]

        @pl.when(pl.program_id(0) == 0)
        def _():
            sin_yaw, cos_yaw, sin_tilt, cos_tilt = camera[0:4]
            terms = harmonics(sin_yaw * cos_tilt, -sin_tilt, cos_yaw * cos_tilt)
            for k in range(8):
                row = lax.broadcasted_iota(jnp.int32, (8, BLK), 0) + (8 * k - 11)
                wave = jnp.zeros((8, BLK), jnp.float32)
                for j in range(16):
                    wave = jnp.where((row >= 0) & (row % 16 == j), terms[j], wave)
                waves[v, 8 * k : 8 * k + 8, :] = wave

    for r in range(11):
        turned[:, r, :] = total[r]
    row_in = lax.broadcasted_iota(jnp.int32, (8, BLK), 0)
    for j in range(8):
        columns = slice(j * BLK, (j + 1) * BLK)
        for k in range(8):
            gradient = None
            if k > 0:
                first = (8 * k - 11) // 16 if k > 1 else 0
                last = min((8 * k + 7 - 11) // 16, 2)
                for v in range(views):
                    tint = shades[j, 3 * v + first : 3 * v + first + 1, :]
                    if last != first:
                        tint = jnp.where(
                            row_in + (8 * k - 11) < 16 * last,
                            tint,
                            shades[j, 3 * v + last : 3 * v + last + 1, :],
                        )
                    term = waves[v, 8 * k : 8 * k + 8, :] * tint
                    gradient = term if gradient is None else gradient + term
            if k == 0:
                gradient = turned[j, 0:8, :]
            if k == 1:
                gradient = jnp.where(row_in < 3, turned[j, 8:16, :], gradient)
            height = min(8, PARAMS - 8 * k)
            at = (slice(8 * k, 8 * k + height), columns)
            values = adam(params_ref[at], first_ref[at], second_ref[at], gradient[0:height])
            new_params_ref[at], new_first_ref[at], new_second_ref[at] = values


def shards(
    gauss_params, first_moment, second_moment, view_pose, tile_blocks, tile_order, target_image
):
    groups = lax.axis_size("gs")
    views = lax.axis_size("view")
    columns = gauss_params.shape[1]
    blocks = columns // BLK
    tiles, slots = tile_blocks.shape[1:]
    f32, i32 = jnp.float32, jnp.int32
    shape = jax.ShapeDtypeStruct
    pose = view_pose[0]
    camera = jnp.concatenate(
        [jnp.stack([jnp.sin(pose[0]), jnp.cos(pose[0]), jnp.sin(pose[1]), jnp.cos(pose[1])]), pose[2:4]]
    )

    wanted, table, count = pl.pallas_call(
        request_kernel,
        out_shape=[shape((groups, 1, CAP), i32), shape((tiles, slots), i32), shape((tiles,), i32)],
        in_specs=[SMEM, SMEM],
        out_specs=[SMEM, SMEM, SMEM],
        scratch_shapes=[pltpu.SMEM((groups,), i32)],
        name="requests",
    )(tile_blocks[0], tile_order[0])
    asked = lax.all_to_all(wanted, "gs", split_axis=0, concat_axis=0, tiled=True)
    feats = pl.pallas_call(
        project_kernel,
        out_shape=shape((blocks, 16, BLK), f32),
        in_specs=[SMEM, VMEM],
        out_specs=VMEM,
        scratch_shapes=[pltpu.VMEM((blocks, 16, BLK), f32)],
        compiler_params=params_of(24),
        name="project",
    )(camera, gauss_params)
    outgoing = pl.pallas_call(
        pick_kernel,
        out_shape=shape((groups, FEATS, CAP, BLK), f32),
        in_specs=[SMEM, VMEM],
        out_specs=VMEM,
        compiler_params=params_of(16),
        name="pick",
    )(asked, feats)
    arrived = lax.all_to_all(outgoing, "gs", split_axis=0, concat_axis=0, tiled=True)
    image, back = pl.pallas_call(
        render_kernel,
        out_shape=[shape((tiles, 3, PIX), f32), shape((groups, FEATS, CAP, BLK), f32)],
        in_specs=[SMEM, SMEM, VMEM, VMEM],
        out_specs=[VMEM, VMEM],
        scratch_shapes=[
            pltpu.VMEM((BLK, 2 * BLK), jnp.bfloat16),
            pltpu.VMEM((BLK, 2 * BLK), jnp.bfloat16),
            pltpu.VMEM((48, PIX), f32),
            pltpu.VMEM((slots, BLK, PIX), f32),
            pltpu.VMEM((slots, BLK, PIX), f32),
            pltpu.VMEM((slots, 2 * BLK, PIX), jnp.bfloat16),
            pltpu.VMEM((slots, BLK, 48), jnp.bfloat16),
        ],
        compiler_params=params_of(32),
        name="render",
    )(table, count, arrived, target_image[0])
    landed = lax.all_to_all(back, "gs", split_axis=0, concat_axis=0, tiled=True)
    own = pl.pallas_call(
        land_kernel,
        out_shape=shape((blocks // 8, FEATS + 1, 8, BLK), f32),
        in_specs=[SMEM, SMEM, VMEM, VMEM],
        out_specs=VMEM,
        scratch_shapes=[pltpu.VMEM((blocks, 16, BLK), f32)],
        compiler_params=params_of(16),
        name="land",
    )(asked, camera, landed, feats)
    others = [
        lax.ppermute(own, "view", [((i + k) % views, i) for i in range(views)]) for k in range(1, views)
    ]
    chunk = 8 * BLK
    wide = pl.BlockSpec((PARAMS, chunk), lambda i: (0, i))
    deep = pl.BlockSpec((1, FEATS + 1, 8, BLK), lambda i: (i, 0, 0, 0))
    new_params, new_first, new_second = pl.pallas_call(
        update_kernel,
        grid=(columns // chunk,),
        out_shape=[shape((PARAMS, columns), f32)] * 3,
        in_specs=[wide] * 3 + [deep] * 4,
        out_specs=[wide] * 3,
        scratch_shapes=[
            pltpu.VMEM((views, FEATS + 1, 8, BLK), f32),
            pltpu.VMEM((8, 16, BLK), f32),
            pltpu.VMEM((8, 16, BLK), f32),
            pltpu.VMEM((views, 64, BLK), f32),
        ],
        compiler_params=params_of(24),
        name="update",
    )(gauss_params, first_moment, second_moment, own, *others)
    return (new_params, new_first, new_second, image[None])


def solution(mesh):
    placed = (
        P(None, "gs"),
        P(None, "gs"),
        P(None, "gs"),
        P("view", None),
        P("view", "gs", None),
        P("view", "gs", None),
        P("view", "gs", None, None),
    )
    return jax.shard_map(
        shards,
        mesh=mesh,
        in_specs=placed,
        out_specs=(P(None, "gs"), P(None, "gs"), P(None, "gs"), P("view", "gs", None, None)),
        check_vma=False,
    )
```

time: 742 us -> 187 us (0.25); the launches traced: 732 us -> 188 us
  other arithmetic: 249 us -> 0 us
  waiting for transfers between devices: 237 us -> 32.9 us
  matrix products: 97.4 us -> 0 us
  local copies, waits for them, and re-layouts: 102 us -> 6.77 us
  Pallas kernels: 0 us -> 70.8 us
  blocking collectives: 0 us -> 48.1 us
  between operations: 18.4 us -> 3.44 us
    all_to_all x3 -> x2, waiting for transfers between devices: 177 us -> 18.7 us  [the longest x1 18.7 us: shards(): lax.all_to_all(outgoing, 'gs', split_axis=0, concat_axis=0, tiled=True)]
    dot_general x49 -> x0, matrix products: 97.4 us -> none  [the longest x48 95.3 us: advance(): jnp.dot(feature[6:9], weights, precision=lax.Precision.HIGHEST, preferred...]
    another operation x49 -> x0, other arithmetic: 85.9 us -> none  [the longest x48 85.8 us: advance(): running = jnp.cumsum(losses, axis=0)]
    pallas_call x0 -> x6, Pallas kernels: none -> 70.8 us  [the longest x1 50.7 us: shards(): pl.pallas_call(render_kernel, out_shape=[shape((tiles, 3, PIX), f32), sha...]
    psum x1 -> x0, waiting for transfers between devices: 59.8 us -> none  [view_total(): return lax.psum(gradient, 'view')]
    reduce_sum x20 -> x0, other arithmetic: 50.4 us -> none  [the longest x16 49.8 us: advance(): offset_y = downward[None, :] - feature[1][:, None]]
    all_to_all x0 -> x1, blocking collectives: none -> 48.1 us  [shards(): landed = lax.all_to_all(back, 'gs', split_axis=0, concat_axis=0, tiled=True)]
    mul x123 -> x0, other arithmetic: 43.6 us -> none  [the longest x16 39.1 us: advance(): 0.5 * (feature[2][:, None] * offset_x * offset_x + 2.0 * feature[3][:, No...]
  transfers between devices with their start and end apart: 4 -> 5, of which waited for: 4 -> 4; matrix products, arithmetic and copies ran while one was open for 1% -> 1% of each run, Pallas kernels for 0% -> 1%
where the time goes in v1:
time: 187 us; the launch traced here: 188 us
  Pallas kernels  70.8 us (38%)
  blocking collectives  48.1 us (26%)
  waiting for transfers between devices  32.9 us (18%)
  starting transfers between devices  26.4 us (14%)
  local copies, waits for them, and re-layouts  6.77 us (4%)
  between operations  3.44 us (2%)
    pallas_call x1, Pallas kernels, shards(): pl.pallas_call(render_kernel, out_shape=[shape((tiles, 3, PIX), f32), sha...  50.7 us
    all_to_all x1, blocking collectives, shards(): landed = lax.all_to_all(back, 'gs', split_axis=0, concat_axis=0, tiled=True)  48.1 us
    all_to_all x1, waiting for transfers between devices, shards(): lax.all_to_all(outgoing, 'gs', split_axis=0, concat_axis=0, tiled=True)  18.7 us
    ppermute x3, waiting for transfers between devices, shards(): lax.ppermute(own, 'view', [((i + k) % views, i) for i in range(views)])  14.2 us
    all_to_all x1, starting transfers between devices, shards(): lax.all_to_all(wanted, 'gs', split_axis=0, concat_axis=0, tiled=True)  13.2 us
    all_to_all x1, starting transfers between devices, shards(): lax.all_to_all(outgoing, 'gs', split_axis=0, concat_axis=0, tiled=True)  10.5 us
    pallas_call x1, Pallas kernels, shards(): pl.pallas_call(update_kernel, grid=(columns // chunk,), out_shape=[shape(...  6.89 us
    pallas_call x1, Pallas kernels, shards(): pl.pallas_call(request_kernel, out_shape=[shape((groups, 1, CAP), i32), s...  5.28 us
  transfers between devices with their start and end apart: 5, of which 4 were waited for; matrix products, arithmetic and copies ran while one was open for 1% of the time, Pallas kernels for 1%

profile of v1, /device:TPU:1, one launch (start us, length us, event | category | flops | bytes accessed | tf_op | source)
XLA Modules:
  0.0 188.5 jit_solution(1735534251406909274)
XLA Ops:
  0.6 5.3 %requests.1 = (s32[64,1,2]{2,1,0:T(1,128)}, s32[8,16]{1,0:T(8,128)}, s32[8]{0:T(128)}) custom-call(s32[8,16]{1,0:T(8,128)} %bitcast.14, s32[8,16]{1,0:T(8,128)} %bitcast.15), custom_call_target="tpu_custom_call" | custom-call | tf_op jit(solution)/shard_map/requests/pallas_call | solution.py:460
  5.9 13.2 %all-to-all-start = ((s32[64,1,2]{2,1,0:T(1,128)}), s32[64,1,2]{2,1,0:T(1,128)S(1)}, u32[]{:S(2)}, u32[]{:S(2)}) async-start(s32[64,1,2]{2,1,0:T(1,128)} %get-tuple-element.12), calls=%async_computation | async-start | bytes 65536 | tf_op jit(solution)/shard_map/all_to_all | solution.py:468
  19.1 0.7 slice_bitcast_fusion
  19.8 1.3 fusion
  23.8 0.1 concatenate.3.camera_ref
  23.9 0.0 copy-start
  23.9 1.6 copy-done
  25.5 0.0 copy-start.7
  25.5 0.0 copy-start.5
  25.5 0.0 copy-start.6
  25.5 2.8 %project.1.feats_ref = f32[64,16,128]{2,1,0:T(8,128)S(1)} custom-call(f32[6]{0:T(128)S(1)} %concatenate.3.camera_ref, f32[59,8192]{1,0:T(8,128)S(1)} %copy-done), custom_call_target="tpu_custom_call" | custom-call | tf_op jit(solution)/shard_map/project/pallas_call | solution.py:469
  28.3 0.0 all-to-all-done.asked_ref
  28.3 2.1 %pick.1 = f32[64,9,2,128]{3,2,1,0:T(2,128)S(1)} custom-call(s32[64,1,2]{2,1,0:T(1,128)S(1)} %all-to-all-done.asked_ref, f32[64,16,128]{2,1,0:T(8,128)S(1)} %project.1.feats_ref), custom_call_target="tpu_custom_call" | custom-call | tf_op jit(solution)/shard_map/pick/pallas_call | solution.py:478
  30.5 0.0 copy-start.2
  30.5 0.8 copy-done.2
  31.3 0.0 copy-start.1
  31.3 10.5 %all-to-all-start.1 = ((f32[64,9,2,128]{3,2,1,0:T(2,128)}), f32[64,9,2,128]{3,2,1,0:T(2,128)S(1)}, u32[]{:S(2)}, u32[]{:S(2)}) async-start(f32[64,9,2,128]{3,2,1,0:T(2,128)} %copy-done.2), calls=%async_computation.1 | async-start | bytes 1179648 | tf_op jit(solution)/shard_map/all_to_all | solution.py:486
  41.7 0.0 copy-done.7
  41.8 18.7 %all-to-all-done.1.arrived_ref = f32[64,9,2,128]{3,2,1,0:T(2,128)S(1)} async-done(((f32[64,9,2,128]{3,2,1,0:T(2,128)}), f32[64,9,2,128]{3,2,1,0:T(2,128)S(1)}, u32[]{:S(2)}, u32[]{:S(2)}) %all-to-all-start.1) | async-done | bytes 589856 | tf_op jit(solution)/shard_map/all_to_all | solution.py:486
  60.5 0.0 copy-start.3
  60.5 0.0 copy-done.5
  60.5 0.0 copy-done.6
  60.5 50.7 %render.1 = (f32[8,3,256]{2,1,0:T(4,128)S(1)}, f32[64,9,2,128]{3,2,1,0:T(2,128)S(1)}) custom-call(s32[8,16]{1,0:T(8,128)S(1)} %copy-done.5, s32[8]{0:T(128)S(1)} %copy-done.6, f32[64,9,2,128]{3,2,1,0:T(2,128)S(1)} %all-to-all-done.1.arrived_ref, f32[8,3,256]{2,1,0:T(4,128)S(1)} %bitcast.12), custom_call_target="tpu_custom_call" | custom-call | tf_op jit(solution)/shard_map/render/pallas_call | solution.py:487
  111.2 48.1 %all_to_all.15.landed_ref = f32[64,9,2,128]{3,2,1,0:T(2,128)S(1)} all-to-all(f32[64,9,2,128]{3,2,1,0:T(2,128)S(1)} %get-tuple-element.15), channel_id=1, replica_groups=mesh['gs'=64,'view'=4] {'gs'}, dimensions={0} | all-to-all | bytes 1179648 | tf_op jit(solution)/shard_map/all_to_all | solution.py:504
  159.3 3.0 %land.1.own_ref = f32[8,10,8,128]{3,2,1,0:T(8,128)S(1)} custom-call(s32[64,1,2]{2,1,0:T(1,128)S(1)} %all-to-all-done.asked_ref, f32[6]{0:T(128)S(1)} %concatenate.3.camera_ref, f32[64,9,2,128]{3,2,1,0:T(2,128)S(1)} %all_to_all.15.landed_ref, f32[64,16,128]{2,1,0:T(8,128)S(1)} %project.1.feats_ref), custom_call_target="tpu_custom_call" | custom-call | tf_op jit(solution)/shard_map/land/pallas_call | solution.py:505
  162.4 0.1 collective-permute-start.2
  162.5 2.4 %collective-permute-start.1 = (f32[8,10,8,128]{3,2,1,0:T(8,128)S(1)}, f32[8,10,8,128]{3,2,1,0:T(8,128)S(1)}, u32[]{:S(2)}, u32[]{:S(2)}) collective-permute-start(f32[8,10,8,128]{3,2,1,0:T(8,128)S(1)} %land.1.own_ref), channel_id=1, source_target_pairs={{2,0},{3,1},{0,2},{1,3},{6,4},{7,5},{4,6},{5,7},{10,8},{11,9},{8,1... | collective-permute-start | bytes 983048 | tf_op jit(solution)/shard_map/ppermute | solution.py:515
  164.9 0.3 collective-permute-start
  165.1 0.6 copy.12
  165.7 7.1 %collective-permute-done.2.last_ref = f32[8,10,8,128]{3,2,1,0:T(8,128)S(1)} collective-permute-done((f32[8,10,8,128]{3,2,1,0:T(8,128)S(1)}, f32[8,10,8,128]{3,2,1,0:T(8,128)S(1)}, u32[]{:S(2)}, u32[]{:S(2)}) %collective-permute-start.2) | collective-permute-done | bytes 327712 | tf_op jit(solution)/shard_map/ppermute | solution.py:515
  172.9 6.5 %collective-permute-done.1.across_ref = f32[8,10,8,128]{3,2,1,0:T(8,128)S(1)} collective-permute-done((f32[8,10,8,128]{3,2,1,0:T(8,128)S(1)}, f32[8,10,8,128]{3,2,1,0:T(8,128)S(1)}, u32[]{:S(2)}, u32[]{:S(2)}) %collective-permute-start.1) | collective-permute-done | bytes 327712 | tf_op jit(solution)/shard_map/ppermute | solution.py:515
  179.4 0.6 collective-permute-done.next_ref
  180.0 0.0 copy-done.1
  180.0 0.0 copy-done.3
  180.0 0.0 copy-start.4
  180.0 1.6 copy-done.4
  181.6 6.9 %update.1 = (f32[59,8192]{1,0:T(8,128)}, f32[59,8192]{1,0:T(8,128)}, f32[59,8192]{1,0:T(8,128)}) custom-call(f32[59,8192]{1,0:T(8,128)S(1)} %copy-done.1, f32[59,8192]{1,0:T(8,128)S(1)} %copy-done.3, f32[59,8192]{1,0:T(8,128)S(1)} %copy-done.4, f32[8,10,8,128]{3,2,1,0:T(8,128)S(1)} %land.1.own_ref, f32[8,10,8,128]{3,2,1,0:T(8,128)S(1)} %collective-permute-done.next_ref, ...), custom_call_target="tpu_custom_call" | custom-call | tf_op jit(solution)/shard_map/update/pallas_call | solution.py:520
  (1 shorter events, 0.0 us)
Async XLA Ops:
  5.9 22.4 %all-to-all-start = ((s32[64,1,2]{2,1,0:T(1,128)}), s32[64,1,2]{2,1,0:T(1,128)S(1)}, u32[]{:S(2)}, u32[]{:S(2)}) async-start(s32[64,1,2]{2,1,0:T(1,128)} %get-tuple-element.12), calls=%async_computation | async-start | bytes 65536 | tf_op jit(solution)/shard_map/all_to_all | solution.py:468
  23.9 1.6 copy-start
  25.5 16.2 %copy-start.7 = (f32[1,8,3,256]{3,1,2,0:T(8,128)S(1)}, f32[1,8,3,256]{3,1,2,0:T(8,128)}, u32[]{:S(2)}) copy-start(f32[1,8,3,256]{3,1,2,0:T(8,128)} %param.13) | copy-start | bytes 73732
  25.5 35.0 %copy-start.5 = (s32[8,16]{1,0:T(8,128)S(1)}, s32[8,16]{1,0:T(8,128)}, u32[]{:S(2)}) copy-start(s32[8,16]{1,0:T(8,128)} %get-tuple-element.13.table_ref) | copy-start | bytes 1540
  25.5 35.0 %copy-start.6 = (s32[8]{0:T(128)S(1)}, s32[8]{0:T(128)}, u32[]{:S(2)}) copy-start(s32[8]{0:T(128)} %get-tuple-element.14.count_ref) | copy-start | bytes 100
  30.5 0.8 copy-start.2
  31.3 148.7 %copy-start.1 = (f32[59,8192]{1,0:T(8,128)S(1)}, f32[59,8192]{1,0:T(8,128)}, u32[]{:S(2)}) copy-start(f32[59,8192]{1,0:T(8,128)} %params_ref.3) | copy-start | bytes 5799940
  31.3 29.2 %all-to-all-start.1 = ((f32[64,9,2,128]{3,2,1,0:T(2,128)}), f32[64,9,2,128]{3,2,1,0:T(2,128)S(1)}, u32[]{:S(2)}, u32[]{:S(2)}) async-start(f32[64,9,2,128]{3,2,1,0:T(2,128)} %copy-done.2), calls=%async_computation.1 | async-start | bytes 1179648 | tf_op jit(solution)/shard_map/all_to_all | solution.py:486
  60.5 119.5 %copy-start.3 = (f32[59,8192]{1,0:T(8,128)S(1)}, f32[59,8192]{1,0:T(8,128)}, u32[]{:S(2)}) copy-start(f32[59,8192]{1,0:T(8,128)} %first_ref.1) | copy-start | bytes 5799940
  162.4 10.5 %collective-permute-start.2 = (f32[8,10,8,128]{3,2,1,0:T(8,128)S(1)}, f32[8,10,8,128]{3,2,1,0:T(8,128)S(1)}, u32[]{:S(2)}, u32[]{:S(2)}) collective-permute-start(f32[8,10,8,128]{3,2,1,0:T(8,128)S(1)} %land.1.own_ref), channel_id=1, source_target_pairs={{3,0},{0,1},{1,2},{2,3},{7,4},{4,5},{5,6},{6,7},{11,8},{8,9},{9,10... | collective-permute-start | bytes 983048 | tf_op jit(solution)/shard_map/ppermute | solution.py:515
  162.5 16.9 %collective-permute-start.1 = (f32[8,10,8,128]{3,2,1,0:T(8,128)S(1)}, f32[8,10,8,128]{3,2,1,0:T(8,128)S(1)}, u32[]{:S(2)}, u32[]{:S(2)}) collective-permute-start(f32[8,10,8,128]{3,2,1,0:T(8,128)S(1)} %land.1.own_ref), channel_id=1, source_target_pairs={{2,0},{3,1},{0,2},{1,3},{6,4},{7,5},{4,6},{5,7},{10,8},{11,9},{8,1... | collective-permute-start | bytes 983048 | tf_op jit(solution)/shard_map/ppermute | solution.py:515
  164.9 15.1 %collective-permute-start = (f32[8,10,8,128]{3,2,1,0:T(8,128)S(1)}, f32[8,10,8,128]{3,2,1,0:T(8,128)S(1)}, u32[]{:S(2)}, u32[]{:S(2)}) collective-permute-start(f32[8,10,8,128]{3,2,1,0:T(8,128)S(1)} %land.1.own_ref), channel_id=1, source_target_pairs={{1,0},{2,1},{3,2},{0,3},{5,4},{6,5},{7,6},{4,7},{9,8},{10,9},{11,1... | collective-permute-start | bytes 983048 | tf_op jit(solution)/shard_map/ppermute | solution.py:515
  180.0 1.6 copy-start.4

commit v2 on v1

--- a/solution.py
+++ b/solution.py
@@ -184,15 +184,32 @@
     lax.fori_loop(0, out_ref.shape[0], one, 0)
 
 
-def bands(lower):
-    row = lax.broadcasted_iota(jnp.int32, (BLK, 2 * BLK), 0)
-    column = lax.broadcasted_iota(jnp.int32, (BLK, 2 * BLK), 1) % BLK
-    inside = column < row if lower else column > row
+def bands(earlier):
+    row = lax.broadcasted_iota(jnp.int32, (4 * BLK, 2 * BLK), 0) % (2 * BLK)
+    column = lax.broadcasted_iota(jnp.int32, (4 * BLK, 2 * BLK), 1)
+    inside = row < column if earlier else row > column
     return inside.astype(jnp.float32).astype(jnp.bfloat16)
 
 
-def nt(a, b):
-    return lax.dot_general(a, b, (((1,), (1,)), ((), ())), preferred_element_type=jnp.float32)
+def halves_of(value):
+    high = value.astype(jnp.bfloat16)
+    low = (value - high.astype(jnp.float32)).astype(jnp.bfloat16)
+    return jnp.concatenate([high, low], axis=1)
+
+
+def sums_by(values, band):
+    rows = values[0].shape[0]
+    halves = jnp.concatenate([halves_of(value) for value in values], axis=0)
+    total = jnp.dot(halves, band[...], preferred_element_type=jnp.float32)
+    return [total[rows * h : rows * (h + 1)] for h in range(len(values))]
+
+
+def twice(value):
+    return jnp.concatenate([value, value], axis=1)
+
+
+def fold(value):
+    return jnp.sum(value.reshape(-1, 8, BLK), axis=0)
 
 
 def render_kernel(
@@ -202,142 +219,216 @@
     goal_ref,
     image_ref,
     back_ref,
+    ranked,
     before,
     after,
     basis,
-    alphas,
-    weights,
-    halves,
-    coefs,
+    *buffers,
 ):
     my_row = lax.axis_index("gs")
+    lanes = tuple(buffers[h::4] for h in range(4))
+    tiles, slots = table_ref.shape
     before[...] = bands(True)
     after[...] = bands(False)
-    pixel = lax.broadcasted_iota(jnp.int32, (8, PIX), 1)
-    place = lax.broadcasted_iota(jnp.int32, (8, PIX), 0)
+    pixel = lax.broadcasted_iota(jnp.int32, (PIX, 48), 0)
+    place = lax.broadcasted_iota(jnp.int32, (PIX, 48), 1)
     x = (pixel % 16).astype(jnp.float32) - 7.5
     y = (pixel // 16).astype(jnp.float32) - 7.5
-    terms = jnp.where(place == 0, 1.0, 0.0)
+    powers = jnp.where((place < 24) & (place % 8 == 0), 1.0, 0.0)
     for k, value in enumerate((x, y, x * x, x * y, y * y)):
-        terms = jnp.where(place == k + 1, value, terms)
-    basis[0:8] = terms
-    basis[8:16] = terms
-    basis[16:24] = terms
-    basis[24:48] = jnp.zeros((24, PIX), jnp.float32)
+        powers = jnp.where((place < 24) & (place % 8 == k + 1), value, powers)
+    basis[...] = powers.astype(jnp.bfloat16)
+    x = lax.broadcasted_iota(jnp.int32, (16, BLK), 0).astype(jnp.float32) - 7.5
+    blank = jnp.zeros((8, PIX), jnp.float32)
     back_ref[...] = jnp.zeros_like(back_ref)
-    zero = jnp.zeros((1, BLK), jnp.float32)
-
-    def fetch(t, i):
-        slot = table_ref[t, i]
-        holder, place = slot // CAP, slot % CAP
-        rows = [arrived_ref[holder, f, pl.ds(place, 1), :] for f in range(FEATS)]
-        rows[0] = rows[0] - (16 * t + 8).astype(jnp.float32)
-        rows[1] = rows[1] - (16 * my_row + 8).astype(jnp.float32)
-        return holder, place, rows
-
-    def tile(t, _):
-        used = count_ref[t]
-
-        def forward(i, carry):
-            logs, image = carry
-            _, _, (u, v, a, b, c, opacity, red, green, blue) = fetch(t, i)
-            au, bv = (a * u + b * v, b * u + c * v)
-            ks = [
-                jnp.log2(jnp.maximum(opacity, TINY)) - (0.5 * LOG2E) * (au * u + bv * v),
-                LOG2E * au,
-                LOG2E * bv,
-                (-0.5 * LOG2E) * a,
-                -LOG2E * b,
-                (-0.5 * LOG2E) * c,
-                zero,
-                zero,
+    slot_at = lax.broadcasted_iota(jnp.int32, (slots, BLK), 0)
+    for _, terms, *_ in lanes:
+        terms[...] = jnp.zeros_like(terms)
+    counts = [count_ref[t] for t in range(tiles)]
+    for t in range(tiles):
+        rank = jnp.int32(0)
+        for s in range(tiles):
+            ahead = counts[s] >= counts[t] if s < t else counts[s] > counts[t]
+            if s != t:
+                rank = rank + ahead.astype(jnp.int32)
+        ranked[rank] = t
+
+    def side_by_side(ref, at, j):
+        return jnp.concatenate(
+            [ref[at, pl.ds(2 * j + k, 1), :].reshape(-1, BLK) for k in range(2)], axis=1
+        )
+
+    def local(t, rows):
+        u = rows[0] - (16 * t + 8).astype(jnp.float32)
+        v = rows[1] - (16 * my_row + 8).astype(jnp.float32)
+        return u, v, rows[2], rows[3], rows[4]
+
+    def prepare(t, used, rows, terms):
+        for i in range(slots):
+            slot = jnp.where(i < used, table_ref[t, i], 0)
+            holder, place = slot // CAP, slot % CAP
+            for f in range(FEATS):
+                rows[f, i : i + 1, :] = arrived_ref[holder, f, pl.ds(place, 1), :]
+        u, v, a, b, d = local(t, rows)
+        au, bv = (a * u + b * v, b * u + d * v)
+        full = jnp.log2(jnp.maximum(rows[5], TINY)) - (0.5 * LOG2E) * (au * u + bv * v)
+        shape = [full, LOG2E * au, LOG2E * bv, (-0.5 * LOG2E) * a, -LOG2E * b, (-0.5 * LOG2E) * d]
+        for k, value in enumerate(shape):
+            value = jnp.where(slot_at < used, value, -2e4 if k == 0 else 0.0)
+            for p, part in enumerate(split(value, 3)):
+                terms[8 * p + k] = part
+        for k in range(3):
+            tint = jnp.where(slot_at < used, rows[6 + k], 0.0)
+            rows[6 + k] = tint
+            high, mid, low = split(tint, 3)
+            for p, part in enumerate((high, high, mid, high, low, mid)):
+                terms[24 + 3 * p + k] = part
+
+    def tile_pair(g, _):
+        chosen = [ranked[4 * g + h] for h in range(4)]
+        used = [count_ref[t] for t in chosen]
+        pairs = (functools.reduce(lax.max, used) + 1) // 2
+        for h, (rows, terms, _, _, shades, _, _) in enumerate(lanes):
+            prepare(chosen[h], used[h], rows, terms)
+            shades[...] = jnp.zeros_like(shades)
+
+        def forward(j, logs):
+            state = []
+            for rows, terms, *_ in lanes:
+                coefs = side_by_side(terms, slice(None), j).astype(jnp.bfloat16)
+                state.append(jnp.dot(basis[...], coefs, preferred_element_type=jnp.float32))
+            state = [jnp.minimum(jnp.exp2(value), BELOW_ONE) for value in state]
+            losses = [jnp.log2(1.0 - alpha) for alpha in state]
+            runs = sums_by(losses, before)
+            out = []
+            for h, (rows, _, ratios, weights, shades, _, _) in enumerate(lanes):
+                alpha, loss, run = state[h], losses[h], runs[h]
+                ratios[j] = alpha * jnp.exp2(-loss)
+                weight = alpha * jnp.exp2(run + twice(logs[h]))
+                weights[j] = weight
+                tints = side_by_side(rows, slice(6, 9), j)
+                for c in range(3):
+                    shade = weight * tints[c : c + 1]
+                    shades[c] += shade[:, 0:BLK] + shade[:, BLK:]
+                last = run[:, 2 * BLK - 1 :] + loss[:, 2 * BLK - 1 :]
+                out.append(logs[h] + jnp.broadcast_to(last, (PIX, BLK)))
+            return tuple(out)
+
+        still = jnp.zeros((PIX, BLK), jnp.float32)
+        lax.fori_loop(0, pairs, forward, (still,) * 4)
+        lane = lax.broadcasted_iota(jnp.int32, (PIX, BLK), 1)
+        pulled = []
+        for h, (_, _, _, _, shades, pulls, _) in enumerate(lanes):
+            columns = jnp.zeros((PIX, BLK), jnp.float32)
+            for c in range(3):
+                columns = jnp.where(lane == c, jnp.sum(shades[c], axis=1, keepdims=True), columns)
+            image = columns.T[0:3]
+            image_ref[chosen[h]] = image
+            pull = image - goal_ref[chosen[h]]
+            high, mid, low = split(pull, 3)
+            turned = jnp.concatenate(
+                [blank] * 3 + [high, mid, high, low, high, mid, pull, blank[0:3]], axis=0
+            ).T
+            for c in range(3):
+                pulls[c] = jnp.broadcast_to(turned[:, 42 + c : 43 + c], (PIX, BLK))
+            pulled.append(turned.astype(jnp.bfloat16))
+
+        def backward(step, later):
+            j = pairs - 1 - step
+            reaches = []
+            for h, (_, terms, _, weights, *_) in enumerate(lanes):
+                coefs = side_by_side(terms, slice(None), j).astype(jnp.bfloat16)
+                reaches.append(
+                    jnp.dot(pulled[h], coefs, preferred_element_type=jnp.float32) * weights[j]
+                )
+            behinds = sums_by(reaches, after)
+            out = []
+            for h, (_, _, ratios, weights, _, pulls, sums) in enumerate(lanes):
+                reach, behind, weight = reaches[h], behinds[h], weights[j]
+                push = reach - (behind + twice(later[h])) * ratios[j]
+                for k in range(2):
+                    at = slice(BLK * k, BLK * (k + 1))
+                    slot = pl.ds(2 * j + k, 1)
+                    part = push[:, at].reshape(16, 16, BLK)
+                    plain, tilted, bent = (None, None, None)
+                    for n in range(8):
+                        y = 7.5 - n
+                        even, odd = (part[15 - n] + part[n], y * (part[15 - n] - part[n]))
+                        square = (y * y) * even
+                        plain = even if n == 0 else plain + even
+                        tilted = odd if n == 0 else tilted + odd
+                        bent = square if n == 0 else bent + square
+                    values = (plain, x * plain, tilted, x * x * plain, x * tilted, bent)
+                    for f, value in enumerate(values):
+                        sums[f, slot] = (value[0:8] + value[8:16]).reshape(1, 8, BLK)
+                    for c in range(3):
+                        sums[6 + c, slot] = fold(weight[:, at] * pulls[c]).reshape(1, 8, BLK)
+                out.append(
+                    later[h] + jnp.broadcast_to(behind[:, 0:1] + reach[:, 0:1], (PIX, BLK))
+                )
+            return tuple(out)
+
+        lax.fori_loop(0, pairs, backward, (still,) * 4)
+        for h, (rows, _, _, _, _, _, sums) in enumerate(lanes):
+            t = chosen[h]
+            u, v, a, b, d = local(t, rows)
+            m0, mx, my, mxx, mxy, myy, red, green, blue = [
+                sum(sums[f, :, s, :] for s in range(8)) for f in range(FEATS)
             ]
-            geo = split(jnp.concatenate(ks, axis=0), 3)
-            high, mid, low = split(jnp.concatenate([red, green, blue] + [zero] * 5, axis=0), 3)
-            stack = jnp.concatenate(
-                geo + [
-                    high[0:3], high[0:3], mid[0:3], high[0:3], low[0:3], mid[0:3],
-                    jnp.zeros((6, BLK), jnp.float32),
-                ],
-                axis=0,
+            cx, cy = (mx - u * m0, my - v * m0)
+            rows[0] = a * cx + b * cy
+            rows[1] = b * cx + d * cy
+            rows[2] = -0.5 * (mxx - u * (mx + cx))
+            rows[3] = -(mxy - u * my - v * cx)
+            rows[4] = -0.5 * (myy - v * (my + cy))
+            for f, value in ((5, m0), (6, red), (7, green), (8, blue)):
+                rows[f] = value
+
+            def send(i, _, t=t, rows=rows):
+                slot = table_ref[t, i]
+                holder, place = slot // CAP, slot % CAP
+                for f in range(FEATS):
+                    back_ref[holder, f, pl.ds(place, 1), :] = rows[f, pl.ds(i, 1), :]
+                return 0
+
+            lax.fori_loop(0, used[h], send, 0)
+        return 0
+
+    lax.fori_loop(0, tiles // 4, tile_pair, 0)
+
+
+def render(table, count, arrived, goal):
+    tiles, slots = table.shape
+    groups = arrived.shape[0]
+    f32 = jnp.float32
+    shape = jax.ShapeDtypeStruct
+    return pl.pallas_call(
+        render_kernel,
+        out_shape=[shape((tiles, 3, PIX), f32), shape((groups, FEATS, CAP, BLK), f32)],
+        in_specs=[SMEM, SMEM, VMEM, VMEM],
+        out_specs=[VMEM, VMEM],
+        scratch_shapes=[
+            pltpu.SMEM((tiles,), jnp.int32),
+            pltpu.VMEM((4 * BLK, 2 * BLK), jnp.bfloat16),
+            pltpu.VMEM((4 * BLK, 2 * BLK), jnp.bfloat16),
+            pltpu.VMEM((PIX, 48), jnp.bfloat16),
+        ]
+        + [
+            pltpu.VMEM(dims, f32)
+            for dims in (
+                (FEATS, slots, BLK),
+                (48, slots, BLK),
+                (slots // 2, PIX, 2 * BLK),
+                (slots // 2, PIX, 2 * BLK),
+                (3, PIX, BLK),
+                (3, PIX, BLK),
+                (FEATS, slots, 8, BLK),
             )
-            turned = stack.T.astype(jnp.bfloat16)
-            coefs[i] = turned
-            alpha = jnp.exp2(
-                jnp.dot(turned, basis[...].astype(jnp.bfloat16), preferred_element_type=jnp.float32)
-            )
-            alpha = jnp.minimum(alpha, BELOW_ONE)
-            alphas[i] = alpha
-            loss = jnp.log2(1.0 - alpha)
-            pair = jnp.concatenate([q.astype(jnp.bfloat16) for q in split(loss, 2)], axis=0)
-            run = jnp.dot(before[...], pair, preferred_element_type=jnp.float32)
-            weight = alpha * jnp.exp2(run + logs)
-            weights[i] = weight
-            pair = jnp.concatenate([q.astype(jnp.bfloat16) for q in split(weight, 2)], axis=0)
-            halves[i] = pair
-            colours = stack[24:48].astype(jnp.bfloat16)
-            shade = jnp.dot(
-                jnp.concatenate([colours, colours], axis=1), pair, preferred_element_type=jnp.float32
-            )
-            image = image + (shade[0:3] + (shade[6:9] + shade[12:15]))
-            logs = logs + (run[BLK - 1 : BLK] + loss[BLK - 1 : BLK])
-            return logs, image
-
-        _, image = lax.fori_loop(
-            0, used, forward,
-            (jnp.zeros((1, PIX), jnp.float32), jnp.zeros((3, PIX), jnp.float32)),
-        )
-        image_ref[t] = image
-        pull = image - goal_ref[t]
-        high, mid, low = split(pull, 3)
-        pulls = jnp.concatenate(
-            [high, mid, high, low, high, mid, jnp.zeros((6, PIX), jnp.float32)], axis=0
-        )
-        basis[24:48] = pulls
-        pulled = jnp.concatenate([jnp.zeros((24, PIX), jnp.float32), pulls], axis=0).astype(
-            jnp.bfloat16
-        )
-        colour_pulls = jnp.concatenate(
-            [high, mid, low, jnp.zeros((7, PIX), jnp.float32)], axis=0
-        ).astype(jnp.bfloat16)
-        moments_of = basis[0:16].astype(jnp.bfloat16)
-
-        def backward(step, later):
-            i = used - 1 - step
-            holder, place, (u, v, a, b, c, _, _, _, _) = fetch(t, i)
-            reach = jnp.dot(coefs[i], pulled, preferred_element_type=jnp.float32) * weights[i]
-            pair = jnp.concatenate([q.astype(jnp.bfloat16) for q in split(reach, 2)], axis=0)
-            behind = jnp.dot(after[...], pair, preferred_element_type=jnp.float32)
-            alpha = alphas[i]
-            push = reach - (behind + later) * (alpha / (1.0 - alpha))
-            trio = jnp.concatenate([q.astype(jnp.bfloat16) for q in split(push, 3)], axis=0)
-            moments = nt(moments_of, trio)
-            moments = moments[:, 0:BLK] + (moments[:, BLK : 2 * BLK] + moments[:, 2 * BLK :])
-            tints = nt(colour_pulls, halves[i])
-            tints = tints[:, 0:BLK] + tints[:, BLK:]
-            tints = tints[0:3] + (tints[3:6] + tints[6:9])
-            m0, mx, my, mxx, mxy, myy = [moments[k : k + 1] for k in range(6)]
-            cx, cy = (mx - u * m0, my - v * m0)
-            grads = [
-                a * cx + b * cy,
-                b * cx + c * cy,
-                -0.5 * (mxx - u * (mx + cx)),
-                -(mxy - u * my - v * cx),
-                -0.5 * (myy - v * (my + cy)),
-                m0,
-                tints[0:1],
-                tints[1:2],
-                tints[2:3],
-            ]
-            for f, value in enumerate(grads):
-                back_ref[holder, f, pl.ds(place, 1), :] = value
-            return later + (behind[0:1] + reach[0:1])
-
-        lax.fori_loop(0, used, backward, jnp.zeros((1, PIX), jnp.float32))
-        basis[24:48] = jnp.zeros((24, PIX), jnp.float32)
-        return 0
-
-    lax.fori_loop(0, image_ref.shape[0], tile, 0)
+            for _ in range(4)
+        ],
+        compiler_params=params_of(48),
+        name="render",
+    )(table, count, arrived, goal)
 
 
 def land_kernel(asked_ref, camera_ref, landed_ref, feats_ref, out_ref, total):
@@ -484,23 +575,7 @@
         name="pick",
     )(asked, feats)
     arrived = lax.all_to_all(outgoing, "gs", split_axis=0, concat_axis=0, tiled=True)
-    image, back = pl.pallas_call(
-        render_kernel,
-        out_shape=[shape((tiles, 3, PIX), f32), shape((groups, FEATS, CAP, BLK), f32)],
-        in_specs=[SMEM, SMEM, VMEM, VMEM],
-        out_specs=[VMEM, VMEM],
-        scratch_shapes=[
-            pltpu.VMEM((BLK, 2 * BLK), jnp.bfloat16),
-            pltpu.VMEM((BLK, 2 * BLK), jnp.bfloat16),
-            pltpu.VMEM((48, PIX), f32),
-            pltpu.VMEM((slots, BLK, PIX), f32),
-            pltpu.VMEM((slots, BLK, PIX), f32),
-            pltpu.VMEM((slots, 2 * BLK, PIX), jnp.bfloat16),
-            pltpu.VMEM((slots, BLK, 48), jnp.bfloat16),
-        ],
-        compiler_params=params_of(32),
-        name="render",
-    )(table, count, arrived, target_image[0])
+    image, back = render(table, count, arrived, target_image[0])
     landed = lax.all_to_all(back, "gs", split_axis=0, concat_axis=0, tiled=True)
     own = pl.pallas_call(
         land_kernel,

time: 187 us -> 146 us (0.78); the launches traced: 188 us -> 145 us
  blocking collectives: 48.1 us -> 24.2 us
  Pallas kernels: 70.8 us -> 50.8 us
    all_to_all x1, blocking collectives: 48.1 us -> 24.2 us  [shards(): landed = lax.all_to_all(back, 'gs', split_axis=0, concat_axis=0, tiled=True)]
    pallas_call x1, Pallas kernels: 50.7 us -> 30.6 us  [render(): pl.pallas_call(render_kernel, out_shape=[shape((tiles, 3, PIX), f32), sha...]
  transfers between devices with their start and end apart: 5 -> 5, of which waited for: 4 -> 3; matrix products, arithmetic and copies ran while one was open for 1% -> 2% of each run, Pallas kernels for 1% -> 2%
where the time goes in v2:
time: 146 us; the launch traced here: 145 us
  Pallas kernels  50.8 us (35%)
  waiting for transfers between devices  31.5 us (22%)
  starting transfers between devices  28.1 us (19%)
  blocking collectives  24.2 us (17%)
  local copies, waits for them, and re-layouts  6.76 us (5%)
  between operations  3.44 us (2%)
    pallas_call x1, Pallas kernels, render(): pl.pallas_call(render_kernel, out_shape=[shape((tiles, 3, PIX), f32), sha...  30.6 us
    all_to_all x1, blocking collectives, shards(): landed = lax.all_to_all(back, 'gs', split_axis=0, concat_axis=0, tiled=True)  24.2 us
    all_to_all x1, waiting for transfers between devices, shards(): lax.all_to_all(outgoing, 'gs', split_axis=0, concat_axis=0, tiled=True)  18.7 us
    all_to_all x1, starting transfers between devices, shards(): lax.all_to_all(wanted, 'gs', split_axis=0, concat_axis=0, tiled=True)  13.2 us
    ppermute x3, waiting for transfers between devices, shards(): lax.ppermute(own, 'view', [((i + k) % views, i) for i in range(views)])  12.8 us
    all_to_all x1, starting transfers between devices, shards(): lax.all_to_all(outgoing, 'gs', split_axis=0, concat_axis=0, tiled=True)  10.5 us
    pallas_call x1, Pallas kernels, shards(): pl.pallas_call(update_kernel, grid=(columns // chunk,), out_shape=[shape(...  6.89 us
    pallas_call x1, Pallas kernels, shards(): pl.pallas_call(request_kernel, out_shape=[shape((groups, 1, CAP), i32), s...  5.28 us
  transfers between devices with their start and end apart: 5, of which 3 were waited for; matrix products, arithmetic and copies ran while one was open for 2% of the time, Pallas kernels for 2%

profile of v2, /device:TPU:1, one launch (start us, length us, event | category | flops | bytes accessed | tf_op | source)
XLA Modules:
  0.0 144.7 jit_solution(6040152092992362270)
XLA Ops:
  0.6 5.3 %requests.1 = (s32[64,1,2]{2,1,0:T(1,128)}, s32[8,16]{1,0:T(8,128)}, s32[8]{0:T(128)}) custom-call(s32[8,16]{1,0:T(8,128)} %bitcast.14, s32[8,16]{1,0:T(8,128)} %bitcast.15), custom_call_target="tpu_custom_call" | custom-call | tf_op jit(solution)/shard_map/requests/pallas_call | solution.py:551
  5.9 13.2 %all-to-all-start = ((s32[64,1,2]{2,1,0:T(1,128)}), s32[64,1,2]{2,1,0:T(1,128)S(1)}, u32[]{:S(2)}, u32[]{:S(2)}) async-start(s32[64,1,2]{2,1,0:T(1,128)} %get-tuple-element.12), calls=%async_computation | async-start | bytes 65536 | tf_op jit(solution)/shard_map/all_to_all | solution.py:559
  19.1 0.7 slice_bitcast_fusion
  19.8 1.3 fusion
  23.8 0.1 concatenate.3.camera_ref
  23.9 0.0 copy-start
  23.9 1.6 %copy-done = f32[59,8192]{1,0:T(8,128)S(1)} copy-done((f32[59,8192]{1,0:T(8,128)S(1)}, f32[59,8192]{1,0:T(8,128)}, u32[]{:S(2)}) %copy-start) | copy-done | bytes 1933336
  25.5 0.0 copy-start.7
  25.5 0.0 copy-start.5
  25.5 0.0 copy-start.6
  25.5 2.8 %project.1.feats_ref = f32[64,16,128]{2,1,0:T(8,128)S(1)} custom-call(f32[6]{0:T(128)S(1)} %concatenate.3.camera_ref, f32[59,8192]{1,0:T(8,128)S(1)} %copy-done), custom_call_target="tpu_custom_call" | custom-call | tf_op jit(solution)/shard_map/project/pallas_call | solution.py:560
  28.3 0.0 all-to-all-done.asked_ref
  28.3 2.1 %pick.1 = f32[64,9,2,128]{3,2,1,0:T(2,128)S(1)} custom-call(s32[64,1,2]{2,1,0:T(1,128)S(1)} %all-to-all-done.asked_ref, f32[64,16,128]{2,1,0:T(8,128)S(1)} %project.1.feats_ref), custom_call_target="tpu_custom_call" | custom-call | tf_op jit(solution)/shard_map/pick/pallas_call | solution.py:569
  30.5 0.0 copy-start.2
  30.5 0.8 copy-done.2
  31.3 0.0 copy-start.1
  31.3 10.5 %all-to-all-start.1 = ((f32[64,9,2,128]{3,2,1,0:T(2,128)}), f32[64,9,2,128]{3,2,1,0:T(2,128)S(1)}, u32[]{:S(2)}, u32[]{:S(2)}) async-start(f32[64,9,2,128]{3,2,1,0:T(2,128)} %copy-done.2), calls=%async_computation.1 | async-start | bytes 1179648 | tf_op jit(solution)/shard_map/all_to_all | solution.py:577
  41.7 0.0 copy-done.7
  41.8 18.7 %all-to-all-done.1.arrived_ref = f32[64,9,2,128]{3,2,1,0:T(2,128)S(1)} async-done(((f32[64,9,2,128]{3,2,1,0:T(2,128)}), f32[64,9,2,128]{3,2,1,0:T(2,128)S(1)}, u32[]{:S(2)}, u32[]{:S(2)}) %all-to-all-start.1) | async-done | bytes 589856 | tf_op jit(solution)/shard_map/all_to_all | solution.py:577
  60.5 0.0 copy-start.3
  60.5 0.0 copy-done.5
  60.5 0.0 copy-done.6
  60.5 30.6 %render.1 = (f32[8,3,256]{2,1,0:T(4,128)S(1)}, f32[64,9,2,128]{3,2,1,0:T(2,128)S(1)}) custom-call(s32[8,16]{1,0:T(8,128)S(1)} %copy-done.5, s32[8]{0:T(128)S(1)} %copy-done.6, f32[64,9,2,128]{3,2,1,0:T(2,128)S(1)} %all-to-all-done.1.arrived_ref, f32[8,3,256]{2,1,0:T(4,128)S(1)} %bitcast.12), custom_call_target="tpu_custom_call" | custom-call | tf_op jit(solution)/shard_map/render/pallas_call | solution.py:405
  91.1 24.2 %all_to_all.15.landed_ref = f32[64,9,2,128]{3,2,1,0:T(2,128)S(1)} all-to-all(f32[64,9,2,128]{3,2,1,0:T(2,128)S(1)} %get-tuple-element.15), channel_id=1, replica_groups=mesh['gs'=64,'view'=4] {'gs'}, dimensions={0} | all-to-all | bytes 1179648 | tf_op jit(solution)/shard_map/all_to_all | solution.py:579
  115.3 3.0 %land.1.own_ref = f32[8,10,8,128]{3,2,1,0:T(8,128)S(1)} custom-call(s32[64,1,2]{2,1,0:T(1,128)S(1)} %all-to-all-done.asked_ref, f32[6]{0:T(128)S(1)} %concatenate.3.camera_ref, f32[64,9,2,128]{3,2,1,0:T(2,128)S(1)} %all_to_all.15.landed_ref, f32[64,16,128]{2,1,0:T(8,128)S(1)} %project.1.feats_ref), custom_call_target="tpu_custom_call" | custom-call | tf_op jit(solution)/shard_map/land/pallas_call | solution.py:580
  118.4 0.6 collective-permute-start.2
  118.9 2.7 %collective-permute-start.1 = (f32[8,10,8,128]{3,2,1,0:T(8,128)S(1)}, f32[8,10,8,128]{3,2,1,0:T(8,128)S(1)}, u32[]{:S(2)}, u32[]{:S(2)}) collective-permute-start(f32[8,10,8,128]{3,2,1,0:T(8,128)S(1)} %land.1.own_ref), channel_id=1, source_target_pairs={{2,0},{3,1},{0,2},{1,3},{6,4},{7,5},{4,6},{5,7},{10,8},{11,9},{8,1... | collective-permute-start | bytes 983048 | tf_op jit(solution)/shard_map/ppermute | solution.py:590
  121.7 1.2 collective-permute-start
  122.8 0.6 copy.12
  123.4 5.2 %collective-permute-done.2.last_ref = f32[8,10,8,128]{3,2,1,0:T(8,128)S(1)} collective-permute-done((f32[8,10,8,128]{3,2,1,0:T(8,128)S(1)}, f32[8,10,8,128]{3,2,1,0:T(8,128)S(1)}, u32[]{:S(2)}, u32[]{:S(2)}) %collective-permute-start.2) | collective-permute-done | bytes 327712 | tf_op jit(solution)/shard_map/ppermute | solution.py:590
  128.6 7.5 %collective-permute-done.1.across_ref = f32[8,10,8,128]{3,2,1,0:T(8,128)S(1)} collective-permute-done((f32[8,10,8,128]{3,2,1,0:T(8,128)S(1)}, f32[8,10,8,128]{3,2,1,0:T(8,128)S(1)}, u32[]{:S(2)}, u32[]{:S(2)}) %collective-permute-start.1) | collective-permute-done | bytes 327712 | tf_op jit(solution)/shard_map/ppermute | solution.py:590
  136.2 0.0 collective-permute-done.next_ref
  136.2 0.0 copy-done.1
  136.2 0.0 copy-done.3
  136.2 0.0 copy-start.4
  136.2 1.6 %copy-done.4 = f32[59,8192]{1,0:T(8,128)S(1)} copy-done((f32[59,8192]{1,0:T(8,128)S(1)}, f32[59,8192]{1,0:T(8,128)}, u32[]{:S(2)}) %copy-start.4) | copy-done | bytes 1933336
  137.8 6.9 %update.1 = (f32[59,8192]{1,0:T(8,128)}, f32[59,8192]{1,0:T(8,128)}, f32[59,8192]{1,0:T(8,128)}) custom-call(f32[59,8192]{1,0:T(8,128)S(1)} %copy-done.1, f32[59,8192]{1,0:T(8,128)S(1)} %copy-done.3, f32[59,8192]{1,0:T(8,128)S(1)} %copy-done.4, f32[8,10,8,128]{3,2,1,0:T(8,128)S(1)} %land.1.own_ref, f32[8,10,8,128]{3,2,1,0:T(8,128)S(1)} %collective-permute-done.next_ref, ...), custom_call_target="tpu_custom_call" | custom-call | tf_op jit(solution)/shard_map/update/pallas_call | solution.py:595
  (1 shorter events, 0.0 us)
Async XLA Ops:
  5.9 22.4 %all-to-all-start = ((s32[64,1,2]{2,1,0:T(1,128)}), s32[64,1,2]{2,1,0:T(1,128)S(1)}, u32[]{:S(2)}, u32[]{:S(2)}) async-start(s32[64,1,2]{2,1,0:T(1,128)} %get-tuple-element.12), calls=%async_computation | async-start | bytes 65536 | tf_op jit(solution)/shard_map/all_to_all | solution.py:559
  23.9 1.6 %copy-start = (f32[59,8192]{1,0:T(8,128)S(1)}, f32[59,8192]{1,0:T(8,128)}, u32[]{:S(2)}) copy-start(f32[59,8192]{1,0:T(8,128)} %params_ref.3) | copy-start | bytes 5799940
  25.5 16.2 %copy-start.7 = (f32[1,8,3,256]{3,1,2,0:T(8,128)S(1)}, f32[1,8,3,256]{3,1,2,0:T(8,128)}, u32[]{:S(2)}) copy-start(f32[1,8,3,256]{3,1,2,0:T(8,128)} %param.13) | copy-start | bytes 73732
  25.5 35.0 %copy-start.5 = (s32[8,16]{1,0:T(8,128)S(1)}, s32[8,16]{1,0:T(8,128)}, u32[]{:S(2)}) copy-start(s32[8,16]{1,0:T(8,128)} %get-tuple-element.13.table_ref) | copy-start | bytes 1540
  25.5 35.0 %copy-start.6 = (s32[8]{0:T(128)S(1)}, s32[8]{0:T(128)}, u32[]{:S(2)}) copy-start(s32[8]{0:T(128)} %get-tuple-element.14.count_ref) | copy-start | bytes 100
  30.5 0.8 copy-start.2
  31.3 104.9 %copy-start.1 = (f32[59,8192]{1,0:T(8,128)S(1)}, f32[59,8192]{1,0:T(8,128)}, u32[]{:S(2)}) copy-start(f32[59,8192]{1,0:T(8,128)} %params_ref.3) | copy-start | bytes 5799940
  31.3 29.2 %all-to-all-start.1 = ((f32[64,9,2,128]{3,2,1,0:T(2,128)}), f32[64,9,2,128]{3,2,1,0:T(2,128)S(1)}, u32[]{:S(2)}, u32[]{:S(2)}) async-start(f32[64,9,2,128]{3,2,1,0:T(2,128)} %copy-done.2), calls=%async_computation.1 | async-start | bytes 1179648 | tf_op jit(solution)/shard_map/all_to_all | solution.py:577
  60.5 75.7 %copy-start.3 = (f32[59,8192]{1,0:T(8,128)S(1)}, f32[59,8192]{1,0:T(8,128)}, u32[]{:S(2)}) copy-start(f32[59,8192]{1,0:T(8,128)} %first_ref.1) | copy-start | bytes 5799940
  118.4 10.3 %collective-permute-start.2 = (f32[8,10,8,128]{3,2,1,0:T(8,128)S(1)}, f32[8,10,8,128]{3,2,1,0:T(8,128)S(1)}, u32[]{:S(2)}, u32[]{:S(2)}) collective-permute-start(f32[8,10,8,128]{3,2,1,0:T(8,128)S(1)} %land.1.own_ref), channel_id=1, source_target_pairs={{3,0},{0,1},{1,2},{2,3},{7,4},{4,5},{5,6},{6,7},{11,8},{8,9},{9,10... | collective-permute-start | bytes 983048 | tf_op jit(solution)/shard_map/ppermute | solution.py:590
  118.9 17.2 %collective-permute-start.1 = (f32[8,10,8,128]{3,2,1,0:T(8,128)S(1)}, f32[8,10,8,128]{3,2,1,0:T(8,128)S(1)}, u32[]{:S(2)}, u32[]{:S(2)}) collective-permute-start(f32[8,10,8,128]{3,2,1,0:T(8,128)S(1)} %land.1.own_ref), channel_id=1, source_target_pairs={{2,0},{3,1},{0,2},{1,3},{6,4},{7,5},{4,6},{5,7},{10,8},{11,9},{8,1... | collective-permute-start | bytes 983048 | tf_op jit(solution)/shard_map/ppermute | solution.py:590
  121.7 14.5 %collective-permute-start = (f32[8,10,8,128]{3,2,1,0:T(8,128)S(1)}, f32[8,10,8,128]{3,2,1,0:T(8,128)S(1)}, u32[]{:S(2)}, u32[]{:S(2)}) collective-permute-start(f32[8,10,8,128]{3,2,1,0:T(8,128)S(1)} %land.1.own_ref), channel_id=1, source_target_pairs={{1,0},{2,1},{3,2},{0,3},{5,4},{6,5},{7,6},{4,7},{9,8},{10,9},{11,1... | collective-permute-start | bytes 983048 | tf_op jit(solution)/shard_map/ppermute | solution.py:590
  136.2 1.6 %copy-start.4 = (f32[59,8192]{1,0:T(8,128)S(1)}, f32[59,8192]{1,0:T(8,128)}, u32[]{:S(2)}) copy-start(f32[59,8192]{1,0:T(8,128)} %second_ref.1) | copy-start | bytes 5799940

commit v3 on v2

--- a/solution.py
+++ b/solution.py
@@ -23,6 +23,10 @@
 LOG2E = 1.4426950408889634
 TINY = 1.1754944e-38
 BELOW_ONE = 0.99999994
+PROJECT_MB = 56
+UPDATE_MB = 24
+PROJECT_BLOCKS = 32
+UPDATE_BLOCKS = 8
 
 VMEM = pl.BlockSpec(memory_space=pltpu.VMEM)
 SMEM = pl.BlockSpec(memory_space=pltpu.SMEM)
@@ -54,17 +58,24 @@
     ]
 
 
-def geometry(rows, camera):
-    sin_yaw, cos_yaw, sin_tilt, cos_tilt, shift_x, shift_y = camera
-    right_axis = (cos_yaw, 0.0 * cos_yaw, -sin_yaw)
-    upward = (sin_yaw * sin_tilt, cos_tilt, cos_yaw * sin_tilt)
-    across = (
-        16.0 * (right_axis[0] * rows[0] + right_axis[1] * rows[1] + right_axis[2] * rows[2])
-        + shift_x
-    )
-    downward = 16.0 * (upward[0] * rows[0] + upward[1] * rows[1] + upward[2] * rows[2]) + shift_y
-    scales = [jnp.exp(rows[3]), jnp.exp(rows[4]), jnp.exp(rows[5])]
-    w, x, y, z = rows[6:10]
+def camera_of(pose_ref):
+    yaw, tilt, shift_x, shift_y = [jnp.full((1, BLK), pose_ref[0, k]) for k in range(4)]
+    return [jnp.sin(yaw), jnp.cos(yaw), jnp.sin(tilt), jnp.cos(tilt), shift_x, shift_y]
+
+
+def look_terms(camera):
+    sin_yaw, cos_yaw, sin_tilt, cos_tilt = camera[0:4]
+    return harmonics(sin_yaw * cos_tilt, -sin_tilt, cos_yaw * cos_tilt)
+
+
+def axes(camera):
+    sin_yaw, cos_yaw, sin_tilt, cos_tilt = camera[0:4]
+    return (cos_yaw, -sin_yaw), (sin_yaw * sin_tilt, cos_tilt, cos_yaw * sin_tilt)
+
+
+def frame(*rows):
+    scales = [16.0 * jnp.exp(value) for value in rows[0:3]]
+    w, x, y, z = rows[3:7]
     inverse = lax.rsqrt(jnp.maximum(w * w + x * x + y * y + z * z, 1.0))
     w, x, y, z = (w * inverse, x * inverse, y * inverse, z * inverse)
     rotation = (
@@ -72,30 +83,28 @@
         (2.0 * (x * y + w * z), 1.0 - 2.0 * (x * x + z * z), 2.0 * (y * z - w * x)),
         (2.0 * (x * z - w * y), 2.0 * (y * z + w * x), 1.0 - 2.0 * (x * x + y * y)),
     )
-    first, second = [
-        [
-            16.0
-            * scales[k]
-            * (
-                direction[0] * rotation[0][k]
-                + direction[1] * rotation[1][k]
-                + direction[2] * rotation[2][k]
-            )
-            for k in range(3)
-        ]
-        for direction in (right_axis, upward)
+    return tuple(scales[k] * rotation[r][k] for r in range(3) for k in range(3))
+
+
+def conic(matrix, camera):
+    right, upward = axes(camera)
+    first = [right[0] * matrix[k] + right[1] * matrix[6 + k] for k in range(3)]
+    second = [
+        upward[0] * matrix[k] + upward[1] * matrix[3 + k] + upward[2] * matrix[6 + k]
+        for k in range(3)
     ]
     spread_first = first[0] * first[0] + first[1] * first[1] + first[2] * first[2] + dilation
     spread_mixed = first[0] * second[0] + first[1] * second[1] + first[2] * second[2]
     spread_second = second[0] * second[0] + second[1] * second[1] + second[2] * second[2] + dilation
     determinant = spread_first * spread_second - spread_mixed * spread_mixed
-    return [
-        across,
-        downward,
-        spread_second / determinant,
-        -spread_mixed / determinant,
-        spread_first / determinant,
-    ]
+    return (spread_second / determinant, -spread_mixed / determinant, spread_first / determinant)
+
+
+def geometry(rows, camera):
+    right, upward = axes(camera)
+    across = 16.0 * (right[0] * rows[0] + right[1] * rows[2]) + camera[4]
+    downward = 16.0 * (upward[0] * rows[0] + upward[1] * rows[1] + upward[2] * rows[2]) + camera[5]
+    return [across, downward, *conic(frame(*rows[3:10]), camera)]
 
 
 def split(value, parts):
@@ -108,70 +117,91 @@
     return out
 
 
-def request_kernel(blocks_ref, order_ref, wanted_ref, table_ref, count_ref, held_ref):
+def request_kernel(blocks_ref, order_ref, wanted_ref, table_ref, count_ref):
+    tiles, slots = blocks_ref.shape
     holders = wanted_ref.shape[0]
-    tiles, slots = blocks_ref.shape
-    per_holder = 64
-
-    def clear(h, _):
-        wanted_ref[h, 0, 0] = -1
-        wanted_ref[h, 0, 1] = -1
-        held_ref[h] = 0
-        return 0
-
-    lax.fori_loop(0, holders, clear, 0)
-
-    def tile(t, _):
-        def slot(i, used):
-            block = blocks_ref[t, order_ref[t, i]]
-            holder = lax.max(block, 0) // per_holder
-            position = held_ref[holder]
-
-            @pl.when(block >= 0)
-            def _():
-                held_ref[holder] = position + 1
-                wanted_ref[holder, 0, position] = block - holder * per_holder
-                table_ref[t, used] = holder * CAP + position
-
-            return used + (block >= 0).astype(jnp.int32)
-
-        count_ref[t] = lax.fori_loop(0, slots, slot, jnp.int32(0))
-        return 0
-
-    lax.fori_loop(0, tiles, tile, 0)
-
-
-def project_kernel(camera_ref, params_ref, feats_ref, turned):
-    blocks = feats_ref.shape[0]
-    sin_yaw, cos_yaw, sin_tilt, cos_tilt = [camera_ref[k] for k in range(4)]
-    camera = [camera_ref[k] for k in range(6)]
-    terms = harmonics(sin_yaw * cos_tilt, -sin_tilt, cos_yaw * cos_tilt)
-    row = lax.broadcasted_iota(jnp.int32, (8, PARAMS), 0)
-    column = lax.broadcasted_iota(jnp.int32, (8, PARAMS), 1)
-    which = column - 11 - 16 * row
-    weight = jnp.zeros((8, PARAMS), jnp.float32)
-    for j in range(16):
-        weight = jnp.where((which == j) & (row < 3), terms[j], weight)
-    for j in range(blocks):
+    count = tiles * slots
+    by_holder = 6
+    by_tile = 4
+
+    def flat(ref):
+        return jnp.concatenate([ref[t : t + 1, :] for t in range(tiles)], axis=1)
+
+    def spread(row):
+        return jnp.broadcast_to(row, (count, count))
+
+    def add(keep, value, axis):
+        return jnp.sum(jnp.where(keep, value, 0.0), axis=axis, keepdims=True)
+
+    def whole(value):
+        return value.astype(jnp.int32)
+
+    row = lax.broadcasted_iota(jnp.int32, (count, count), 0)
+    lane = lax.broadcasted_iota(jnp.int32, (count, count), 1)
+    row_tile, lane_tile = (row >> by_tile, lane >> by_tile)
+    block = spread(flat(blocks_ref))
+    holder = block >> by_holder
+    earlier = whole(add((holder.T == holder) & (row < lane), 1.0, 0))
+    slot = spread(jnp.where(block[0:1] >= 0, holder[0:1] * CAP + earlier, -1))
+    within = (block - (holder << by_holder) + 1).astype(jnp.float32)
+    wanted = [
+        whole(add(slot[0:holders] == CAP * row[0:holders] + c, within[0:holders], 1)) - 1
+        for c in range(CAP)
+    ]
+    wanted = jnp.where(lane[0:holders] == 0, wanted[0], wanted[1])
+    for h in range(holders):
+        wanted_ref[h] = wanted[h : h + 1, 0:CAP]
+    filled = add(slot.T == lane, 1.0, 0)
+    spare = jnp.max(
+        jnp.where(filled > 0.0, 0.0, lane[0:1].astype(jnp.float32)), axis=1, keepdims=True
+    )
+    place = spread(flat(order_ref) + (lane_tile[0:1] << by_tile)).T
+    chosen = add(place == lane, (slot + 1).astype(jnp.float32), 1) - 1.0
+    used = jnp.broadcast_to((chosen >= 0.0).astype(jnp.float32), (count, count))
+    same = row_tile == lane_tile
+    rank = whole(add(same & (lane < row), used.T, 1))
+    target = jnp.where(chosen >= 0.0, (row[:, 0:1] & -slots) + rank, -1)
+    table_ref[...] = whole(add(target == lane, chosen - spare, 0) + spare)
+    count_ref[...] = whole(add(row_tile == lane, used, 0))
+
+
+def project_kernel(pose_ref, params_ref, feats_ref, turned, seen, weight):
+    @pl.when(pl.program_id(0) == 0)
+    def _():
+        camera = camera_of(pose_ref)
+        for k in range(6):
+            seen[k : k + 1, :] = camera[k]
+        terms = look_terms(camera)
+        for c in range(3):
+            row = lax.broadcasted_iota(jnp.int32, (24, BLK), 0) - 3
+            value = jnp.zeros((24, BLK), jnp.float32)
+            for j in range(16):
+                value = jnp.where(row == j, terms[j], value)
+            weight[c] = value
+
+    camera = [seen[k : k + 1, :] for k in range(6)]
+    for j in range(PROJECT_BLOCKS):
         turned[j] = params_ref[0:16, j * BLK : (j + 1) * BLK]
-    chunk = 8 * BLK
-    for g in range(blocks // 8):
-        shade = 0.5 + jnp.dot(
-            weight,
-            params_ref[:, g * chunk : (g + 1) * chunk],
-            precision=lax.Precision.HIGHEST,
-            preferred_element_type=jnp.float32,
-        )
-        mask = jnp.where(shade > 0.0, 1.0, jnp.where(shade == 0.0, 0.5, 0.0))
-        shade = jnp.maximum(shade, 0.0)
-        for j in range(8):
-            feats_ref[8 * g + j, 6:9, :] = shade[0:3, j * BLK : (j + 1) * BLK]
-            feats_ref[8 * g + j, 9:12, :] = mask[0:3, j * BLK : (j + 1) * BLK]
-        rows = [turned[8 * g : 8 * g + 8, r, :] for r in range(11)]
-        shaped = geometry(rows, camera)
-        opacity = 1.0 / (1.0 + jnp.exp(-rows[10]))
-        for r, value in enumerate(shaped + [opacity]):
-            feats_ref[8 * g : 8 * g + 8, r, :] = value
+    for j in range(PROJECT_BLOCKS):
+        columns = slice(j * BLK, (j + 1) * BLK)
+        for c in range(3):
+            low = 16 * c + 8
+            high = min(low + 24, PARAMS)
+            terms = params_ref[low : low + 16, columns] * weight[c, 0:16]
+            ends = params_ref[low + 16 : high, columns] * weight[c, 16 : high - low]
+            terms = terms[0:8] + terms[8:16]
+            if high - low == 24:
+                shade = jnp.sum(terms + ends, axis=0, keepdims=True)
+            else:
+                shade = jnp.sum(terms, axis=0, keepdims=True) + jnp.sum(ends, axis=0, keepdims=True)
+            shade = 0.5 + shade
+            mask = jnp.where(shade > 0.0, 1.0, jnp.where(shade == 0.0, 0.5, 0.0))
+            feats_ref[j, 6 + c : 7 + c, :] = jnp.maximum(shade, 0.0)
+            feats_ref[j, 9 + c : 10 + c, :] = mask
+    rows = [turned[:, r, :] for r in range(11)]
+    opacity = 1.0 / (1.0 + jnp.exp(-rows[10]))
+    for r, value in enumerate(geometry(rows, camera) + [opacity]):
+        feats_ref[:, r, :] = value
 
 
 def pick_kernel(asked_ref, feats_ref, out_ref):
@@ -181,7 +211,7 @@
             out_ref[h, :, c, :] = feats_ref[block][0:FEATS]
         return 0
 
-    lax.fori_loop(0, out_ref.shape[0], one, 0)
+    lax.fori_loop(0, out_ref.shape[0], one, 0, unroll=8)
 
 
 def bands(earlier):
@@ -227,7 +257,8 @@
 ):
     my_row = lax.axis_index("gs")
     lanes = tuple(buffers[h::4] for h in range(4))
-    tiles, slots = table_ref.shape
+    tiles = goal_ref.shape[1]
+    slots = table_ref.shape[1] // tiles
     before[...] = bands(True)
     after[...] = bands(False)
     pixel = lax.broadcasted_iota(jnp.int32, (PIX, 48), 0)
@@ -240,11 +271,10 @@
     basis[...] = powers.astype(jnp.bfloat16)
     x = lax.broadcasted_iota(jnp.int32, (16, BLK), 0).astype(jnp.float32) - 7.5
     blank = jnp.zeros((8, PIX), jnp.float32)
-    back_ref[...] = jnp.zeros_like(back_ref)
     slot_at = lax.broadcasted_iota(jnp.int32, (slots, BLK), 0)
     for _, terms, *_ in lanes:
         terms[...] = jnp.zeros_like(terms)
-    counts = [count_ref[t] for t in range(tiles)]
+    counts = [count_ref[0, t] for t in range(tiles)]
     for t in range(tiles):
         rank = jnp.int32(0)
         for s in range(tiles):
@@ -265,7 +295,7 @@
 
     def prepare(t, used, rows, terms):
         for i in range(slots):
-            slot = jnp.where(i < used, table_ref[t, i], 0)
+            slot = table_ref[0, t * slots + i]
             holder, place = slot // CAP, slot % CAP
             for f in range(FEATS):
                 rows[f, i : i + 1, :] = arrived_ref[holder, f, pl.ds(place, 1), :]
@@ -286,7 +316,7 @@
 
     def tile_pair(g, _):
         chosen = [ranked[4 * g + h] for h in range(4)]
-        used = [count_ref[t] for t in chosen]
+        used = [count_ref[0, t] for t in chosen]
         pairs = (functools.reduce(lax.max, used) + 1) // 2
         for h, (rows, terms, _, _, shades, _, _) in enumerate(lanes):
             prepare(chosen[h], used[h], rows, terms)
@@ -323,8 +353,10 @@
             for c in range(3):
                 columns = jnp.where(lane == c, jnp.sum(shades[c], axis=1, keepdims=True), columns)
             image = columns.T[0:3]
-            image_ref[chosen[h]] = image
-            pull = image - goal_ref[chosen[h]]
+            at = pl.ds(chosen[h], 1)
+            for c in range(3):
+                image_ref[c, at, :] = image[c : c + 1]
+            pull = image - jnp.concatenate([goal_ref[c, at, :] for c in range(3)], axis=0)
             high, mid, low = split(pull, 3)
             turned = jnp.concatenate(
                 [blank] * 3 + [high, mid, high, low, high, mid, pull, blank[0:3]], axis=0
@@ -384,27 +416,25 @@
             for f, value in ((5, m0), (6, red), (7, green), (8, blue)):
                 rows[f] = value
 
-            def send(i, _, t=t, rows=rows):
-                slot = table_ref[t, i]
+            for i in range(slots):
+                slot = table_ref[0, t * slots + i]
                 holder, place = slot // CAP, slot % CAP
                 for f in range(FEATS):
-                    back_ref[holder, f, pl.ds(place, 1), :] = rows[f, pl.ds(i, 1), :]
-                return 0
-
-            lax.fori_loop(0, used[h], send, 0)
+                    back_ref[holder, f, pl.ds(place, 1), :] = rows[f, i : i + 1, :]
         return 0
 
     lax.fori_loop(0, tiles // 4, tile_pair, 0)
 
 
 def render(table, count, arrived, goal):
-    tiles, slots = table.shape
+    tiles = goal.shape[1]
+    slots = table.shape[1] // tiles
     groups = arrived.shape[0]
     f32 = jnp.float32
     shape = jax.ShapeDtypeStruct
     return pl.pallas_call(
         render_kernel,
-        out_shape=[shape((tiles, 3, PIX), f32), shape((groups, FEATS, CAP, BLK), f32)],
+        out_shape=[shape((3, tiles, PIX), f32), shape((groups, FEATS, CAP, BLK), f32)],
         in_specs=[SMEM, SMEM, VMEM, VMEM],
         out_specs=[VMEM, VMEM],
         scratch_shapes=[
@@ -426,37 +456,33 @@
             )
             for _ in range(4)
         ],
-        compiler_params=params_of(48),
+        compiler_params=params_of(40),
         name="render",
     )(table, count, arrived, goal)
 
 
-def land_kernel(asked_ref, camera_ref, landed_ref, feats_ref, out_ref, total):
+def land_kernel(asked_ref, pose_ref, landed_ref, feats_ref, out_ref, total):
     total[...] = jnp.zeros_like(total)
+    groups = out_ref.shape[0]
 
     def one(h, _):
         for c in range(CAP):
             block = asked_ref[h, 0, c]
-
-            @pl.when(block >= 0)
-            def _():
-                total[block, 0:FEATS, :] = total[block, 0:FEATS, :] + landed_ref[h, :, c, :]
-
+            block = jnp.where(block < 0, 8 * groups, block)
+            total[block, 0:FEATS, :] = total[block, 0:FEATS, :] + landed_ref[h, :, c, :]
         return 0
 
-    lax.fori_loop(0, landed_ref.shape[0], one, 0)
-    groups = total.shape[0] // 8
+    lax.fori_loop(0, landed_ref.shape[0], one, 0, unroll=8)
+    place = lax.broadcasted_iota(jnp.int32, (8, BLK), 0)
+    shown = jnp.zeros((8, BLK), jnp.float32)
+    for k, value in enumerate(camera_of(pose_ref)):
+        shown = jnp.where(place == k, value, shown)
     for g in range(groups):
         for f in range(FEATS):
             value = total[8 * g : 8 * g + 8, f, :]
             if f >= 6:
                 value = value * feats_ref[8 * g : 8 * g + 8, f + 3, :]
             out_ref[g, f] = value
-    place = lax.broadcasted_iota(jnp.int32, (8, BLK), 0)
-    shown = jnp.zeros((8, BLK), jnp.float32)
-    for k in range(6):
-        shown = jnp.where(place == k, camera_ref[k], shown)
-    for g in range(groups):
         out_ref[g, FEATS] = shown
 
 
@@ -471,66 +497,155 @@
 
 
 def update_kernel(
-    params_ref, first_ref, second_ref, own_ref, next_ref, across_ref, last_ref,
-    new_params_ref, new_first_ref, new_second_ref, pulls, turned, shades, waves,
+    params_ref, first_ref, second_ref, own_ref, next_ref, low_ref, high_ref, last_ref,
+    new_params_ref, new_first_ref, new_second_ref, pulls, turned, shades, waves, ready, sent,
 ):
     me = lax.axis_index("view")
     views = 4
-    for k, ref in enumerate((own_ref, next_ref, across_ref, last_ref)):
-        pulls[(me + k) % views] = ref[0]
-    for j in range(8):
-        turned[j] = params_ref[0:16, j * BLK : (j + 1) * BLK]
-    rows = [turned[:, r, :] for r in range(11)]
-    opacity = 1.0 / (1.0 + jnp.exp(-rows[10]))
-    total = [None] * 11
+    outs = (new_params_ref, new_first_ref, new_second_ref)
+    groups = own_ref.shape[0]
+    span = UPDATE_BLOCKS // 8
+    steps = groups // span
+    chunk = UPDATE_BLOCKS * BLK
     for v in range(views):
-        camera = [pulls[v, FEATS, k : k + 1, :] for k in range(6)]
-        _, pull_back = jax.vjp(lambda *r: geometry(r, camera), *rows[0:10])
-        grads = list(pull_back([pulls[v, f] for f in range(5)]))
-        grads.append(pulls[v, 5] * (1.0 - opacity))
-        total = grads if v == 0 else [p + q for p, q in zip(total, grads)]
-        for c in range(3):
-            shades[:, 3 * v + c, :] = pulls[v, 6 + c]
-
-        @pl.when(pl.program_id(0) == 0)
-        def _():
-            sin_yaw, cos_yaw, sin_tilt, cos_tilt = camera[0:4]
-            terms = harmonics(sin_yaw * cos_tilt, -sin_tilt, cos_yaw * cos_tilt)
+        from_one = [own_ref, next_ref, None, last_ref]
+        pulls[(me + v) % views] = (
+            jnp.concatenate([low_ref[...], high_ref[...]], axis=0) if v == 2 else from_one[v][...]
+        )
+    for v in range(views):
+        terms = look_terms([pulls[v, 0, FEATS, k : k + 1, :] for k in range(6)])
+        for k in range(8):
+            row = lax.broadcasted_iota(jnp.int32, (8, BLK), 0) + (8 * k - 11)
+            wave = jnp.zeros((8, BLK), jnp.float32)
+            for j in range(16):
+                wave = jnp.where((row >= 0) & (row % 16 == j), terms[j], wave)
+            waves[v, 8 * k : 8 * k + 8, :] = wave
+
+    def plus(left, right):
+        return right if left is None else [p + q for p, q in zip(left, right)]
+
+    def copies(step):
+        slot = step % 2
+        at = slice(step * chunk, (step + 1) * chunk)
+        return [
+            pltpu.make_async_copy(ready.at[slot, n], outs[n].at[:, at], sent.at[slot, n])
+            for n in range(3)
+        ]
+
+    row_in = lax.broadcasted_iota(jnp.int32, (8, BLK), 0)
+    for step in range(steps):
+        base = step * chunk
+        for j in range(UPDATE_BLOCKS):
+            turned[j] = params_ref[0:16, base + j * BLK : base + (j + 1) * BLK]
+
+        def of(r):
+            return turned[:, r, :].reshape(span, 8, BLK)
+
+        rows = [of(r) for r in range(11)]
+        opacity = 1.0 / (1.0 + jnp.exp(-rows[10]))
+        matrix, pull_frame = jax.vjp(frame, *rows[3:10])
+        centre, bent = (None, None)
+        for v in range(views):
+            camera = [pulls[v, 0, FEATS, k : k + 1, :] for k in range(6)]
+            right, upward = axes(camera)
+            seen = [pulls[v, step * span : (step + 1) * span, f] for f in range(FEATS)]
+            across, downward = (16.0 * seen[0], 16.0 * seen[1])
+            moved = [
+                right[0] * across + upward[0] * downward,
+                upward[1] * downward,
+                right[1] * across + upward[2] * downward,
+                seen[5],
+            ]
+            centre = plus(centre, moved)
+            _, pull_conic = jax.vjp(lambda m: conic(m, camera), matrix)
+            bent = plus(bent, pull_conic(tuple(seen[2:5]))[0])
+            for c in range(3):
+                shades[:, 3 * v + c, :] = seen[6 + c].reshape(UPDATE_BLOCKS, BLK)
+        total = centre[0:3] + list(pull_frame(tuple(bent))) + [centre[3] * (1.0 - opacity)]
+        for r in range(11):
+            turned[:, r, :] = total[r].reshape(UPDATE_BLOCKS, BLK)
+        if step >= 2:
+            for copy in copies(step - 2):
+                copy.wait()
+        slot = step % 2
+        for j in range(UPDATE_BLOCKS):
+            columns = slice(base + j * BLK, base + (j + 1) * BLK)
             for k in range(8):
-                row = lax.broadcasted_iota(jnp.int32, (8, BLK), 0) + (8 * k - 11)
-                wave = jnp.zeros((8, BLK), jnp.float32)
-                for j in range(16):
-                    wave = jnp.where((row >= 0) & (row % 16 == j), terms[j], wave)
-                waves[v, 8 * k : 8 * k + 8, :] = wave
-
-    for r in range(11):
-        turned[:, r, :] = total[r]
-    row_in = lax.broadcasted_iota(jnp.int32, (8, BLK), 0)
-    for j in range(8):
-        columns = slice(j * BLK, (j + 1) * BLK)
-        for k in range(8):
-            gradient = None
-            if k > 0:
-                first = (8 * k - 11) // 16 if k > 1 else 0
-                last = min((8 * k + 7 - 11) // 16, 2)
-                for v in range(views):
-                    tint = shades[j, 3 * v + first : 3 * v + first + 1, :]
-                    if last != first:
-                        tint = jnp.where(
-                            row_in + (8 * k - 11) < 16 * last,
-                            tint,
-                            shades[j, 3 * v + last : 3 * v + last + 1, :],
-                        )
-                    term = waves[v, 8 * k : 8 * k + 8, :] * tint
-                    gradient = term if gradient is None else gradient + term
-            if k == 0:
-                gradient = turned[j, 0:8, :]
-            if k == 1:
-                gradient = jnp.where(row_in < 3, turned[j, 8:16, :], gradient)
-            height = min(8, PARAMS - 8 * k)
-            at = (slice(8 * k, 8 * k + height), columns)
-            values = adam(params_ref[at], first_ref[at], second_ref[at], gradient[0:height])
-            new_params_ref[at], new_first_ref[at], new_second_ref[at] = values
+                gradient = None
+                if k > 0:
+                    first = (8 * k - 11) // 16 if k > 1 else 0
+                    last = min((8 * k + 7 - 11) // 16, 2)
+                    for v in range(views):
+                        tint = shades[j, 3 * v + first : 3 * v + first + 1, :]
+                        if last != first:
+                            tint = jnp.where(
+                                row_in + (8 * k - 11) < 16 * last,
+                                tint,
+                                shades[j, 3 * v + last : 3 * v + last + 1, :],
+                            )
+                        term = waves[v, 8 * k : 8 * k + 8, :] * tint
+                        gradient = term if gradient is None else gradient + term
+                if k == 0:
+                    gradient = turned[j, 0:8, :]
+                if k == 1:
+                    gradient = jnp.where(row_in < 3, turned[j, 8:16, :], gradient)
+                height = min(8, PARAMS - 8 * k)
+                at = (slice(8 * k, 8 * k + height), columns)
+                values = adam(params_ref[at], first_ref[at], second_ref[at], gradient[0:height])
+                for n in range(3):
+                    ready[slot, n, 8 * k : 8 * k + height, j * BLK : (j + 1) * BLK] = values[n]
+        for copy in copies(step):
+            copy.start()
+    for step in range(max(steps - 2, 0), steps):
+        for copy in copies(step):
+            copy.wait()
+
+
+def project(view_pose, gauss_params):
+    columns = gauss_params.shape[1]
+    blocks = columns // BLK
+    f32 = jnp.float32
+    shape = jax.ShapeDtypeStruct
+    chunk = PROJECT_BLOCKS * BLK
+    wide = pl.BlockSpec((PARAMS, chunk), lambda i: (0, i))
+    steps = columns // chunk
+    return pl.pallas_call(
+        project_kernel,
+        grid=(steps,),
+        out_shape=shape((blocks, 16, BLK), f32),
+        in_specs=[SMEM, wide],
+        out_specs=pl.BlockSpec((PROJECT_BLOCKS, 16, BLK), lambda i: (i, 0, 0)),
+        scratch_shapes=[
+            pltpu.VMEM((PROJECT_BLOCKS, 16, BLK), f32),
+            pltpu.VMEM((8, BLK), f32),
+            pltpu.VMEM((3, 24, BLK), f32),
+        ],
+        compiler_params=params_of(PROJECT_MB),
+        name="project",
+    )(view_pose, gauss_params)
+
+
+def update(gauss_params, first_moment, second_moment, own, after, low, high, prior):
+    groups = own.shape[0]
+    f32 = jnp.float32
+    views = 4
+    chunk = UPDATE_BLOCKS * BLK
+    return pl.pallas_call(
+        update_kernel,
+        out_shape=[jax.ShapeDtypeStruct(gauss_params.shape, f32)] * 3,
+        in_specs=[VMEM] * 8,
+        out_specs=[pl.BlockSpec(memory_space=pl.ANY)] * 3,
+        scratch_shapes=[
+            pltpu.VMEM((views, groups, FEATS + 1, 8, BLK), f32),
+            pltpu.VMEM((UPDATE_BLOCKS, 16, BLK), f32),
+            pltpu.VMEM((UPDATE_BLOCKS, 16, BLK), f32),
+            pltpu.VMEM((views, 64, BLK), f32),
+            pltpu.VMEM((2, 3, PARAMS, chunk), f32),
+            pltpu.SemaphoreType.DMA((2, 3)),
+        ],
+        compiler_params=params_of(UPDATE_MB),
+        name="update",
+    )(gauss_params, first_moment, second_moment, own, after, low, high, prior)
 
 
 def shards(
@@ -543,29 +658,17 @@
     tiles, slots = tile_blocks.shape[1:]
     f32, i32 = jnp.float32, jnp.int32
     shape = jax.ShapeDtypeStruct
-    pose = view_pose[0]
-    camera = jnp.concatenate(
-        [jnp.stack([jnp.sin(pose[0]), jnp.cos(pose[0]), jnp.sin(pose[1]), jnp.cos(pose[1])]), pose[2:4]]
-    )
+    steps = blocks // 8
 
     wanted, table, count = pl.pallas_call(
         request_kernel,
-        out_shape=[shape((groups, 1, CAP), i32), shape((tiles, slots), i32), shape((tiles,), i32)],
-        in_specs=[SMEM, SMEM],
-        out_specs=[SMEM, SMEM, SMEM],
-        scratch_shapes=[pltpu.SMEM((groups,), i32)],
+        out_shape=[shape((groups, 1, CAP), i32)] + [shape((1, tiles * slots), i32)] * 2,
+        in_specs=[VMEM, VMEM],
+        out_specs=[VMEM, VMEM, VMEM],
         name="requests",
     )(tile_blocks[0], tile_order[0])
     asked = lax.all_to_all(wanted, "gs", split_axis=0, concat_axis=0, tiled=True)
-    feats = pl.pallas_call(
-        project_kernel,
-        out_shape=shape((blocks, 16, BLK), f32),
-        in_specs=[SMEM, VMEM],
-        out_specs=VMEM,
-        scratch_shapes=[pltpu.VMEM((blocks, 16, BLK), f32)],
-        compiler_params=params_of(24),
-        name="project",
-    )(camera, gauss_params)
+    feats = project(view_pose, gauss_params)
     outgoing = pl.pallas_call(
         pick_kernel,
         out_shape=shape((groups, FEATS, CAP, BLK), f32),
@@ -575,39 +678,30 @@
         name="pick",
     )(asked, feats)
     arrived = lax.all_to_all(outgoing, "gs", split_axis=0, concat_axis=0, tiled=True)
-    image, back = render(table, count, arrived, target_image[0])
+    image, back = render(table, count, arrived, jnp.transpose(target_image[0], (1, 0, 2)))
     landed = lax.all_to_all(back, "gs", split_axis=0, concat_axis=0, tiled=True)
     own = pl.pallas_call(
         land_kernel,
         out_shape=shape((blocks // 8, FEATS + 1, 8, BLK), f32),
         in_specs=[SMEM, SMEM, VMEM, VMEM],
         out_specs=VMEM,
-        scratch_shapes=[pltpu.VMEM((blocks, 16, BLK), f32)],
+        scratch_shapes=[pltpu.VMEM((blocks + 1, 16, BLK), f32)],
         compiler_params=params_of(16),
         name="land",
-    )(asked, camera, landed, feats)
-    others = [
-        lax.ppermute(own, "view", [((i + k) % views, i) for i in range(views)]) for k in range(1, views)
-    ]
-    chunk = 8 * BLK
-    wide = pl.BlockSpec((PARAMS, chunk), lambda i: (0, i))
-    deep = pl.BlockSpec((1, FEATS + 1, 8, BLK), lambda i: (i, 0, 0, 0))
-    new_params, new_first, new_second = pl.pallas_call(
-        update_kernel,
-        grid=(columns // chunk,),
-        out_shape=[shape((PARAMS, columns), f32)] * 3,
-        in_specs=[wide] * 3 + [deep] * 4,
-        out_specs=[wide] * 3,
-        scratch_shapes=[
-            pltpu.VMEM((views, FEATS + 1, 8, BLK), f32),
-            pltpu.VMEM((8, 16, BLK), f32),
-            pltpu.VMEM((8, 16, BLK), f32),
-            pltpu.VMEM((views, 64, BLK), f32),
-        ],
-        compiler_params=params_of(24),
-        name="update",
-    )(gauss_params, first_moment, second_moment, own, *others)
-    return (new_params, new_first, new_second, image[None])
+    )(asked, view_pose, landed, feats)
+
+    def from_next(value, k):
+        return lax.ppermute(value, "view", [((i + k) % views, i) for i in range(views)])
+
+    half = steps // 2
+    after = from_next(own, 1)
+    prior = from_next(own, views - 1)
+    low = from_next(after[:half], 1)
+    high = from_next(prior[half:], views - 1)
+    new_params, new_first, new_second = update(
+        gauss_params, first_moment, second_moment, own, after, low, high, prior
+    )
+    return (new_params, new_first, new_second, jnp.transpose(image, (1, 0, 2))[None])
 
 
 def solution(mesh):

time: 146 us -> 131 us (0.90)
  blocking collectives: 24.2 us -> 51.5 us
  waiting for transfers between devices: 31.5 us -> 15.6 us
  Pallas kernels: 50.8 us -> 41.4 us
  starting transfers between devices: 28.1 us -> 18.9 us
  local copies, waits for them, and re-layouts: 6.76 us -> 1.11 us
  between operations: 3.44 us -> 0.89 us
    all_to_all x0 -> x1, blocking collectives: none -> 23.8 us  [shards(): lax.all_to_all(outgoing, 'gs', split_axis=0, concat_axis=0, tiled=True)]
    all_to_all x1 -> x0, waiting for transfers between devices: 18.7 us -> none  [shards(): lax.all_to_all(outgoing, 'gs', split_axis=0, concat_axis=0, tiled=True)]
    all_to_all x1 -> x0, starting transfers between devices: 10.5 us -> none  [shards(): lax.all_to_all(outgoing, 'gs', split_axis=0, concat_axis=0, tiled=True)]
    pallas_call x4, Pallas kernels: 45.6 us -> 37.8 us  [the longest x1 26.3 us: render(): pl.pallas_call(render_kernel, out_shape=[shape((3, tiles, PIX), f32), sha...]
    all_to_all x1, waiting for transfers between devices: 0.01 us -> 5.14 us  [shards(): lax.all_to_all(wanted, 'gs', split_axis=0, concat_axis=0, tiled=True)]
    unnamed x18, local copies, waits for them, and re-layouts: 4.63 us -> 1.08 us
    all_to_all x1, blocking collectives: 24.2 us -> 27.7 us  [shards(): landed = lax.all_to_all(back, 'gs', split_axis=0, concat_axis=0, tiled=True)]
    ppermute x3 -> x4, waiting for transfers between devices: 12.8 us -> 10.5 us  [from_next(): lax.ppermute(value, 'view', [((i + k) % views, i) for i in range(views)])]
  transfers between devices with their start and end apart: 5 -> 5, of which waited for: 3 -> 3; matrix products, arithmetic and copies ran while one was open for 2% -> 0% of each run, Pallas kernels for 2% -> 3%
where the time goes in v3:
time: 131 us; the launch traced here: 129 us
  blocking collectives  51.5 us (39%)
  Pallas kernels  41.4 us (32%)
  starting transfers between devices  18.9 us (14%)
  waiting for transfers between devices  15.6 us (12%)
    all_to_all x1, blocking collectives, shards(): landed = lax.all_to_all(back, 'gs', split_axis=0, concat_axis=0, tiled=True)  27.7 us
    pallas_call x1, Pallas kernels, render(): pl.pallas_call(render_kernel, out_shape=[shape((3, tiles, PIX), f32), sha...  26.3 us
    all_to_all x1, blocking collectives, shards(): lax.all_to_all(outgoing, 'gs', split_axis=0, concat_axis=0, tiled=True)  23.8 us
    all_to_all x1, starting transfers between devices, shards(): lax.all_to_all(wanted, 'gs', split_axis=0, concat_axis=0, tiled=True)  13.2 us
    ppermute x4, waiting for transfers between devices, from_next(): lax.ppermute(value, 'view', [((i + k) % views, i) for i in range(views)])  10.5 us
    ppermute x4, starting transfers between devices, from_next(): lax.ppermute(value, 'view', [((i + k) % views, i) for i in range(views)])  5.77 us
    pallas_call x1, Pallas kernels, update(): pl.pallas_call(update_kernel, out_shape=[jax.ShapeDtypeStruct(gauss_param...  5.73 us
    all_to_all x1, waiting for transfers between devices, shards(): lax.all_to_all(wanted, 'gs', split_axis=0, concat_axis=0, tiled=True)  5.14 us
  transfers between devices with their start and end apart: 5, of which 3 were waited for; matrix products, arithmetic and copies ran while one was open for 0% of the time, Pallas kernels for 3%

profile of v3, /device:TPU:1, one launch (start us, length us, event | category | flops | bytes accessed | tf_op | source)
XLA Modules:
  0.0 129.4 jit_solution(1848975412048263088)
XLA Ops:
  0.6 1.8 %requests.1 = (s32[64,1,2]{2,1,0:T(1,128)}, s32[1,128]{1,0:T(1,128)}, s32[1,128]{1,0:T(1,128)}) custom-call(s32[8,16]{1,0:T(8,128)} %bitcast.9, s32[8,16]{1,0:T(8,128)} %bitcast.10), custom_call_target="tpu_custom_call" | custom-call | tf_op jit(solution)/shard_map/requests/pallas_call | solution.py:663
  2.4 13.2 %all-to-all-start = ((s32[64,1,2]{2,1,0:T(1,128)}), s32[64,1,2]{2,1,0:T(1,128)S(1)}, u32[]{:S(2)}, u32[]{:S(2)}) async-start(s32[64,1,2]{2,1,0:T(1,128)} %get-tuple-element.12), calls=%async_computation | async-start | bytes 65536 | tf_op jit(solution)/shard_map/all_to_all | solution.py:670
  15.6 0.0 copy-start.5
  15.6 0.0 copy-start.7
  15.6 0.0 copy-start.8
  15.6 0.0 copy-start.4
  15.6 4.0 %project.1.feats_ref = f32[64,16,128]{2,1,0:T(8,128)} custom-call(f32[1,4]{1,0:T(1,128)} %pose_ref.3, f32[59,8192]{1,0:T(8,128)} %params_ref.3), custom_call_target="tpu_custom_call" | custom-call | tf_op jit(solution)/shard_map/project/pallas_call | solution.py:612
  19.7 5.1 %all-to-all-done.asked_ref = s32[64,1,2]{2,1,0:T(1,128)S(1)} async-done(((s32[64,1,2]{2,1,0:T(1,128)}), s32[64,1,2]{2,1,0:T(1,128)S(1)}, u32[]{:S(2)}, u32[]{:S(2)}) %all-to-all-start) | async-done | bytes 544 | tf_op jit(solution)/shard_map/all_to_all | solution.py:670
  24.8 0.0 copy-start.1
  24.8 1.0 copy-done.1
  25.8 0.0 copy-start.2
  25.8 0.0 copy-start.6
  25.8 1.6 %pick.1 = f32[64,9,2,128]{3,2,1,0:T(2,128)S(1)} custom-call(s32[64,1,2]{2,1,0:T(1,128)S(1)} %all-to-all-done.asked_ref, f32[64,16,128]{2,1,0:T(8,128)S(1)} %copy-done.1), custom_call_target="tpu_custom_call" | custom-call | tf_op jit(solution)/shard_map/pick/pallas_call | solution.py:672
  27.4 0.0 copy-start.3
  27.4 23.8 %all_to_all.15.arrived_ref = f32[64,9,2,128]{3,2,1,0:T(2,128)S(1)} all-to-all(f32[64,9,2,128]{3,2,1,0:T(2,128)S(1)} %pick.1), channel_id=1, replica_groups=mesh['gs'=64,'view'=4] {'gs'}, dimensions={0} | all-to-all | bytes 1179648 | tf_op jit(solution)/shard_map/all_to_all | solution.py:680
  51.3 0.0 copy-start
  51.3 0.0 copy-done.5
  51.3 0.0 copy-done.7
  51.3 0.0 copy-done.8
  51.3 26.3 %render.1 = (f32[3,8,256]{2,1,0:T(8,128)}, f32[64,9,2,128]{3,2,1,0:T(2,128)S(1)}) custom-call(s32[1,128]{1,0:T(1,128)S(1)} %copy-done.7, s32[1,128]{1,0:T(1,128)S(1)} %copy-done.8, f32[64,9,2,128]{3,2,1,0:T(2,128)S(1)} %all_to_all.15.arrived_ref, f32[3,8,256]{2,1,0:T(8,128)S(1)} %bitcast.8), custom_call_target="tpu_custom_call" | custom-call | tf_op jit(solution)/shard_map/render/pallas_call | solution.py:435
  77.6 27.7 %all_to_all.16.landed_ref = f32[64,9,2,128]{3,2,1,0:T(2,128)S(1)} all-to-all(f32[64,9,2,128]{3,2,1,0:T(2,128)S(1)} %get-tuple-element.15), channel_id=1, replica_groups=mesh['gs'=64,'view'=4] {'gs'}, dimensions={0} | all-to-all | bytes 1179648 | tf_op jit(solution)/shard_map/all_to_all | solution.py:682
  105.2 0.0 copy-done.2
  105.2 0.0 copy-done.6
  105.2 2.0 %land.1.own_ref = f32[8,10,8,128]{3,2,1,0:T(8,128)S(1)} custom-call(s32[64,1,2]{2,1,0:T(1,128)S(1)} %all-to-all-done.asked_ref, f32[1,4]{1,0:T(1,128)S(1)} %copy-done.6, f32[64,9,2,128]{3,2,1,0:T(2,128)S(1)} %all_to_all.16.landed_ref, f32[64,16,128]{2,1,0:T(8,128)S(1)} %copy-done.2), custom_call_target="tpu_custom_call" | custom-call | tf_op jit(solution)/shard_map/land/pallas_call | solution.py:683
  107.2 2.0 %collective-permute-start.2 = (f32[8,10,8,128]{3,2,1,0:T(8,128)S(1)}, f32[8,10,8,128]{3,2,1,0:T(8,128)S(1)}, u32[]{:S(2)}, u32[]{:S(2)}) collective-permute-start(f32[8,10,8,128]{3,2,1,0:T(8,128)S(1)} %land.1.own_ref), channel_id=1, source_target_pairs={{3,0},{0,1},{1,2},{2,3},{7,4},{4,5},{5,6},{6,7},{11,8},{8,9},{9,10... | collective-permute-start | bytes 983048 | tf_op jit(solution)/shard_map/ppermute | solution.py:694
  109.2 0.7 collective-permute-start
  110.0 7.5 %collective-permute-done.2.last_ref = f32[8,10,8,128]{3,2,1,0:T(8,128)S(1)} collective-permute-done((f32[8,10,8,128]{3,2,1,0:T(8,128)S(1)}, f32[8,10,8,128]{3,2,1,0:T(8,128)S(1)}, u32[]{:S(2)}, u32[]{:S(2)}) %collective-permute-start.2) | collective-permute-done | bytes 327712 | tf_op jit(solution)/shard_map/ppermute | solution.py:694
  117.5 1.0 collective-permute-start.3
  118.5 0.0 collective-permute-done.next_ref
  118.5 2.0 %collective-permute-start.1 = (f32[4,10,8,128]{3,2,1,0:T(8,128)S(1)}, f32[4,10,8,128]{3,2,1,0:T(8,128)S(1)}, u32[]{:S(2)}, u32[]{:S(2)}) collective-permute-start(f32[4,10,8,128]{3,2,1,0:T(8,128)S(1)} %slice.8), channel_id=1, source_target_pairs={{1,0},{2,1},{3,2},{0,3},{5,4},{6,5},{7,6},{4,7},{9,8},{10,9},{11,1... | collective-permute-start | bytes 491528 | tf_op jit(solution)/shard_map/ppermute | solution.py:694
  120.5 3.0 %collective-permute-done.3.high_ref = f32[4,10,8,128]{3,2,1,0:T(8,128)S(1)} collective-permute-done((f32[4,10,8,128]{3,2,1,0:T(8,128)S(1)}, f32[4,10,8,128]{3,2,1,0:T(8,128)S(1)}, u32[]{:S(2)}, u32[]{:S(2)}) %collective-permute-start.3) | collective-permute-done | bytes 163872 | tf_op jit(solution)/shard_map/ppermute | solution.py:694
  123.5 0.0 collective-permute-done.1.low_ref
  123.5 0.0 copy-done.4
  123.5 0.0 copy-done.3
  123.5 0.0 copy-done
  123.5 5.7 %update.1 = (f32[59,8192]{1,0:T(8,128)}, f32[59,8192]{1,0:T(8,128)}, f32[59,8192]{1,0:T(8,128)}) custom-call(f32[59,8192]{1,0:T(8,128)S(1)} %copy-done, f32[59,8192]{1,0:T(8,128)S(1)} %copy-done.3, f32[59,8192]{1,0:T(8,128)S(1)} %copy-done.4, f32[8,10,8,128]{3,2,1,0:T(8,128)S(1)} %land.1.own_ref, f32[8,10,8,128]{3,2,1,0:T(8,128)S(1)} %collective-permute-done.next_ref, ...), custom_call_target="tpu_custom_call" | custom-call | tf_op jit(solution)/shard_map/update/pallas_call | solution.py:633
  (2 shorter events, 0.0 us)
Async XLA Ops:
  2.4 22.4 %all-to-all-start = ((s32[64,1,2]{2,1,0:T(1,128)}), s32[64,1,2]{2,1,0:T(1,128)S(1)}, u32[]{:S(2)}, u32[]{:S(2)}) async-start(s32[64,1,2]{2,1,0:T(1,128)} %get-tuple-element.12), calls=%async_computation | async-start | bytes 65536 | tf_op jit(solution)/shard_map/all_to_all | solution.py:670
  15.6 35.7 %copy-start.5 = (f32[1,8,3,256]{3,1,2,0:T(8,128)S(1)}, f32[1,8,3,256]{3,1,2,0:T(8,128)}, u32[]{:S(2)}) copy-start(f32[1,8,3,256]{3,1,2,0:T(8,128)} %param.13) | copy-start | bytes 73732
  15.6 35.7 %copy-start.7 = (s32[1,128]{1,0:T(1,128)S(1)}, s32[1,128]{1,0:T(1,128)}, u32[]{:S(2)}) copy-start(s32[1,128]{1,0:T(1,128)} %get-tuple-element.13.table_ref) | copy-start | bytes 1540
  15.6 35.7 %copy-start.8 = (s32[1,128]{1,0:T(1,128)S(1)}, s32[1,128]{1,0:T(1,128)}, u32[]{:S(2)}) copy-start(s32[1,128]{1,0:T(1,128)} %get-tuple-element.14.count_ref) | copy-start | bytes 1540
  15.6 107.9 %copy-start.4 = (f32[59,8192]{1,0:T(8,128)S(1)}, f32[59,8192]{1,0:T(8,128)}, u32[]{:S(2)}) copy-start(f32[59,8192]{1,0:T(8,128)} %second_ref.1) | copy-start | bytes 5799940
  24.8 1.0 copy-start.1
  25.8 79.4 %copy-start.2 = (f32[64,16,128]{2,1,0:T(8,128)S(1)}, f32[64,16,128]{2,1,0:T(8,128)}, u32[]{:S(2)}) copy-start(f32[64,16,128]{2,1,0:T(8,128)} %project.1.feats_ref) | copy-start | bytes 1572868
  25.8 79.4 %copy-start.6 = (f32[1,4]{1,0:T(1,128)S(1)}, f32[1,4]{1,0:T(1,128)}, u32[]{:S(2)}) copy-start(f32[1,4]{1,0:T(1,128)} %pose_ref.3) | copy-start | bytes 52
  27.4 96.1 %copy-start.3 = (f32[59,8192]{1,0:T(8,128)S(1)}, f32[59,8192]{1,0:T(8,128)}, u32[]{:S(2)}) copy-start(f32[59,8192]{1,0:T(8,128)} %first_ref.1) | copy-start | bytes 5799940
  51.3 72.2 %copy-start = (f32[59,8192]{1,0:T(8,128)S(1)}, f32[59,8192]{1,0:T(8,128)}, u32[]{:S(2)}) copy-start(f32[59,8192]{1,0:T(8,128)} %params_ref.3) | copy-start | bytes 5799940
  107.2 10.3 %collective-permute-start.2 = (f32[8,10,8,128]{3,2,1,0:T(8,128)S(1)}, f32[8,10,8,128]{3,2,1,0:T(8,128)S(1)}, u32[]{:S(2)}, u32[]{:S(2)}) collective-permute-start(f32[8,10,8,128]{3,2,1,0:T(8,128)S(1)} %land.1.own_ref), channel_id=1, source_target_pairs={{3,0},{0,1},{1,2},{2,3},{7,4},{4,5},{5,6},{6,7},{11,8},{8,9},{9,10... | collective-permute-start | bytes 983048 | tf_op jit(solution)/shard_map/ppermute | solution.py:694
  109.2 9.2 %collective-permute-start = (f32[8,10,8,128]{3,2,1,0:T(8,128)S(1)}, f32[8,10,8,128]{3,2,1,0:T(8,128)S(1)}, u32[]{:S(2)}, u32[]{:S(2)}) collective-permute-start(f32[8,10,8,128]{3,2,1,0:T(8,128)S(1)} %land.1.own_ref), channel_id=1, source_target_pairs={{1,0},{2,1},{3,2},{0,3},{5,4},{6,5},{7,6},{4,7},{9,8},{10,9},{11,1... | collective-permute-start | bytes 983048 | tf_op jit(solution)/shard_map/ppermute | solution.py:694
  117.5 6.0 %collective-permute-start.3 = (f32[4,10,8,128]{3,2,1,0:T(8,128)S(1)}, f32[4,10,8,128]{3,2,1,0:T(8,128)S(1)}, u32[]{:S(2)}, u32[]{:S(2)}) collective-permute-start(f32[4,10,8,128]{3,2,1,0:T(8,128)S(1)} %slice.9), channel_id=1, source_target_pairs={{3,0},{0,1},{1,2},{2,3},{7,4},{4,5},{5,6},{6,7},{11,8},{8,9},{9,10... | collective-permute-start | bytes 491528 | tf_op jit(solution)/shard_map/ppermute | solution.py:694
  118.5 5.0 %collective-permute-start.1 = (f32[4,10,8,128]{3,2,1,0:T(8,128)S(1)}, f32[4,10,8,128]{3,2,1,0:T(8,128)S(1)}, u32[]{:S(2)}, u32[]{:S(2)}) collective-permute-start(f32[4,10,8,128]{3,2,1,0:T(8,128)S(1)} %slice.8), channel_id=1, source_target_pairs={{1,0},{2,1},{3,2},{0,3},{5,4},{6,5},{7,6},{4,7},{9,8},{10,9},{11,1... | collective-permute-start | bytes 491528 | tf_op jit(solution)/shard_map/ppermute | solution.py:694

commit v4 on v3

--- a/solution.py
+++ b/solution.py
@@ -23,10 +23,11 @@
 LOG2E = 1.4426950408889634
 TINY = 1.1754944e-38
 BELOW_ONE = 0.99999994
-PROJECT_MB = 56
+PROJECT_MB = 24
 UPDATE_MB = 24
 PROJECT_BLOCKS = 32
-UPDATE_BLOCKS = 8
+ROWS = 64
+HALF = 4
 
 VMEM = pl.BlockSpec(memory_space=pltpu.VMEM)
 SMEM = pl.BlockSpec(memory_space=pltpu.SMEM)
@@ -86,7 +87,7 @@
     return tuple(scales[k] * rotation[r][k] for r in range(3) for k in range(3))
 
 
-def conic(matrix, camera):
+def spreads(matrix, camera):
     right, upward = axes(camera)
     first = [right[0] * matrix[k] + right[1] * matrix[6 + k] for k in range(3)]
     second = [
@@ -97,7 +98,30 @@
     spread_mixed = first[0] * second[0] + first[1] * second[1] + first[2] * second[2]
     spread_second = second[0] * second[0] + second[1] * second[1] + second[2] * second[2] + dilation
     determinant = spread_first * spread_second - spread_mixed * spread_mixed
+    return first, second, spread_first, spread_mixed, spread_second, determinant
+
+
+def conic(matrix, camera):
+    _, _, spread_first, spread_mixed, spread_second, determinant = spreads(matrix, camera)
     return (spread_second / determinant, -spread_mixed / determinant, spread_first / determinant)
+
+
+def conic_pull(matrix, camera, pulls):
+    right, upward = axes(camera)
+    first, second, spread_first, spread_mixed, spread_second, determinant = spreads(matrix, camera)
+    inverse = 1.0 / determinant
+    pull_a, pull_b, pull_c = [value * inverse for value in pulls]
+    shrink = (pull_b * spread_mixed - pull_a * spread_second - pull_c * spread_first) * inverse
+    to_first = 2.0 * (pull_c + shrink * spread_second)
+    to_second = 2.0 * (pull_a + shrink * spread_first)
+    to_mixed = -pull_b - 2.0 * (shrink * spread_mixed)
+    on_first = [to_first * p + to_mixed * q for p, q in zip(first, second)]
+    on_second = [to_second * q + to_mixed * p for p, q in zip(first, second)]
+    return (
+        [right[0] * p + upward[0] * q for p, q in zip(on_first, on_second)]
+        + [upward[1] * q for q in on_second]
+        + [right[1] * p + upward[2] * q for p, q in zip(on_first, on_second)]
+    )
 
 
 def geometry(rows, camera):
@@ -227,19 +251,8 @@
     return jnp.concatenate([high, low], axis=1)
 
 
-def sums_by(values, band):
-    rows = values[0].shape[0]
-    halves = jnp.concatenate([halves_of(value) for value in values], axis=0)
-    total = jnp.dot(halves, band[...], preferred_element_type=jnp.float32)
-    return [total[rows * h : rows * (h + 1)] for h in range(len(values))]
-
-
 def twice(value):
     return jnp.concatenate([value, value], axis=1)
-
-
-def fold(value):
-    return jnp.sum(value.reshape(-1, 8, BLK), axis=0)
 
 
 def render_kernel(
@@ -269,7 +282,7 @@
     for k, value in enumerate((x, y, x * x, x * y, y * y)):
         powers = jnp.where((place < 24) & (place % 8 == k + 1), value, powers)
     basis[...] = powers.astype(jnp.bfloat16)
-    x = lax.broadcasted_iota(jnp.int32, (16, BLK), 0).astype(jnp.float32) - 7.5
+    x = lax.broadcasted_iota(jnp.int32, (16, 2 * BLK), 0).astype(jnp.float32) - 7.5
     blank = jnp.zeros((8, PIX), jnp.float32)
     slot_at = lax.broadcasted_iota(jnp.int32, (slots, BLK), 0)
     for _, terms, *_ in lanes:
@@ -327,21 +340,34 @@
             for rows, terms, *_ in lanes:
                 coefs = side_by_side(terms, slice(None), j).astype(jnp.bfloat16)
                 state.append(jnp.dot(basis[...], coefs, preferred_element_type=jnp.float32))
-            state = [jnp.minimum(jnp.exp2(value), BELOW_ONE) for value in state]
-            losses = [jnp.log2(1.0 - alpha) for alpha in state]
-            runs = sums_by(losses, before)
+            alphas, losses, halves = ([], [], [])
+            for h, (_, _, ratios, *_) in enumerate(lanes):
+                for r in range(0, PIX, ROWS):
+                    alpha = jnp.minimum(jnp.exp2(state[h][r : r + ROWS]), BELOW_ONE)
+                    loss = jnp.log2(1.0 - alpha)
+                    ratios[j, r : r + ROWS] = alpha * jnp.exp2(-loss)
+                    alphas.append(alpha)
+                    losses.append(loss)
+                    halves.append(halves_of(loss))
+            run = jnp.dot(
+                jnp.concatenate(halves, axis=0), before[...], preferred_element_type=jnp.float32
+            )
             out = []
-            for h, (rows, _, ratios, weights, shades, _, _) in enumerate(lanes):
-                alpha, loss, run = state[h], losses[h], runs[h]
-                ratios[j] = alpha * jnp.exp2(-loss)
-                weight = alpha * jnp.exp2(run + twice(logs[h]))
-                weights[j] = weight
+            for h, (rows, _, _, weights, shades, _, _) in enumerate(lanes):
                 tints = side_by_side(rows, slice(6, 9), j)
-                for c in range(3):
-                    shade = weight * tints[c : c + 1]
-                    shades[c] += shade[:, 0:BLK] + shade[:, BLK:]
-                last = run[:, 2 * BLK - 1 :] + loss[:, 2 * BLK - 1 :]
-                out.append(logs[h] + jnp.broadcast_to(last, (PIX, BLK)))
+                lasts = []
+                for r in range(0, PIX, ROWS):
+                    n = (h * PIX + r) // ROWS
+                    mine = run[h * PIX + r : h * PIX + r + ROWS]
+                    log = logs[h][r : r + ROWS]
+                    weight = alphas[n] * jnp.exp2(mine + twice(log))
+                    weights[j, r : r + ROWS] = weight
+                    for c in range(3):
+                        shade = weight * tints[c : c + 1]
+                        shades[c, r : r + ROWS] += shade[:, 0:BLK] + shade[:, BLK:]
+                    last = mine[:, 2 * BLK - 1 :] + losses[n][:, 2 * BLK - 1 :]
+                    lasts.append(log + jnp.broadcast_to(last, (ROWS, BLK)))
+                out.append(jnp.concatenate(lasts, axis=0))
             return tuple(out)
 
         still = jnp.zeros((PIX, BLK), jnp.float32)
@@ -367,37 +393,50 @@
 
         def backward(step, later):
             j = pairs - 1 - step
-            reaches = []
+            reaches, halves = ([], [])
             for h, (_, terms, _, weights, *_) in enumerate(lanes):
                 coefs = side_by_side(terms, slice(None), j).astype(jnp.bfloat16)
-                reaches.append(
-                    jnp.dot(pulled[h], coefs, preferred_element_type=jnp.float32) * weights[j]
-                )
-            behinds = sums_by(reaches, after)
+                pull = jnp.dot(pulled[h], coefs, preferred_element_type=jnp.float32)
+                for r in range(0, PIX, 16):
+                    reach = pull[r : r + 16] * weights[j, r : r + 16]
+                    reaches.append(reach)
+                    halves.append(halves_of(reach))
+            behinds = jnp.dot(
+                jnp.concatenate(halves, axis=0), after[...], preferred_element_type=jnp.float32
+            )
             out = []
             for h, (_, _, ratios, weights, _, pulls, sums) in enumerate(lanes):
-                reach, behind, weight = reaches[h], behinds[h], weights[j]
-                push = reach - (behind + twice(later[h])) * ratios[j]
-                for k in range(2):
-                    at = slice(BLK * k, BLK * (k + 1))
-                    slot = pl.ds(2 * j + k, 1)
-                    part = push[:, at].reshape(16, 16, BLK)
-                    plain, tilted, bent = (None, None, None)
-                    for n in range(8):
-                        y = 7.5 - n
-                        even, odd = (part[15 - n] + part[n], y * (part[15 - n] - part[n]))
-                        square = (y * y) * even
-                        plain = even if n == 0 else plain + even
-                        tilted = odd if n == 0 else tilted + odd
-                        bent = square if n == 0 else bent + square
-                    values = (plain, x * plain, tilted, x * x * plain, x * tilted, bent)
-                    for f, value in enumerate(values):
-                        sums[f, slot] = (value[0:8] + value[8:16]).reshape(1, 8, BLK)
-                    for c in range(3):
-                        sums[6 + c, slot] = fold(weight[:, at] * pulls[c]).reshape(1, 8, BLK)
-                out.append(
-                    later[h] + jnp.broadcast_to(behind[:, 0:1] + reach[:, 0:1], (PIX, BLK))
-                )
+                plain, tilted, bent = (None, None, None)
+                tints = [None] * 3
+                lasts = [None] * 16
+                for n in range(8):
+                    pair = []
+                    for m in (n, 15 - n):
+                        at = slice(16 * m, 16 * m + 16)
+                        reach = reaches[16 * h + m]
+                        behind = behinds[h * PIX + 16 * m : h * PIX + 16 * m + 16]
+                        log = later[h][at]
+                        pair.append(reach - (behind + twice(log)) * ratios[j, at])
+                        last = jnp.broadcast_to(behind[:, 0:1] + reach[:, 0:1], (16, BLK))
+                        lasts[m] = log + last
+                        weight = weights[j, at]
+                        for c in range(3):
+                            tint = weight * twice(pulls[c, at])
+                            tint = tint[0:8] + tint[8:16]
+                            tints[c] = tint if tints[c] is None else tints[c] + tint
+                    y = 7.5 - n
+                    even, odd = (pair[1] + pair[0], y * (pair[1] - pair[0]))
+                    square = (y * y) * even
+                    plain = even if n == 0 else plain + even
+                    tilted = odd if n == 0 else tilted + odd
+                    bent = square if n == 0 else bent + square
+                values = (plain, x * plain, tilted, x * x * plain, x * tilted, bent)
+                values = [value[0:8] + value[8:16] for value in values] + tints
+                for f, value in enumerate(values):
+                    for k in range(2):
+                        at = slice(BLK * k, BLK * (k + 1))
+                        sums[f, pl.ds(2 * j + k, 1)] = value[:, at].reshape(1, 8, BLK)
+                out.append(jnp.concatenate(lasts, axis=0))
             return tuple(out)
 
         lax.fori_loop(0, pairs, backward, (still,) * 4)
@@ -463,7 +502,7 @@
 
 def land_kernel(asked_ref, pose_ref, landed_ref, feats_ref, out_ref, total):
     total[...] = jnp.zeros_like(total)
-    groups = out_ref.shape[0]
+    groups = HALF * out_ref.shape[0]
 
     def one(h, _):
         for c in range(CAP):
@@ -482,18 +521,20 @@
             value = total[8 * g : 8 * g + 8, f, :]
             if f >= 6:
                 value = value * feats_ref[8 * g : 8 * g + 8, f + 3, :]
-            out_ref[g, f] = value
-        out_ref[g, FEATS] = shown
+            out_ref[g // HALF, FEATS * (g % HALF) + f] = value
+    for n in range(out_ref.shape[0]):
+        out_ref[n, FEATS * HALF] = shown
 
 
 def adam(weights_in, moment_one, moment_two, gradient):
     new_first = beta_one * moment_one + (1.0 - beta_one) * gradient
     new_second = beta_two * moment_two + (1.0 - beta_two) * gradient * gradient
     step_size = learn_rate / (1.0 - beta_one**ADAM_STEP)
-    new_params = weights_in - step_size * new_first / (
-        jnp.sqrt(new_second / (1.0 - beta_two**ADAM_STEP)) + adam_eps
-    )
-    return (new_params, new_first, new_second)
+    root = new_second * lax.rsqrt(new_second) * (1.0 / math.sqrt(1.0 - beta_two**ADAM_STEP))
+    below = root + adam_eps
+    inverse = pl.reciprocal(below, approx=True)
+    inverse = inverse * (2.0 - below * inverse)
+    return (weights_in - step_size * new_first * inverse, new_first, new_second)
 
 
 def update_kernel(
@@ -503,17 +544,15 @@
     me = lax.axis_index("view")
     views = 4
     outs = (new_params_ref, new_first_ref, new_second_ref)
-    groups = own_ref.shape[0]
-    span = UPDATE_BLOCKS // 8
-    steps = groups // span
-    chunk = UPDATE_BLOCKS * BLK
+    steps = HALF * own_ref.shape[0]
+    chunk = 8 * BLK
+    for k, ref in ((0, own_ref), (1, next_ref), (3, last_ref)):
+        pulls[(me + k) % views] = ref[...]
+    for k, ref in enumerate((low_ref, high_ref)):
+        pulls[(me + 2) % views, k] = ref[0]
+    cameras = [[pulls[v, 0, FEATS * HALF, k : k + 1, :] for k in range(6)] for v in range(views)]
     for v in range(views):
-        from_one = [own_ref, next_ref, None, last_ref]
-        pulls[(me + v) % views] = (
-            jnp.concatenate([low_ref[...], high_ref[...]], axis=0) if v == 2 else from_one[v][...]
-        )
-    for v in range(views):
-        terms = look_terms([pulls[v, 0, FEATS, k : k + 1, :] for k in range(6)])
+        terms = look_terms(cameras[v])
         for k in range(8):
             row = lax.broadcasted_iota(jnp.int32, (8, BLK), 0) + (8 * k - 11)
             wave = jnp.zeros((8, BLK), jnp.float32)
@@ -535,20 +574,16 @@
     row_in = lax.broadcasted_iota(jnp.int32, (8, BLK), 0)
     for step in range(steps):
         base = step * chunk
-        for j in range(UPDATE_BLOCKS):
+        for j in range(8):
             turned[j] = params_ref[0:16, base + j * BLK : base + (j + 1) * BLK]
 
-        def of(r):
-            return turned[:, r, :].reshape(span, 8, BLK)
-
-        rows = [of(r) for r in range(11)]
+        rows = [turned[:, r, :] for r in range(11)]
         opacity = 1.0 / (1.0 + jnp.exp(-rows[10]))
         matrix, pull_frame = jax.vjp(frame, *rows[3:10])
         centre, bent = (None, None)
         for v in range(views):
-            camera = [pulls[v, 0, FEATS, k : k + 1, :] for k in range(6)]
-            right, upward = axes(camera)
-            seen = [pulls[v, step * span : (step + 1) * span, f] for f in range(FEATS)]
+            right, upward = axes(cameras[v])
+            seen = [pulls[v, step // HALF, FEATS * (step % HALF) + f] for f in range(FEATS)]
             across, downward = (16.0 * seen[0], 16.0 * seen[1])
             moved = [
                 right[0] * across + upward[0] * downward,
@@ -557,18 +592,17 @@
                 seen[5],
             ]
             centre = plus(centre, moved)
-            _, pull_conic = jax.vjp(lambda m: conic(m, camera), matrix)
-            bent = plus(bent, pull_conic(tuple(seen[2:5]))[0])
+            bent = plus(bent, conic_pull(matrix, cameras[v], seen[2:5]))
             for c in range(3):
-                shades[:, 3 * v + c, :] = seen[6 + c].reshape(UPDATE_BLOCKS, BLK)
+                shades[:, 3 * v + c, :] = seen[6 + c]
         total = centre[0:3] + list(pull_frame(tuple(bent))) + [centre[3] * (1.0 - opacity)]
         for r in range(11):
-            turned[:, r, :] = total[r].reshape(UPDATE_BLOCKS, BLK)
+            turned[:, r, :] = total[r]
         if step >= 2:
             for copy in copies(step - 2):
                 copy.wait()
         slot = step % 2
-        for j in range(UPDATE_BLOCKS):
+        for j in range(8):
             columns = slice(base + j * BLK, base + (j + 1) * BLK)
             for k in range(8):
                 gradient = None
@@ -626,19 +660,18 @@
 
 
 def update(gauss_params, first_moment, second_moment, own, after, low, high, prior):
-    groups = own.shape[0]
     f32 = jnp.float32
     views = 4
-    chunk = UPDATE_BLOCKS * BLK
+    chunk = 8 * BLK
     return pl.pallas_call(
         update_kernel,
         out_shape=[jax.ShapeDtypeStruct(gauss_params.shape, f32)] * 3,
         in_specs=[VMEM] * 8,
         out_specs=[pl.BlockSpec(memory_space=pl.ANY)] * 3,
         scratch_shapes=[
-            pltpu.VMEM((views, groups, FEATS + 1, 8, BLK), f32),
-            pltpu.VMEM((UPDATE_BLOCKS, 16, BLK), f32),
-            pltpu.VMEM((UPDATE_BLOCKS, 16, BLK), f32),
+            pltpu.VMEM((views, *own.shape), f32),
+            pltpu.VMEM((8, 16, BLK), f32),
+            pltpu.VMEM((8, 16, BLK), f32),
             pltpu.VMEM((views, 64, BLK), f32),
             pltpu.VMEM((2, 3, PARAMS, chunk), f32),
             pltpu.SemaphoreType.DMA((2, 3)),
@@ -658,7 +691,6 @@
     tiles, slots = tile_blocks.shape[1:]
     f32, i32 = jnp.float32, jnp.int32
     shape = jax.ShapeDtypeStruct
-    steps = blocks // 8
 
     wanted, table, count = pl.pallas_call(
         request_kernel,
@@ -682,7 +714,7 @@
     landed = lax.all_to_all(back, "gs", split_axis=0, concat_axis=0, tiled=True)
     own = pl.pallas_call(
         land_kernel,
-        out_shape=shape((blocks // 8, FEATS + 1, 8, BLK), f32),
+        out_shape=shape((blocks // (8 * HALF), FEATS * HALF + 1, 8, BLK), f32),
         in_specs=[SMEM, SMEM, VMEM, VMEM],
         out_specs=VMEM,
         scratch_shapes=[pltpu.VMEM((blocks + 1, 16, BLK), f32)],
@@ -693,11 +725,10 @@
     def from_next(value, k):
         return lax.ppermute(value, "view", [((i + k) % views, i) for i in range(views)])
 
-    half = steps // 2
     after = from_next(own, 1)
     prior = from_next(own, views - 1)
-    low = from_next(after[:half], 1)
-    high = from_next(prior[half:], views - 1)
+    low = from_next(after[:1], 1)
+    high = from_next(prior[1:], views - 1)
     new_params, new_first, new_second = update(
         gauss_params, first_moment, second_moment, own, after, low, high, prior
     )

time: 131 us -> 129 us (0.985)
  waiting for transfers between devices: 15.6 us -> 13.8 us
    all_to_all x1, blocking collectives: 27.7 us -> 25.7 us  [shards(): landed = lax.all_to_all(back, 'gs', split_axis=0, concat_axis=0, tiled=True)]
    pallas_call x1, Pallas kernels: 4.03 us -> 2.57 us  [project(): pl.pallas_call(project_kernel, grid=(steps,), out_shape=shape((blocks, 16...]
  transfers between devices with their start and end apart: 5 -> 5, of which waited for: 3 -> 3; matrix products, arithmetic and copies ran while one was open for 0% -> 0% of each run, Pallas kernels for 3% -> 2%
where the time goes in v4:
time: 129 us; the launch traced here: 127 us
  blocking collectives  50.4 us (39%)
  Pallas kernels  40.7 us (32%)
  starting transfers between devices  18.9 us (15%)
  waiting for transfers between devices  13.8 us (11%)
  local copies, waits for them, and re-layouts  2.3 us (2%)
    pallas_call x1, Pallas kernels, render(): pl.pallas_call(render_kernel, out_shape=[shape((3, tiles, PIX), f32), sha...  27.2 us
    all_to_all x1, blocking collectives, shards(): landed = lax.all_to_all(back, 'gs', split_axis=0, concat_axis=0, tiled=True)  25.7 us
    all_to_all x1, blocking collectives, shards(): lax.all_to_all(outgoing, 'gs', split_axis=0, concat_axis=0, tiled=True)  24.6 us
    all_to_all x1, starting transfers between devices, shards(): lax.all_to_all(wanted, 'gs', split_axis=0, concat_axis=0, tiled=True)  13.2 us
    ppermute x4, waiting for transfers between devices, from_next(): lax.ppermute(value, 'view', [((i + k) % views, i) for i in range(views)])  9.43 us
    ppermute x4, starting transfers between devices, from_next(): lax.ppermute(value, 'view', [((i + k) % views, i) for i in range(views)])  5.75 us
    pallas_call x1, Pallas kernels, update(): pl.pallas_call(update_kernel, out_shape=[jax.ShapeDtypeStruct(gauss_param...  5.54 us
    all_to_all x1, waiting for transfers between devices, shards(): lax.all_to_all(wanted, 'gs', split_axis=0, concat_axis=0, tiled=True)  4.36 us
  transfers between devices with their start and end apart: 5, of which 3 were waited for; matrix products, arithmetic and copies ran while one was open for 0% of the time, Pallas kernels for 2%

profile of v4, /device:TPU:1, one launch (start us, length us, event | category | flops | bytes accessed | tf_op | source)
XLA Modules:
  0.0 127.0 jit_solution(3415523885295644004)
XLA Ops:
  0.6 1.8 %requests.1 = (s32[64,1,2]{2,1,0:T(1,128)}, s32[1,128]{1,0:T(1,128)}, s32[1,128]{1,0:T(1,128)}) custom-call(s32[8,16]{1,0:T(8,128)} %bitcast.9, s32[8,16]{1,0:T(8,128)} %bitcast.10), custom_call_target="tpu_custom_call" | custom-call | tf_op jit(solution)/shard_map/requests/pallas_call | solution.py:695
  2.4 13.2 %all-to-all-start = ((s32[64,1,2]{2,1,0:T(1,128)}), s32[64,1,2]{2,1,0:T(1,128)S(1)}, u32[]{:S(2)}, u32[]{:S(2)}) async-start(s32[64,1,2]{2,1,0:T(1,128)} %get-tuple-element.12), calls=%async_computation | async-start | bytes 65536 | tf_op jit(solution)/shard_map/all_to_all | solution.py:702
  15.6 0.0 copy-start
  15.6 1.6 %copy-done = f32[59,8192]{1,0:T(8,128)S(1)} copy-done((f32[59,8192]{1,0:T(8,128)S(1)}, f32[59,8192]{1,0:T(8,128)}, u32[]{:S(2)}) %copy-start) | copy-done | bytes 1933336
  17.2 0.0 copy-start.5
  17.2 0.7 copy-done.5
  17.8 0.0 copy-start.4
  17.8 0.0 copy-start.7
  17.8 0.0 copy-start.8
  17.8 0.0 copy-start.3
  17.9 2.6 %project.1.feats_ref = f32[64,16,128]{2,1,0:T(8,128)S(1)} custom-call(f32[1,4]{1,0:T(1,128)S(1)} %copy-done.5, f32[59,8192]{1,0:T(8,128)S(1)} %copy-done), custom_call_target="tpu_custom_call" | custom-call | tf_op jit(solution)/shard_map/project/pallas_call | solution.py:646
  20.4 0.0 copy-start.6
  20.4 4.4 %all-to-all-done.asked_ref = s32[64,1,2]{2,1,0:T(1,128)S(1)} async-done(((s32[64,1,2]{2,1,0:T(1,128)}), s32[64,1,2]{2,1,0:T(1,128)S(1)}, u32[]{:S(2)}, u32[]{:S(2)}) %all-to-all-start) | async-done | bytes 544 | tf_op jit(solution)/shard_map/all_to_all | solution.py:702
  24.8 1.6 %pick.1 = f32[64,9,2,128]{3,2,1,0:T(2,128)S(1)} custom-call(s32[64,1,2]{2,1,0:T(1,128)S(1)} %all-to-all-done.asked_ref, f32[64,16,128]{2,1,0:T(8,128)S(1)} %project.1.feats_ref), custom_call_target="tpu_custom_call" | custom-call | tf_op jit(solution)/shard_map/pick/pallas_call | solution.py:704
  26.4 0.0 copy-start.2
  26.4 24.6 %all_to_all.15.arrived_ref = f32[64,9,2,128]{3,2,1,0:T(2,128)S(1)} all-to-all(f32[64,9,2,128]{3,2,1,0:T(2,128)S(1)} %pick.1), channel_id=1, replica_groups=mesh['gs'=64,'view'=4] {'gs'}, dimensions={0} | all-to-all | bytes 1179648 | tf_op jit(solution)/shard_map/all_to_all | solution.py:712
  51.0 0.0 copy-start.1
  51.0 0.0 copy-done.4
  51.0 0.0 copy-done.7
  51.0 0.0 copy-done.8
  51.0 27.2 %render.1 = (f32[3,8,256]{2,1,0:T(8,128)}, f32[64,9,2,128]{3,2,1,0:T(2,128)S(1)}) custom-call(s32[1,128]{1,0:T(1,128)S(1)} %copy-done.7, s32[1,128]{1,0:T(1,128)S(1)} %copy-done.8, f32[64,9,2,128]{3,2,1,0:T(2,128)S(1)} %all_to_all.15.arrived_ref, f32[3,8,256]{2,1,0:T(8,128)S(1)} %bitcast.8), custom_call_target="tpu_custom_call" | custom-call | tf_op jit(solution)/shard_map/render/pallas_call | solution.py:474
  78.3 25.7 %all_to_all.16.landed_ref = f32[64,9,2,128]{3,2,1,0:T(2,128)S(1)} all-to-all(f32[64,9,2,128]{3,2,1,0:T(2,128)S(1)} %get-tuple-element.15), channel_id=1, replica_groups=mesh['gs'=64,'view'=4] {'gs'}, dimensions={0} | all-to-all | bytes 1179648 | tf_op jit(solution)/shard_map/all_to_all | solution.py:714
  104.0 0.0 copy-done.6
  104.0 2.0 %land.1.own_ref = f32[2,37,8,128]{3,2,1,0:T(8,128)S(1)} custom-call(s32[64,1,2]{2,1,0:T(1,128)S(1)} %all-to-all-done.asked_ref, f32[1,4]{1,0:T(1,128)S(1)} %copy-done.6, f32[64,9,2,128]{3,2,1,0:T(2,128)S(1)} %all_to_all.16.landed_ref, f32[64,16,128]{2,1,0:T(8,128)S(1)} %project.1.feats_ref), custom_call_target="tpu_custom_call" | custom-call | tf_op jit(solution)/shard_map/land/pallas_call | solution.py:715
  106.0 1.1 collective-permute-start.2
  107.2 1.6 %collective-permute-start = (f32[2,37,8,128]{3,2,1,0:T(8,128)S(1)}, f32[2,37,8,128]{3,2,1,0:T(8,128)S(1)}, u32[]{:S(2)}, u32[]{:S(2)}) collective-permute-start(f32[2,37,8,128]{3,2,1,0:T(8,128)S(1)} %land.1.own_ref), channel_id=1, source_target_pairs={{1,0},{2,1},{3,2},{0,3},{5,4},{6,5},{7,6},{4,7},{9,8},{10,9},{11,1... | collective-permute-start | bytes 909320 | tf_op jit(solution)/shard_map/ppermute | solution.py:726
  108.8 7.0 %collective-permute-done.2.last_ref = f32[2,37,8,128]{3,2,1,0:T(8,128)S(1)} collective-permute-done((f32[2,37,8,128]{3,2,1,0:T(8,128)S(1)}, f32[2,37,8,128]{3,2,1,0:T(8,128)S(1)}, u32[]{:S(2)}, u32[]{:S(2)}) %collective-permute-start.2) | collective-permute-done | bytes 303136 | tf_op jit(solution)/shard_map/ppermute | solution.py:726
  115.8 0.3 collective-permute-start.3
  116.0 0.0 collective-permute-done.next_ref
  116.1 2.7 %collective-permute-start.1 = (f32[1,37,8,128]{3,2,1,0:T(8,128)S(1)}, f32[1,37,8,128]{3,2,1,0:T(8,128)S(1)}, u32[]{:S(2)}, u32[]{:S(2)}) collective-permute-start(f32[1,37,8,128]{3,2,1,0:T(8,128)S(1)} %slice.8), channel_id=1, source_target_pairs={{1,0},{2,1},{3,2},{0,3},{5,4},{6,5},{7,6},{4,7},{9,8},{10,9},{11,1... | collective-permute-start | bytes 454664 | tf_op jit(solution)/shard_map/ppermute | solution.py:726
  118.8 2.5 %collective-permute-done.3.high_ref = f32[1,37,8,128]{3,2,1,0:T(8,128)S(1)} collective-permute-done((f32[1,37,8,128]{3,2,1,0:T(8,128)S(1)}, f32[1,37,8,128]{3,2,1,0:T(8,128)S(1)}, u32[]{:S(2)}, u32[]{:S(2)}) %collective-permute-start.3) | collective-permute-done | bytes 151584 | tf_op jit(solution)/shard_map/ppermute | solution.py:726
  121.3 0.0 collective-permute-done.1.low_ref
  121.3 0.0 copy-done.3
  121.3 0.0 copy-done.2
  121.3 0.0 copy-done.1
  121.3 5.5 %update.1 = (f32[59,8192]{1,0:T(8,128)}, f32[59,8192]{1,0:T(8,128)}, f32[59,8192]{1,0:T(8,128)}) custom-call(f32[59,8192]{1,0:T(8,128)S(1)} %copy-done.1, f32[59,8192]{1,0:T(8,128)S(1)} %copy-done.2, f32[59,8192]{1,0:T(8,128)S(1)} %copy-done.3, f32[2,37,8,128]{3,2,1,0:T(8,128)S(1)} %land.1.own_ref, f32[2,37,8,128]{3,2,1,0:T(8,128)S(1)} %collective-permute-done.next_ref, ...), custom_call_target="tpu_custom_call" | custom-call | tf_op jit(solution)/shard_map/update/pallas_call | solution.py:666
  (2 shorter events, 0.0 us)
Async XLA Ops:
  2.4 22.4 %all-to-all-start = ((s32[64,1,2]{2,1,0:T(1,128)}), s32[64,1,2]{2,1,0:T(1,128)S(1)}, u32[]{:S(2)}, u32[]{:S(2)}) async-start(s32[64,1,2]{2,1,0:T(1,128)} %get-tuple-element.12), calls=%async_computation | async-start | bytes 65536 | tf_op jit(solution)/shard_map/all_to_all | solution.py:702
  15.6 1.6 %copy-start = (f32[59,8192]{1,0:T(8,128)S(1)}, f32[59,8192]{1,0:T(8,128)}, u32[]{:S(2)}) copy-start(f32[59,8192]{1,0:T(8,128)} %params_ref.3) | copy-start | bytes 5799940
  17.2 0.7 copy-start.5
  17.8 33.2 %copy-start.4 = (f32[1,8,3,256]{3,1,2,0:T(8,128)S(1)}, f32[1,8,3,256]{3,1,2,0:T(8,128)}, u32[]{:S(2)}) copy-start(f32[1,8,3,256]{3,1,2,0:T(8,128)} %param.13) | copy-start | bytes 73732
  17.8 33.2 %copy-start.7 = (s32[1,128]{1,0:T(1,128)S(1)}, s32[1,128]{1,0:T(1,128)}, u32[]{:S(2)}) copy-start(s32[1,128]{1,0:T(1,128)} %get-tuple-element.13.table_ref) | copy-start | bytes 1540
  17.8 33.2 %copy-start.8 = (s32[1,128]{1,0:T(1,128)S(1)}, s32[1,128]{1,0:T(1,128)}, u32[]{:S(2)}) copy-start(s32[1,128]{1,0:T(1,128)} %get-tuple-element.14.count_ref) | copy-start | bytes 1540
  17.8 103.4 %copy-start.3 = (f32[59,8192]{1,0:T(8,128)S(1)}, f32[59,8192]{1,0:T(8,128)}, u32[]{:S(2)}) copy-start(f32[59,8192]{1,0:T(8,128)} %second_ref.1) | copy-start | bytes 5799940
  20.4 83.6 %copy-start.6 = (f32[1,4]{1,0:T(1,128)S(1)}, f32[1,4]{1,0:T(1,128)}, u32[]{:S(2)}) copy-start(f32[1,4]{1,0:T(1,128)} %pose_ref.3) | copy-start | bytes 52
  26.4 94.9 %copy-start.2 = (f32[59,8192]{1,0:T(8,128)S(1)}, f32[59,8192]{1,0:T(8,128)}, u32[]{:S(2)}) copy-start(f32[59,8192]{1,0:T(8,128)} %first_ref.1) | copy-start | bytes 5799940
  51.0 70.3 %copy-start.1 = (f32[59,8192]{1,0:T(8,128)S(1)}, f32[59,8192]{1,0:T(8,128)}, u32[]{:S(2)}) copy-start(f32[59,8192]{1,0:T(8,128)} %params_ref.3) | copy-start | bytes 5799940
  106.0 9.7 %collective-permute-start.2 = (f32[2,37,8,128]{3,2,1,0:T(8,128)S(1)}, f32[2,37,8,128]{3,2,1,0:T(8,128)S(1)}, u32[]{:S(2)}, u32[]{:S(2)}) collective-permute-start(f32[2,37,8,128]{3,2,1,0:T(8,128)S(1)} %land.1.own_ref), channel_id=1, source_target_pairs={{3,0},{0,1},{1,2},{2,3},{7,4},{4,5},{5,6},{6,7},{11,8},{8,9},{9,10... | collective-permute-start | bytes 909320 | tf_op jit(solution)/shard_map/ppermute | solution.py:726
  107.2 8.9 %collective-permute-start = (f32[2,37,8,128]{3,2,1,0:T(8,128)S(1)}, f32[2,37,8,128]{3,2,1,0:T(8,128)S(1)}, u32[]{:S(2)}, u32[]{:S(2)}) collective-permute-start(f32[2,37,8,128]{3,2,1,0:T(8,128)S(1)} %land.1.own_ref), channel_id=1, source_target_pairs={{1,0},{2,1},{3,2},{0,3},{5,4},{6,5},{7,6},{4,7},{9,8},{10,9},{11,1... | collective-permute-start | bytes 909320 | tf_op jit(solution)/shard_map/ppermute | solution.py:726
  115.8 5.5 %collective-permute-start.3 = (f32[1,37,8,128]{3,2,1,0:T(8,128)S(1)}, f32[1,37,8,128]{3,2,1,0:T(8,128)S(1)}, u32[]{:S(2)}, u32[]{:S(2)}) collective-permute-start(f32[1,37,8,128]{3,2,1,0:T(8,128)S(1)} %slice.9), channel_id=1, source_target_pairs={{3,0},{0,1},{1,2},{2,3},{7,4},{4,5},{5,6},{6,7},{11,8},{8,9},{9,10... | collective-permute-start | bytes 454664 | tf_op jit(solution)/shard_map/ppermute | solution.py:726
  116.1 5.2 %collective-permute-start.1 = (f32[1,37,8,128]{3,2,1,0:T(8,128)S(1)}, f32[1,37,8,128]{3,2,1,0:T(8,128)S(1)}, u32[]{:S(2)}, u32[]{:S(2)}) collective-permute-start(f32[1,37,8,128]{3,2,1,0:T(8,128)S(1)} %slice.8), channel_id=1, source_target_pairs={{1,0},{2,1},{3,2},{0,3},{5,4},{6,5},{7,6},{4,7},{9,8},{10,9},{11,1... | collective-permute-start | bytes 454664 | tf_op jit(solution)/shard_map/ppermute | solution.py:726

commit v5 on v4

--- a/solution.py
+++ b/solution.py
@@ -251,8 +251,13 @@
     return jnp.concatenate([high, low], axis=1)
 
 
-def twice(value):
-    return jnp.concatenate([value, value], axis=1)
+def across(value, wide):
+    return jnp.concatenate([value] * wide, axis=1)
+
+
+def band_of(band, wide):
+    size = wide * BLK
+    return jnp.concatenate([band[0:size, 0:size], band[2 * BLK : 2 * BLK + size, 0:size]], axis=0)
 
 
 def render_kernel(
@@ -296,9 +301,9 @@
                 rank = rank + ahead.astype(jnp.int32)
         ranked[rank] = t
 
-    def side_by_side(ref, at, j):
+    def side_by_side(ref, at, j, wide):
         return jnp.concatenate(
-            [ref[at, pl.ds(2 * j + k, 1), :].reshape(-1, BLK) for k in range(2)], axis=1
+            [ref[at, pl.ds(2 * j + k, 1), :].reshape(-1, BLK) for k in range(wide)], axis=1
         )
 
     def local(t, rows):
@@ -330,48 +335,57 @@
     def tile_pair(g, _):
         chosen = [ranked[4 * g + h] for h in range(4)]
         used = [count_ref[0, t] for t in chosen]
-        pairs = (functools.reduce(lax.max, used) + 1) // 2
+        most = functools.reduce(lax.max, used)
+        pairs, odd_one = (most // 2, most % 2)
         for h, (rows, terms, _, _, shades, _, _) in enumerate(lanes):
             prepare(chosen[h], used[h], rows, terms)
             shades[...] = jnp.zeros_like(shades)
 
-        def forward(j, logs):
+        def forward(j, logs, wide):
+            size = wide * BLK
             state = []
             for rows, terms, *_ in lanes:
-                coefs = side_by_side(terms, slice(None), j).astype(jnp.bfloat16)
+                coefs = side_by_side(terms, slice(None), j, wide).astype(jnp.bfloat16)
                 state.append(jnp.dot(basis[...], coefs, preferred_element_type=jnp.float32))
             alphas, losses, halves = ([], [], [])
             for h, (_, _, ratios, *_) in enumerate(lanes):
                 for r in range(0, PIX, ROWS):
                     alpha = jnp.minimum(jnp.exp2(state[h][r : r + ROWS]), BELOW_ONE)
                     loss = jnp.log2(1.0 - alpha)
-                    ratios[j, r : r + ROWS] = alpha * jnp.exp2(-loss)
+                    ratios[j, r : r + ROWS, 0:size] = alpha * jnp.exp2(-loss)
                     alphas.append(alpha)
                     losses.append(loss)
                     halves.append(halves_of(loss))
             run = jnp.dot(
-                jnp.concatenate(halves, axis=0), before[...], preferred_element_type=jnp.float32
+                jnp.concatenate(halves, axis=0), band_of(before, wide), preferred_element_type=jnp.float32
             )
             out = []
             for h, (rows, _, _, weights, shades, _, _) in enumerate(lanes):
-                tints = side_by_side(rows, slice(6, 9), j)
+                tints = side_by_side(rows, slice(6, 9), j, wide)
                 lasts = []
                 for r in range(0, PIX, ROWS):
                     n = (h * PIX + r) // ROWS
                     mine = run[h * PIX + r : h * PIX + r + ROWS]
                     log = logs[h][r : r + ROWS]
-                    weight = alphas[n] * jnp.exp2(mine + twice(log))
-                    weights[j, r : r + ROWS] = weight
+                    weight = alphas[n] * jnp.exp2(mine + across(log, wide))
+                    weights[j, r : r + ROWS, 0:size] = weight
                     for c in range(3):
                         shade = weight * tints[c : c + 1]
-                        shades[c, r : r + ROWS] += shade[:, 0:BLK] + shade[:, BLK:]
-                    last = mine[:, 2 * BLK - 1 :] + losses[n][:, 2 * BLK - 1 :]
+                        if wide == 2:
+                            shade = shade[:, 0:BLK] + shade[:, BLK:]
+                        shades[c, r : r + ROWS] += shade
+                    last = mine[:, size - 1 :] + losses[n][:, size - 1 :]
                     lasts.append(log + jnp.broadcast_to(last, (ROWS, BLK)))
                 out.append(jnp.concatenate(lasts, axis=0))
             return tuple(out)
 
         still = jnp.zeros((PIX, BLK), jnp.float32)
-        lax.fori_loop(0, pairs, forward, (still,) * 4)
+        logs = lax.fori_loop(0, pairs, functools.partial(forward, wide=2), (still,) * 4)
+
+        @pl.when(odd_one == 1)
+        def _():
+            forward(pairs, logs, 1)
+
         lane = lax.broadcasted_iota(jnp.int32, (PIX, BLK), 1)
         pulled = []
         for h, (_, _, _, _, shades, pulls, _) in enumerate(lanes):
@@ -391,18 +405,20 @@
                 pulls[c] = jnp.broadcast_to(turned[:, 42 + c : 43 + c], (PIX, BLK))
             pulled.append(turned.astype(jnp.bfloat16))
 
-        def backward(step, later):
+        def backward(step, later, wide):
             j = pairs - 1 - step
+            size = wide * BLK
+            tilt = x[:, 0:size]
             reaches, halves = ([], [])
             for h, (_, terms, _, weights, *_) in enumerate(lanes):
-                coefs = side_by_side(terms, slice(None), j).astype(jnp.bfloat16)
+                coefs = side_by_side(terms, slice(None), j, wide).astype(jnp.bfloat16)
                 pull = jnp.dot(pulled[h], coefs, preferred_element_type=jnp.float32)
                 for r in range(0, PIX, 16):
-                    reach = pull[r : r + 16] * weights[j, r : r + 16]
+                    reach = pull[r : r + 16] * weights[j, r : r + 16, 0:size]
                     reaches.append(reach)
                     halves.append(halves_of(reach))
             behinds = jnp.dot(
-                jnp.concatenate(halves, axis=0), after[...], preferred_element_type=jnp.float32
+                jnp.concatenate(halves, axis=0), band_of(after, wide), preferred_element_type=jnp.float32
             )
             out = []
             for h, (_, _, ratios, weights, _, pulls, sums) in enumerate(lanes):
@@ -416,12 +432,12 @@
                         reach = reaches[16 * h + m]
                         behind = behinds[h * PIX + 16 * m : h * PIX + 16 * m + 16]
                         log = later[h][at]
-                        pair.append(reach - (behind + twice(log)) * ratios[j, at])
+                        pair.append(reach - (behind + across(log, wide)) * ratios[j, at, 0:size])
                         last = jnp.broadcast_to(behind[:, 0:1] + reach[:, 0:1], (16, BLK))
                         lasts[m] = log + last
-                        weight = weights[j, at]
+                        weight = weights[j, at, 0:size]
                         for c in range(3):
-                            tint = weight * twice(pulls[c, at])
+                            tint = weight * across(pulls[c, at], wide)
                             tint = tint[0:8] + tint[8:16]
                             tints[c] = tint if tints[c] is None else tints[c] + tint
                     y = 7.5 - n
@@ -430,16 +446,19 @@
                     plain = even if n == 0 else plain + even
                     tilted = odd if n == 0 else tilted + odd
                     bent = square if n == 0 else bent + square
-                values = (plain, x * plain, tilted, x * x * plain, x * tilted, bent)
+                values = (plain, tilt * plain, tilted, tilt * tilt * plain, tilt * tilted, bent)
                 values = [value[0:8] + value[8:16] for value in values] + tints
                 for f, value in enumerate(values):
-                    for k in range(2):
+                    for k in range(wide):
                         at = slice(BLK * k, BLK * (k + 1))
                         sums[f, pl.ds(2 * j + k, 1)] = value[:, at].reshape(1, 8, BLK)
                 out.append(jnp.concatenate(lasts, axis=0))
             return tuple(out)
 
-        lax.fori_loop(0, pairs, backward, (still,) * 4)
+        later = lax.fori_loop(
+            0, odd_one, lambda _, later: backward(-1, later, 1), (still,) * 4
+        )
+        lax.fori_loop(0, pairs, functools.partial(backward, wide=2), later)
         for h, (rows, _, _, _, _, _, sums) in enumerate(lanes):
             t = chosen[h]
             u, v, a, b, d = local(t, rows)

time: 129 us -> 129 us (level)
  Pallas kernels: 40.7 us -> 38.8 us
    pallas_call x1, Pallas kernels: 27.2 us -> 25.4 us  [render(): pl.pallas_call(render_kernel, out_shape=[shape((3, tiles, PIX), f32), sha...]
where the time goes in v5:
time: 129 us; the launch traced here: 127 us
  blocking collectives  50.5 us (39%)
  Pallas kernels  38.8 us (30%)
  starting transfers between devices  19.7 us (15%)
  waiting for transfers between devices  14.6 us (11%)
  local copies, waits for them, and re-layouts  2.3 us (2%)
    all_to_all x1, blocking collectives, shards(): landed = lax.all_to_all(back, 'gs', split_axis=0, concat_axis=0, tiled=True)  25.9 us
    pallas_call x1, Pallas kernels, render(): pl.pallas_call(render_kernel, out_shape=[shape((3, tiles, PIX), f32), sha...  25.4 us
    all_to_all x1, blocking collectives, shards(): lax.all_to_all(outgoing, 'gs', split_axis=0, concat_axis=0, tiled=True)  24.6 us
    all_to_all x1, starting transfers between devices, shards(): lax.all_to_all(wanted, 'gs', split_axis=0, concat_axis=0, tiled=True)  13.2 us
    ppermute x4, waiting for transfers between devices, from_next(): lax.ppermute(value, 'view', [((i + k) % views, i) for i in range(views)])  10.3 us
    ppermute x4, starting transfers between devices, from_next(): lax.ppermute(value, 'view', [((i + k) % views, i) for i in range(views)])  6.5 us
    pallas_call x1, Pallas kernels, update(): pl.pallas_call(update_kernel, out_shape=[jax.ShapeDtypeStruct(gauss_param...  5.54 us
    all_to_all x1, waiting for transfers between devices, shards(): lax.all_to_all(wanted, 'gs', split_axis=0, concat_axis=0, tiled=True)  4.36 us
  transfers between devices with their start and end apart: 5, of which 3 were waited for; matrix products, arithmetic and copies ran while one was open for 0% of the time, Pallas kernels for 2%

profile of v5, /device:TPU:1, one launch (start us, length us, event | category | flops | bytes accessed | tf_op | source)
XLA Modules:
  0.0 126.9 jit_solution(14523238838047563234)
XLA Ops:
  0.6 1.8 %requests.1 = (s32[64,1,2]{2,1,0:T(1,128)}, s32[1,128]{1,0:T(1,128)}, s32[1,128]{1,0:T(1,128)}) custom-call(s32[8,16]{1,0:T(8,128)} %bitcast.9, s32[8,16]{1,0:T(8,128)} %bitcast.10), custom_call_target="tpu_custom_call" | custom-call | tf_op jit(solution)/shard_map/requests/pallas_call | solution.py:714
  2.4 13.2 %all-to-all-start = ((s32[64,1,2]{2,1,0:T(1,128)}), s32[64,1,2]{2,1,0:T(1,128)S(1)}, u32[]{:S(2)}, u32[]{:S(2)}) async-start(s32[64,1,2]{2,1,0:T(1,128)} %get-tuple-element.12), calls=%async_computation | async-start | bytes 65536 | tf_op jit(solution)/shard_map/all_to_all | solution.py:721
  15.6 0.0 copy-start
  15.6 1.6 %copy-done = f32[59,8192]{1,0:T(8,128)S(1)} copy-done((f32[59,8192]{1,0:T(8,128)S(1)}, f32[59,8192]{1,0:T(8,128)}, u32[]{:S(2)}) %copy-start) | copy-done | bytes 1933336
  17.2 0.0 copy-start.5
  17.2 0.7 copy-done.5
  17.8 0.0 copy-start.4
  17.8 0.0 copy-start.7
  17.8 0.0 copy-start.8
  17.8 0.0 copy-start.3
  17.9 2.6 %project.1.feats_ref = f32[64,16,128]{2,1,0:T(8,128)S(1)} custom-call(f32[1,4]{1,0:T(1,128)S(1)} %copy-done.5, f32[59,8192]{1,0:T(8,128)S(1)} %copy-done), custom_call_target="tpu_custom_call" | custom-call | tf_op jit(solution)/shard_map/project/pallas_call | solution.py:665
  20.4 0.0 copy-start.6
  20.4 4.4 %all-to-all-done.asked_ref = s32[64,1,2]{2,1,0:T(1,128)S(1)} async-done(((s32[64,1,2]{2,1,0:T(1,128)}), s32[64,1,2]{2,1,0:T(1,128)S(1)}, u32[]{:S(2)}, u32[]{:S(2)}) %all-to-all-start) | async-done | bytes 544 | tf_op jit(solution)/shard_map/all_to_all | solution.py:721
  24.8 1.6 %pick.1 = f32[64,9,2,128]{3,2,1,0:T(2,128)S(1)} custom-call(s32[64,1,2]{2,1,0:T(1,128)S(1)} %all-to-all-done.asked_ref, f32[64,16,128]{2,1,0:T(8,128)S(1)} %project.1.feats_ref), custom_call_target="tpu_custom_call" | custom-call | tf_op jit(solution)/shard_map/pick/pallas_call | solution.py:723
  26.4 0.0 copy-start.2
  26.4 24.6 %all_to_all.15.arrived_ref = f32[64,9,2,128]{3,2,1,0:T(2,128)S(1)} all-to-all(f32[64,9,2,128]{3,2,1,0:T(2,128)S(1)} %pick.1), channel_id=1, replica_groups=mesh['gs'=64,'view'=4] {'gs'}, dimensions={0} | all-to-all | bytes 1179648 | tf_op jit(solution)/shard_map/all_to_all | solution.py:731
  51.0 0.0 copy-start.1
  51.0 0.0 copy-done.4
  51.0 0.0 copy-done.7
  51.0 0.0 copy-done.8
  51.0 25.4 %render.1 = (f32[3,8,256]{2,1,0:T(8,128)}, f32[64,9,2,128]{3,2,1,0:T(2,128)S(1)}) custom-call(s32[1,128]{1,0:T(1,128)S(1)} %copy-done.7, s32[1,128]{1,0:T(1,128)S(1)} %copy-done.8, f32[64,9,2,128]{3,2,1,0:T(2,128)S(1)} %all_to_all.15.arrived_ref, f32[3,8,256]{2,1,0:T(8,128)S(1)} %bitcast.8), custom_call_target="tpu_custom_call" | custom-call | tf_op jit(solution)/shard_map/render/pallas_call | solution.py:493
  76.4 25.9 %all_to_all.16.landed_ref = f32[64,9,2,128]{3,2,1,0:T(2,128)S(1)} all-to-all(f32[64,9,2,128]{3,2,1,0:T(2,128)S(1)} %get-tuple-element.15), channel_id=1, replica_groups=mesh['gs'=64,'view'=4] {'gs'}, dimensions={0} | all-to-all | bytes 1179648 | tf_op jit(solution)/shard_map/all_to_all | solution.py:733
  102.3 0.0 copy-done.6
  102.3 2.0 %land.1.own_ref = f32[2,37,8,128]{3,2,1,0:T(8,128)S(1)} custom-call(s32[64,1,2]{2,1,0:T(1,128)S(1)} %all-to-all-done.asked_ref, f32[1,4]{1,0:T(1,128)S(1)} %copy-done.6, f32[64,9,2,128]{3,2,1,0:T(2,128)S(1)} %all_to_all.16.landed_ref, f32[64,16,128]{2,1,0:T(8,128)S(1)} %project.1.feats_ref), custom_call_target="tpu_custom_call" | custom-call | tf_op jit(solution)/shard_map/land/pallas_call | solution.py:734
  104.3 1.6 %collective-permute-start.2 = (f32[2,37,8,128]{3,2,1,0:T(8,128)S(1)}, f32[2,37,8,128]{3,2,1,0:T(8,128)S(1)}, u32[]{:S(2)}, u32[]{:S(2)}) collective-permute-start(f32[2,37,8,128]{3,2,1,0:T(8,128)S(1)} %land.1.own_ref), channel_id=1, source_target_pairs={{3,0},{0,1},{1,2},{2,3},{7,4},{4,5},{5,6},{6,7},{11,8},{8,9},{9,10... | collective-permute-start | bytes 909320 | tf_op jit(solution)/shard_map/ppermute | solution.py:745
  105.9 2.1 %collective-permute-start = (f32[2,37,8,128]{3,2,1,0:T(8,128)S(1)}, f32[2,37,8,128]{3,2,1,0:T(8,128)S(1)}, u32[]{:S(2)}, u32[]{:S(2)}) collective-permute-start(f32[2,37,8,128]{3,2,1,0:T(8,128)S(1)} %land.1.own_ref), channel_id=1, source_target_pairs={{1,0},{2,1},{3,2},{0,3},{5,4},{6,5},{7,6},{4,7},{9,8},{10,9},{11,1... | collective-permute-start | bytes 909320 | tf_op jit(solution)/shard_map/ppermute | solution.py:745
  108.0 7.2 %collective-permute-done.2.last_ref = f32[2,37,8,128]{3,2,1,0:T(8,128)S(1)} collective-permute-done((f32[2,37,8,128]{3,2,1,0:T(8,128)S(1)}, f32[2,37,8,128]{3,2,1,0:T(8,128)S(1)}, u32[]{:S(2)}, u32[]{:S(2)}) %collective-permute-start.2) | collective-permute-done | bytes 303136 | tf_op jit(solution)/shard_map/ppermute | solution.py:745
  115.2 0.1 collective-permute-start.3
  115.3 0.0 collective-permute-done.next_ref
  115.4 2.7 %collective-permute-start.1 = (f32[1,37,8,128]{3,2,1,0:T(8,128)S(1)}, f32[1,37,8,128]{3,2,1,0:T(8,128)S(1)}, u32[]{:S(2)}, u32[]{:S(2)}) collective-permute-start(f32[1,37,8,128]{3,2,1,0:T(8,128)S(1)} %slice.8), channel_id=1, source_target_pairs={{1,0},{2,1},{3,2},{0,3},{5,4},{6,5},{7,6},{4,7},{9,8},{10,9},{11,1... | collective-permute-start | bytes 454664 | tf_op jit(solution)/shard_map/ppermute | solution.py:745
  118.1 3.1 %collective-permute-done.3.high_ref = f32[1,37,8,128]{3,2,1,0:T(8,128)S(1)} collective-permute-done((f32[1,37,8,128]{3,2,1,0:T(8,128)S(1)}, f32[1,37,8,128]{3,2,1,0:T(8,128)S(1)}, u32[]{:S(2)}, u32[]{:S(2)}) %collective-permute-start.3) | collective-permute-done | bytes 151584 | tf_op jit(solution)/shard_map/ppermute | solution.py:745
  121.1 0.0 collective-permute-done.1.low_ref
  121.2 0.0 copy-done.3
  121.2 0.0 copy-done.2
  121.2 0.0 copy-done.1
  121.2 5.5 %update.1 = (f32[59,8192]{1,0:T(8,128)}, f32[59,8192]{1,0:T(8,128)}, f32[59,8192]{1,0:T(8,128)}) custom-call(f32[59,8192]{1,0:T(8,128)S(1)} %copy-done.1, f32[59,8192]{1,0:T(8,128)S(1)} %copy-done.2, f32[59,8192]{1,0:T(8,128)S(1)} %copy-done.3, f32[2,37,8,128]{3,2,1,0:T(8,128)S(1)} %land.1.own_ref, f32[2,37,8,128]{3,2,1,0:T(8,128)S(1)} %collective-permute-done.next_ref, ...), custom_call_target="tpu_custom_call" | custom-call | tf_op jit(solution)/shard_map/update/pallas_call | solution.py:685
  (2 shorter events, 0.0 us)
Async XLA Ops:
  2.4 22.4 %all-to-all-start = ((s32[64,1,2]{2,1,0:T(1,128)}), s32[64,1,2]{2,1,0:T(1,128)S(1)}, u32[]{:S(2)}, u32[]{:S(2)}) async-start(s32[64,1,2]{2,1,0:T(1,128)} %get-tuple-element.12), calls=%async_computation | async-start | bytes 65536 | tf_op jit(solution)/shard_map/all_to_all | solution.py:721
  15.6 1.6 %copy-start = (f32[59,8192]{1,0:T(8,128)S(1)}, f32[59,8192]{1,0:T(8,128)}, u32[]{:S(2)}) copy-start(f32[59,8192]{1,0:T(8,128)} %params_ref.3) | copy-start | bytes 5799940
  17.2 0.7 copy-start.5
  17.8 33.2 %copy-start.4 = (f32[1,8,3,256]{3,1,2,0:T(8,128)S(1)}, f32[1,8,3,256]{3,1,2,0:T(8,128)}, u32[]{:S(2)}) copy-start(f32[1,8,3,256]{3,1,2,0:T(8,128)} %param.13) | copy-start | bytes 73732
  17.8 33.2 %copy-start.7 = (s32[1,128]{1,0:T(1,128)S(1)}, s32[1,128]{1,0:T(1,128)}, u32[]{:S(2)}) copy-start(s32[1,128]{1,0:T(1,128)} %get-tuple-element.13.table_ref) | copy-start | bytes 1540
  17.8 33.2 %copy-start.8 = (s32[1,128]{1,0:T(1,128)S(1)}, s32[1,128]{1,0:T(1,128)}, u32[]{:S(2)}) copy-start(s32[1,128]{1,0:T(1,128)} %get-tuple-element.14.count_ref) | copy-start | bytes 1540
  17.8 103.3 %copy-start.3 = (f32[59,8192]{1,0:T(8,128)S(1)}, f32[59,8192]{1,0:T(8,128)}, u32[]{:S(2)}) copy-start(f32[59,8192]{1,0:T(8,128)} %second_ref.1) | copy-start | bytes 5799940
  20.4 81.8 %copy-start.6 = (f32[1,4]{1,0:T(1,128)S(1)}, f32[1,4]{1,0:T(1,128)}, u32[]{:S(2)}) copy-start(f32[1,4]{1,0:T(1,128)} %pose_ref.3) | copy-start | bytes 52
  26.4 94.8 %copy-start.2 = (f32[59,8192]{1,0:T(8,128)S(1)}, f32[59,8192]{1,0:T(8,128)}, u32[]{:S(2)}) copy-start(f32[59,8192]{1,0:T(8,128)} %first_ref.1) | copy-start | bytes 5799940
  51.0 70.2 %copy-start.1 = (f32[59,8192]{1,0:T(8,128)S(1)}, f32[59,8192]{1,0:T(8,128)}, u32[]{:S(2)}) copy-start(f32[59,8192]{1,0:T(8,128)} %params_ref.3) | copy-start | bytes 5799940
  104.3 10.9 %collective-permute-start.2 = (f32[2,37,8,128]{3,2,1,0:T(8,128)S(1)}, f32[2,37,8,128]{3,2,1,0:T(8,128)S(1)}, u32[]{:S(2)}, u32[]{:S(2)}) collective-permute-start(f32[2,37,8,128]{3,2,1,0:T(8,128)S(1)} %land.1.own_ref), channel_id=1, source_target_pairs={{3,0},{0,1},{1,2},{2,3},{7,4},{4,5},{5,6},{6,7},{11,8},{8,9},{9,10... | collective-permute-start | bytes 909320 | tf_op jit(solution)/shard_map/ppermute | solution.py:745
  105.9 9.5 %collective-permute-start = (f32[2,37,8,128]{3,2,1,0:T(8,128)S(1)}, f32[2,37,8,128]{3,2,1,0:T(8,128)S(1)}, u32[]{:S(2)}, u32[]{:S(2)}) collective-permute-start(f32[2,37,8,128]{3,2,1,0:T(8,128)S(1)} %land.1.own_ref), channel_id=1, source_target_pairs={{1,0},{2,1},{3,2},{0,3},{5,4},{6,5},{7,6},{4,7},{9,8},{10,9},{11,1... | collective-permute-start | bytes 909320 | tf_op jit(solution)/shard_map/ppermute | solution.py:745
  115.2 5.9 %collective-permute-start.3 = (f32[1,37,8,128]{3,2,1,0:T(8,128)S(1)}, f32[1,37,8,128]{3,2,1,0:T(8,128)S(1)}, u32[]{:S(2)}, u32[]{:S(2)}) collective-permute-start(f32[1,37,8,128]{3,2,1,0:T(8,128)S(1)} %slice.9), channel_id=1, source_target_pairs={{3,0},{0,1},{1,2},{2,3},{7,4},{4,5},{5,6},{6,7},{11,8},{8,9},{9,10... | collective-permute-start | bytes 454664 | tf_op jit(solution)/shard_map/ppermute | solution.py:745
  115.4 5.8 %collective-permute-start.1 = (f32[1,37,8,128]{3,2,1,0:T(8,128)S(1)}, f32[1,37,8,128]{3,2,1,0:T(8,128)S(1)}, u32[]{:S(2)}, u32[]{:S(2)}) collective-permute-start(f32[1,37,8,128]{3,2,1,0:T(8,128)S(1)} %slice.8), channel_id=1, source_target_pairs={{1,0},{2,1},{3,2},{0,3},{5,4},{6,5},{7,6},{4,7},{9,8},{10,9},{11,1... | collective-permute-start | bytes 454664 | tf_op jit(solution)/shard_map/ppermute | solution.py:745
